TPU v7x, 32 devices: a whole 2x2x4 slice. The times are simulated.
32 devices in a mesh: groups: 2 (over y), slab: 8 (over z, x), trans: 2 (over core).
Axes of the slice: x: 2, y: 2, z: 4, core: 2. Of those that a mesh axis runs over, the one named last changes fastest.
Arguments:
- volume: float32 [2048, 2048], P(('groups', 'slab'), 'trans'), parts along dimension 0, may hold values from -6 to 6
- col_weight: float32 [2048, 2048], P(('groups', 'slab'), 'trans'), parts along dimension 0, may hold values from 0.5 to 4
- foot_pos: float32 [4, 2048], P(None, 'trans'), may hold values from 0 to 1024
- foot_width: float32 [4, 2048], P(None, 'trans'), may hold values from 1 to 4
- measured: float32 [8, 8, 1024], P(('groups', 'trans'), 'slab'), parts along dimension 0, may hold values from -12 to 12
- row_weight: float32 [8, 8, 1024], P(('groups', 'trans'), 'slab'), parts along dimension 0, may hold values from 0.1 to 1
- row_tiles: bfloat16 [128, 2, 128], P(('groups', 'slab')), parts along dimension 0, may hold values from -0.5 to 0.5
- tile_view_index: int32 [128], P(('groups', 'slab')), parts along dimension 0, may hold values from 0 to 3, as said below
- tile_block: int32 [128], P(('groups', 'slab')), parts along dimension 0, may hold values from 0 to 3, as said below
- tile_count: int32 [16], P(('groups', 'slab')), parts along dimension 0, may hold values from 4 to 8, as said below
Outputs:
- updated: float32 [2048, 2048], P(('groups', 'slab'), 'trans'), parts along dimension 0
- residual: bfloat16 [8, 8, 1024], P(('groups', 'trans'), 'slab'), parts along dimension 0
There are 2 independent parts, one for each index of `groups`. A program takes and returns all parts, laid end to end along the dimension named above; an argument that names none is the same for every part. Nothing has to cross between parts.
Inputs may be any that keep to these rules, and one draw needn't show every extreme that they name: `tile_count`: some slab index has exactly 8 live slots in every draw. `tile_view_index`: slots that are not live hold 0. `tile_block`: slots that are not live hold 0.
All inputs are finite; a program needn't handle non-finite values.
Results may differ from a plain program's by a relative error of at most 0.009.
Values may be sent and summed in bfloat16 or wider, within the bound.
No kernel may reach another device: no remote copies, remote signals or barrier semaphores. Data moves between devices by JAX's collectives and lax.ppermute only.
A program may use at most 64 MiB of HBM per device.

v0:
```python
import jax
import jax.numpy as jnp
from jax import lax
from jax.sharding import PartitionSpec as P


def footprints(foot_pos, foot_width, det_cols):
    det_coord = jnp.arange(det_cols).astype(jnp.float32) + 0.5
    distance = jnp.abs(det_coord[None, None, :] - foot_pos[:, :, None]) / foot_width[:, :, None]
    return jnp.maximum(0.0, 1.0 - distance).astype(jnp.bfloat16)


def body(
    volume,
    col_weight,
    foot_pos,
    foot_width,
    measured,
    row_weight,
    row_tiles,
    tile_view_index,
    tile_block,
    tile_count,
):
    vox_rows = volume.shape[0]
    n_views = foot_pos.shape[0]
    shared_view_list, own_rows, det_cols = measured.shape
    max_tiles, tile_rows = (row_tiles.shape[0], row_tiles.shape[1])
    n_slab = lax.axis_size("slab")
    rows_total = own_rows * n_slab
    zero_idx = jnp.zeros((), jnp.int32)
    live_count = tile_count[0]
    footprint = footprints(foot_pos, foot_width, det_cols)
    vox_lines = jnp.einsum(
        "zt,vtu->vzu", volume.astype(jnp.bfloat16), footprint, preferred_element_type=jnp.float32
    ).astype(jnp.bfloat16)

    def add_tile(tile_idx, running):
        view_id = tile_view_index[tile_idx]
        block_id = tile_block[tile_idx]
        is_live = (tile_idx < live_count).astype(jnp.float32)
        vox_block = lax.dynamic_index_in_dim(vox_lines, view_id, 0, keepdims=False)
        tile_term = (
            jnp.dot(row_tiles[tile_idx], vox_block, preferred_element_type=jnp.float32) * is_live
        )
        current = lax.dynamic_slice(
            running, (block_id * tile_rows, view_id, zero_idx), (tile_rows, 1, det_cols)
        )
        return lax.dynamic_update_slice(
            running, current + tile_term[:, None, :], (block_id * tile_rows, view_id, zero_idx)
        )

    partial_value = lax.fori_loop(
        0, max_tiles, add_tile, jnp.zeros((rows_total, n_views, det_cols), jnp.float32)
    )
    owned = lax.psum_scatter(partial_value, "slab", scatter_dimension=0, tiled=True)
    local_portion = lax.psum_scatter(owned, "trans", scatter_dimension=1, tiled=True)
    measurement_rows = jnp.transpose(measured, (1, 0, 2))
    row_weight_matrix = jnp.transpose(row_weight, (1, 0, 2))
    residual_lines = ((measurement_rows - local_portion) * row_weight_matrix).astype(jnp.bfloat16)
    residual = jnp.transpose(residual_lines, (1, 0, 2))
    empty_sums = jnp.zeros((n_views, vox_rows, det_cols), jnp.float32)
    view_rows = lax.all_gather(residual_lines, "trans", axis=1, tiled=True)
    gathered = lax.all_gather(view_rows, "slab", axis=0, tiled=True)

    def back_tile(tile_idx, running):
        view_id = tile_view_index[tile_idx]
        block_id = tile_block[tile_idx]
        inside = (view_id >= zero_idx) & (view_id < zero_idx + n_views)
        is_live = ((tile_idx < live_count) & inside).astype(jnp.float32)
        taken = jnp.clip(view_id, 0, n_views - 1)
        res_block = lax.dynamic_slice(
            gathered, (block_id * tile_rows, taken, zero_idx), (tile_rows, 1, det_cols)
        )[:, 0, :]
        tile_term = (
            lax.dot_general(
                row_tiles[tile_idx],
                res_block,
                (((0,), (0,)), ((), ())),
                preferred_element_type=jnp.float32,
            )
            * is_live
        )
        current = lax.dynamic_slice(running, (view_id, zero_idx, zero_idx), (1, vox_rows, det_cols))
        return lax.dynamic_update_slice(
            running, current + tile_term[None], (view_id, zero_idx, zero_idx)
        )

    backprojected_totals = lax.fori_loop(0, max_tiles, back_tile, empty_sums)
    gradient = jnp.einsum(
        "vzu,vtu->zt",
        backprojected_totals.astype(jnp.bfloat16),
        footprint,
        preferred_element_type=jnp.float32,
    )
    updated = volume + 0.9 * col_weight * gradient
    return (updated, residual)


def solution(mesh):
    in_specs = (
        P(("groups", "slab"), "trans"),
        P(("groups", "slab"), "trans"),
        P(None, "trans"),
        P(None, "trans"),
        P(("groups", "trans"), "slab", None),
        P(("groups", "trans"), "slab", None),
        P(("groups", "slab"), None, None),
        P(("groups", "slab")),
        P(("groups", "slab")),
        P(("groups", "slab")),
    )
    out_specs = (P(("groups", "slab"), "trans"), P(("groups", "trans"), "slab", None))
    return jax.shard_map(body, mesh=mesh, in_specs=in_specs, out_specs=out_specs, check_vma=False)
```

profile of v0, /device:TPU:0, one launch (start us, length us, event | category | flops | bytes accessed | tf_op | source)
XLA Modules:
  0.0 237.9 jit_solution(4336537649426631027)
XLA Ops:
  7.2 5.8 %fusion.18 = bf16[4,128,1024]{1,2,0:T(8,128)(2,1)S(1)} fusion(f32[4,1024]{1,0:T(4,128)} %param.17, f32[4,1024]{1,0:T(4,128)} %param.16, f32[1024]{0:T(1024)S(1)} %convert_add_fusion, f32[128,1024]{1,0:T(8,128)} %param.14), kind=kOutput, calls=%fused_computation.22 | convolution fusion | flops 1099563008 | bytes 1609728 | tf_op jit(solution)/shard_map/zt,vtu->vzu/dot_general | solution.py:34
  13.2 43.4 %while.26 = (s32[]{:T(128)}, f32[8,4,1024]{2,1,0:T(4,128)S(1)}, s32[8]{0:T(128)S(1)}, s32[8]{0:T(128)S(1)}, bf16[8,2,128]{2,1,0:T(2,128)(2,1)}, /*index=5*/bf16[...) while((s32[]{:T(128)}, f32[8,4,1024]{2,1,0:T(4,128)S(1)}, ...), condition=%wide.region_1.2_spmd, body=%wide.region_0.1_spmd.sunk | while | flops 528395 | bytes 328959 | solution.py:53
  13.2 0.6 dynamic_slice.103
  14.5 0.6 dynamic_slice.102
  17.7 0.8 fusion.38
  18.6 0.6 dynamic_slice.103
  19.9 0.6 dynamic_slice.102
  23.1 0.8 fusion.38
  23.9 0.1 dynamic_update_slice.17
  24.1 0.6 dynamic_slice.103
  25.3 0.6 dynamic_slice.102
  28.5 0.8 fusion.38
  29.4 0.1 dynamic_update_slice.17
  29.5 0.6 dynamic_slice.103
  30.7 0.6 dynamic_slice.102
  33.9 0.8 fusion.38
  34.8 0.1 dynamic_update_slice.17
  34.9 0.6 dynamic_slice.103
  36.1 0.6 dynamic_slice.102
  39.4 0.8 fusion.38
  40.3 0.6 dynamic_slice.103
  41.6 0.6 dynamic_slice.102
  44.8 0.8 fusion.38
  45.7 0.6 dynamic_slice.103
  47.0 0.6 dynamic_slice.102
  50.2 0.8 fusion.38
  51.2 0.6 dynamic_slice.103
  52.4 0.6 dynamic_slice.102
  55.6 0.8 fusion.38
  56.6 0.6 copy-done
  57.3 0.6 dynamic-slice
  57.9 0.6 dynamic-slice.2
  59.0 70.8 %all-reduce.4.cloned.1.call-done = f32[8,4,1024]{2,1,0:T(4,128)} async-done(((f32[8,4,1024]{2,1,0:T(4,128)}), f32[8,4,1024]{2,1,0:T(4,128)}) %all-reduce.4.cloned.1.call-update) | async-done | bytes 131088
  129.8 1.4 constant_dynamic-slice_fusion.3
  131.2 3.3 %all-reduce.1 = f32[1,4,1024]{2,1,0:T(4,128)S(1)} all-reduce(f32[1,4,1024]{2,1,0:T(4,128)S(1)} %constant_dynamic-slice_fusion.3), channel_id=3, replica_groups=mesh['groups'=2,'slab'=8,'trans'=2] {'trans'}, use_global_device_ids=true, to_apply=%region_3.4.clone | all-reduce | flops 4096 | bytes 32768
  134.6 1.8 all_gather.6
  136.4 30.5 %all_gather.7 = bf16[8,4,1024]{2,1,0:T(4,128)(2,1)S(1)} all-gather(bf16[1,4,1024]{2,1,0:T(4,128)(2,1)S(1)} %copy.23), channel_id=1, replica_groups=mesh['groups'=2,'slab'=8,'trans'=2] {'slab'}, dimensions={0}, use_global_device_ids=true | all-gather | bytes 73728 | tf_op jit(solution)/shard_map/all_gather | solution.py:64
  167.0 0.2 broadcast_in_dim.23
  167.3 59.0 %while.27 = (s32[]{:T(128)}, f32[4,128,1024]{2,1,0:T(8,128)S(1)}, s32[8]{0:T(128)S(1)}, bf16[8,2,128]{2,1,0:T(2,128)(2,1)}, s32[8]{0:T(128)S(1)}, /*index=5*/bf1...) while((s32[]{:T(128)}, f32[4,128,1024]{2,1,0:T(8,128)S(1)}, ...), condition=%wide.region_5.6_spmd, body=%wide.region_4.5_spmd.sunk | while | flops 786449 | bytes 1054003 | solution.py:89
  167.3 0.6 dynamic_slice.107
  171.8 0.7 dynamic_slice.108
  173.7 0.9 fusion.41
  174.7 0.6 dynamic_slice.107
  179.1 0.7 dynamic_slice.108
  181.1 0.9 fusion.41
  182.0 0.6 dynamic_slice.107
  186.5 0.7 dynamic_slice.108
  188.4 0.9 fusion.41
  189.4 0.6 dynamic_slice.107
  193.9 0.7 dynamic_slice.108
  195.8 0.9 fusion.41
  196.8 0.6 dynamic_slice.107
  201.3 0.7 dynamic_slice.108
  203.2 0.9 fusion.41
  204.2 0.6 dynamic_slice.107
  208.6 0.7 dynamic_slice.108
  210.6 0.9 fusion.41
  211.5 0.6 dynamic_slice.107
  216.0 0.7 dynamic_slice.108
  217.9 0.9 fusion.41
  218.9 0.6 dynamic_slice.107
  223.4 0.7 dynamic_slice.108
  225.3 0.9 fusion.41
  226.3 4.8 %fusion.21 = f32[128,1024]{1,0:T(8,128)} fusion(f32[128,1024]{1,0:T(8,128)S(1)} %copy-done.4, f32[4,1024]{1,0:T(4,128)S(1)} %copy-done.6, f32[4,1024]{1,0:T(4,128)S(1)} %copy-done.7, f32[1024]{0:T(1024)S(1)} %convert_add_fusion, f32[4,128,1024]{2,1,0:T(8,128)S(1)} %get-tuple-element.251, f32[128,1024]{1,0:T(8,128)S(1)} %copy-done.5), kind=kOutput, calls=%fused_computation.25 | convolution fusion | flops 1099825152 | bytes 3706880 | tf_op jit(solution)/shard_map/vzu,vtu->zt/dot_general | solution.py:90
  (52 shorter events, 1.0 us)
Async XLA Ops:
  7.2 122.7 %all-reduce.4.cloned.1.call-start = ((), (), s32[]{:S(2)}) async-start(), calls=%async_computation | async-start | bytes 262144
  7.2 6.0 %copy-start.8 = (s32[8]{0:T(128)S(1)}, s32[8]{0:T(128)}, u32[]{:S(2)}) copy-start(s32[8]{0:T(128)} %param.21) | copy-start | bytes 100
  7.2 6.0 %copy-start.9 = (s32[8]{0:T(128)S(1)}, s32[8]{0:T(128)}, u32[]{:S(2)}) copy-start(s32[8]{0:T(128)} %param.22) | copy-start | bytes 100
  13.1 44.2 %copy-start.11 = (u32[32]{0:T(128)S(1)}, u32[32]{0:T(128)}, u32[]{:S(2)}) copy-start(u32[32]{0:T(128)} %constant.103) | copy-start | bytes 388
  13.1 44.8 %copy-start.10 = (u32[32]{0:T(128)S(1)}, u32[32]{0:T(128)}, u32[]{:S(2)}) copy-start(u32[32]{0:T(128)} %constant.107) | copy-start | bytes 388
  13.1 121.4 %copy-start.2 = (f32[2,1,1024]{2,1,0:T(1,128)S(1)}, f32[2,1,1024]{2,1,0:T(1,128)}, u32[]{:S(2)}) copy-start(f32[2,1,1024]{2,1,0:T(1,128)} %param.19) | copy-start | bytes 24580
  13.1 121.4 %copy-start.3 = (f32[2,1,1024]{2,1,0:T(1,128)S(1)}, f32[2,1,1024]{2,1,0:T(1,128)}, u32[]{:S(2)}) copy-start(f32[2,1,1024]{2,1,0:T(1,128)} %param.18) | copy-start | bytes 24580
  56.6 0.7 copy-start
  134.6 32.7 %copy-start.1 = (bf16[1,2,1024]{2,1,0:T(2,128)(2,1)}, bf16[1,2,1024]{2,1,0:T(2,128)(2,1)S(1)}, u32[]{:S(2)}) copy-start(bf16[1,2,1024]{2,1,0:T(2,128)(2,1)S(1)} %fusion.25) | copy-start | bytes 12292
  167.2 59.1 %copy-start.4 = (f32[128,1024]{1,0:T(8,128)S(1)}, f32[128,1024]{1,0:T(8,128)}, u32[]{:S(2)}) copy-start(f32[128,1024]{1,0:T(8,128)} %param.14) | copy-start | bytes 1572868
  167.2 59.1 %copy-start.5 = (f32[128,1024]{1,0:T(8,128)S(1)}, f32[128,1024]{1,0:T(8,128)}, u32[]{:S(2)}) copy-start(f32[128,1024]{1,0:T(8,128)} %param.15) | copy-start | bytes 1572868
  167.2 59.1 %copy-start.6 = (f32[4,1024]{1,0:T(4,128)S(1)}, f32[4,1024]{1,0:T(4,128)}, u32[]{:S(2)}) copy-start(f32[4,1024]{1,0:T(4,128)} %param.17) | copy-start | bytes 49156
  167.2 59.1 %copy-start.7 = (f32[4,1024]{1,0:T(4,128)S(1)}, f32[4,1024]{1,0:T(4,128)}, u32[]{:S(2)}) copy-start(f32[4,1024]{1,0:T(4,128)} %param.16) | copy-start | bytes 49156
Sparse Core Ops, SparseCore 0:
  57.4 72.3 all-reduce.3
where the time goes:
time: 239 us; the launch traced here: 238 us
  waiting for transfers between devices  70.8 us (30%)
  loops' own time  67.9 us (28%)
  blocking collectives  35.7 us (15%)
  matrix products  24.8 us (10%)
  local copies, waits for them, and re-layouts  23.9 us (10%)
  between operations  14.8 us (6%)
    unnamed x2, waiting for transfers between devices  70.8 us
    another operation x1, loops' own time, body(): backprojected_totals = lax.fori_loop(0, max_tiles, back_tile, empty_sums)  41.6 us
    all_gather x1, blocking collectives, body(): gathered = lax.all_gather(view_rows, 'slab', axis=0, tiled=True)  30.5 us
    another operation x1, loops' own time, body(): lax.fori_loop(0, max_tiles, add_tile, jnp.zeros((rows_total, n_views, det...  26.3 us
    dot_general x8, matrix products, back_tile(): lax.dot_general(row_tiles[tile_idx], res_block, (((0,), (0,)), ((), ())),...  7.55 us
    dot_general x8, matrix products, add_tile(): jnp.dot(row_tiles[tile_idx], vox_block, preferred_element_type=jnp.float32)  6.62 us
    dot_general x1, matrix products, body(): jnp.einsum('zt,vtu->vzu', volume.astype(jnp.bfloat16), footprint, preferr...  5.85 us
    dynamic_slice x8, local copies, waits for them, and re-layouts, back_tile(): block_id = tile_block[tile_idx]  5.2 us
  transfers between devices with their start and end apart: 1, of which 1 were waited for; matrix products, arithmetic and copies ran while one was open for 0% of the time, Pallas kernels for 0%

commit v1 on v0

v1 whole, which is shorter than its diff:
```python
import functools

import jax
import jax.numpy as jnp
from jax import lax
from jax.experimental import pallas as pl
from jax.experimental.pallas import tpu as pltpu
from jax.sharding import PartitionSpec as P

LANES = 128
WINDOW = 144
F32 = jnp.float32
BF16 = jnp.bfloat16


def segment_of(pos, width, n_seg):
    first = jnp.floor((pos - width - 0.5) * (1.0 / LANES))
    return jnp.clip(first, 0.0, n_seg - 1.0)


def segment_masks(pos_ref, wid_ref, mask_ref):
    n_views, cols = pos_ref.shape
    n_seg = mask_ref.shape[1]
    seg_ids = lax.broadcasted_iota(jnp.int32, (n_seg, cols), 0).astype(F32)
    for v in range(n_views):
        seg = segment_of(pos_ref[v : v + 1, :], wid_ref[v : v + 1, :], n_seg)
        mask_ref[v] = (seg_ids == seg).astype(F32)


def repeated_tiles(tiles_ref, count_ref, n_seg):
    n_slots, tile_rows, depth = tiles_ref.shape
    tiles = tiles_ref[...].astype(F32)
    rows = []
    for s in range(n_slots):
        live = (s < count_ref[0]).astype(F32)
        for r in range(tile_rows):
            rows.append(jnp.broadcast_to(tiles[s, r : r + 1, :] * live, (n_seg, depth)))
    return jnp.concatenate(rows, axis=0).astype(BF16)


def line_of(detector_row, view, n_views, own_rows):
    owner = detector_row // own_rows
    return (owner * n_views + view) * own_rows + detector_row % own_rows


def project_kernel(
    view_ref, block_ref, count_ref, place_ref, vol_ref, pos_ref, wid_ref, meas_ref, rw_ref, tiles_ref,
    sum_ref, send_ref, win_ref, mask_ref, terms_ref,
):
    n_views, cols = pos_ref.shape
    n_seg = mask_ref.shape[1]
    n_slots, tile_rows, _ = tiles_ref.shape
    shared_views, own_rows, _ = meas_ref.shape
    slab, trans = place_ref[0], place_ref[1]
    slot_rows = tile_rows * n_seg
    lines = sum_ref.shape[0] // n_seg - n_views * own_rows
    segment_masks(pos_ref, wid_ref, mask_ref)
    offsets = lax.broadcasted_iota(jnp.int32, (WINDOW, cols), 0).astype(F32)
    for v in range(n_views):
        pos, wid = pos_ref[v : v + 1, :], wid_ref[v : v + 1, :]
        start = segment_of(pos, wid, n_seg) * LANES + 0.5 - pos
        distance = jnp.abs(offsets + start) * (1.0 / wid)
        win_ref[v] = jnp.maximum(0.0, 1.0 - distance).astype(BF16)
    tiles = repeated_tiles(tiles_ref, count_ref, n_seg)
    rows = jnp.dot(tiles, vol_ref[...].astype(BF16), preferred_element_type=F32)
    terms_ref[...] = jnp.zeros_like(terms_ref)
    for s in range(n_slots):
        view = view_ref[s]
        mask = mask_ref[view]
        spread = rows[s * slot_rows : (s + 1) * slot_rows] * jnp.concatenate([mask] * tile_rows, axis=0)
        terms_ref[s * slot_rows : (s + 1) * slot_rows, :WINDOW] = lax.dot_general(
            spread.astype(BF16), win_ref[view], (((1,), (1,)), ((), ())), preferred_element_type=F32
        )
    over = pltpu.roll(terms_ref[:, LANES:], 1, 0)
    row_ids = lax.broadcasted_iota(jnp.int32, over.shape, 0)
    totals = terms_ref[:, :LANES] + jnp.where(row_ids % n_seg == 0, 0.0, over)
    sum_ref[...] = jnp.zeros_like(sum_ref)

    def place(line):
        return pl.ds(pl.multiple_of(line * n_seg, n_seg), n_seg)

    for s in range(n_slots):
        for r in range(tile_rows):
            k = (s * tile_rows + r) * n_seg
            at = place(line_of(block_ref[s] * tile_rows + r, view_ref[s], n_views, own_rows))
            sum_ref[at, :] = sum_ref[at, :] + totals[k : k + n_seg]
    for i in range(shared_views):
        view = trans * shared_views + i
        for j in range(own_rows):
            at = place((slab * n_views + view) * own_rows + j)
            sum_ref[at, :] = sum_ref[at, :] - folded(meas_ref, i, j, n_seg)
            sum_ref[place(lines + view * own_rows + j), :] = folded(rw_ref, i, j, n_seg)
    send_ref[...] = sum_ref[...].astype(BF16)


def folded(ref, i, j, n_seg):
    return jnp.concatenate([ref[i, j : j + 1, a * LANES : (a + 1) * LANES] for a in range(n_seg)], axis=0)


def update_kernel(
    view_ref, block_ref, count_ref, place_ref, vol_ref, cw_ref, pos_ref, wid_ref, tiles_ref, win_ref, res_ref, got_ref,
    upd_ref, out_ref, mask_ref, val_ref, near_ref, back_ref,
):
    n_views, cols = pos_ref.shape
    n_seg = mask_ref.shape[1]
    n_slots, tile_rows, _ = tiles_ref.shape
    shared_views, own_rows, _ = out_ref.shape
    slab, trans = place_ref[0], place_ref[1]
    slot_rows = tile_rows * n_seg
    segment_masks(pos_ref, wid_ref, mask_ref)
    tiles = repeated_tiles(tiles_ref, count_ref, n_seg)
    val_ref[...] = jnp.where(trans == 0, got_ref[...].astype(F32), res_ref[...].astype(F32))

    def taken(line):
        return val_ref[pl.ds(pl.multiple_of(line * n_seg, n_seg), n_seg), :]

    seg_ids = lax.broadcasted_iota(jnp.int32, (n_seg, LANES), 0)
    for s in range(n_slots):
        for r in range(tile_rows):
            k = (s * tile_rows + r) * n_seg
            line = taken(line_of(block_ref[s] * tile_rows + r, view_ref[s], n_views, own_rows))
            near_ref[k : k + n_seg, :LANES] = line
            near_ref[k : k + n_seg, LANES:] = jnp.where(seg_ids == n_seg - 1, 0.0, pltpu.roll(line, n_seg - 1, 0))
    near = near_ref[:, :WINDOW].astype(BF16)
    for s in range(n_slots):
        view = view_ref[s]
        mask = mask_ref[view]
        part = jnp.dot(near[s * slot_rows : (s + 1) * slot_rows], win_ref[view], preferred_element_type=F32)
        back_ref[s * slot_rows : (s + 1) * slot_rows, :] = (part * jnp.concatenate([mask] * tile_rows, axis=0)).astype(BF16)
    gradient = lax.dot_general(tiles, back_ref[...], (((0,), (0,)), ((), ())), preferred_element_type=F32)
    upd_ref[...] = vol_ref[...] + 0.9 * cw_ref[...] * gradient
    for i in range(shared_views):
        for j in range(own_rows):
            line = taken((slab * n_views + trans * shared_views + i) * own_rows + j).astype(BF16)
            for a in range(n_seg):
                out_ref[i, j : j + 1, a * LANES : (a + 1) * LANES] = line[a : a + 1]


def body(
    volume, col_weight, foot_pos, foot_width, measured, row_weight, row_tiles, tile_view_index, tile_block, tile_count
):
    n_views = foot_pos.shape[0]
    shared_views, own_rows, det_cols = measured.shape
    n_slots, tile_rows, depth = row_tiles.shape
    n_slab, n_trans = lax.axis_size("slab"), lax.axis_size("trans")
    n_seg = det_cols // LANES
    cols = volume.shape[1]
    lines = n_slab * n_views * own_rows
    own_lines = n_views * own_rows
    all_rows = n_slots * tile_rows * n_seg
    slab, trans = lax.axis_index("slab"), lax.axis_index("trans")
    place = jnp.stack([slab, trans]).astype(jnp.int32)
    smem, vmem = pl.BlockSpec(memory_space=pltpu.SMEM), pl.BlockSpec(memory_space=pltpu.VMEM)
    params = pltpu.CompilerParams(vmem_limit_bytes=32 * 1024 * 1024)
    sent = ((lines + own_lines) * n_seg, LANES)
    sums, first, windows = pl.pallas_call(
        project_kernel,
        out_shape=(
            jax.ShapeDtypeStruct(sent, F32),
            jax.ShapeDtypeStruct(sent, BF16),
            jax.ShapeDtypeStruct((n_views, WINDOW, cols), BF16),
        ),
        in_specs=[smem] * 4 + [vmem] * 6,
        out_specs=(vmem,) * 3,
        scratch_shapes=[pltpu.VMEM((n_views, n_seg, cols), F32), pltpu.VMEM((all_rows, 2 * LANES), F32)],
        compiler_params=params,
        name="project",
    )(tile_view_index, tile_block, tile_count, place, volume, foot_pos, foot_width, measured, row_weight, row_tiles)
    sums = sums + lax.ppermute(first, "trans", [(0, 1)]).astype(F32)
    partial, weights = sums[: lines * n_seg], sums[lines * n_seg :].astype(BF16)
    step = 1
    while step < n_slab:
        pairs = [(i * n_trans + 1, (i ^ step) * n_trans + 1) for i in range(n_slab)]
        got = lax.ppermute(jnp.concatenate([partial.astype(BF16), weights], axis=0), ("slab", "trans"), pairs)
        partial = partial + got[: lines * n_seg].astype(F32)
        theirs = got[lines * n_seg :]
        upper = (slab & step) != 0
        weights = jnp.concatenate([jnp.where(upper, theirs, weights), jnp.where(upper, weights, theirs)], axis=0)
        step *= 2
    residual_lines = (-partial * weights.astype(F32)).astype(BF16)
    other = lax.ppermute(residual_lines, "trans", [(1, 0)])
    return pl.pallas_call(
        update_kernel,
        out_shape=(
            jax.ShapeDtypeStruct(volume.shape, F32),
            jax.ShapeDtypeStruct(measured.shape, BF16),
        ),
        in_specs=[smem] * 4 + [vmem] * 8,
        out_specs=(vmem,) * 2,
        scratch_shapes=[
            pltpu.VMEM((n_views, n_seg, cols), F32),
            pltpu.VMEM((lines * n_seg, LANES), F32),
            pltpu.VMEM((all_rows, 2 * LANES), F32),
            pltpu.VMEM((all_rows, cols), BF16),
        ],
        compiler_params=params,
        name="update",
    )(
        tile_view_index, tile_block, tile_count, place, volume, col_weight, foot_pos, foot_width, row_tiles, windows,
        residual_lines, other,
    )


def solution(mesh):
    in_specs = (
        P(("groups", "slab"), "trans"),
        P(("groups", "slab"), "trans"),
        P(None, "trans"),
        P(None, "trans"),
        P(("groups", "trans"), "slab", None),
        P(("groups", "trans"), "slab", None),
        P(("groups", "slab"), None, None),
        P(("groups", "slab")),
        P(("groups", "slab")),
        P(("groups", "slab")),
    )
    out_specs = (P(("groups", "slab"), "trans"), P(("groups", "trans"), "slab", None))
    return jax.shard_map(body, mesh=mesh, in_specs=in_specs, out_specs=out_specs, check_vma=False)
```

time: 239 us -> 36 us (0.15)
  loops' own time: 67.9 us -> 0 us
  waiting for transfers between devices: 70.8 us -> 17.2 us
  blocking collectives: 35.7 us -> 0 us
  matrix products: 24.8 us -> 0 us
  local copies, waits for them, and re-layouts: 23.9 us -> 6.52 us
  between operations: 14.8 us -> 1.54 us
  starting transfers between devices: 0.04 us -> 5.78 us
  Pallas kernels: 0 us -> 4.1 us
    unnamed x2 -> x0, waiting for transfers between devices: 70.8 us -> none
    another operation x2 -> x0, loops' own time: 67.9 us -> none  [the longest x1 41.6 us: body(): backprojected_totals = lax.fori_loop(0, max_tiles, back_tile, empty_sums)]
    all_gather x2 -> x0, blocking collectives: 32.3 us -> none  [the longest x1 30.5 us: body(): gathered = lax.all_gather(view_rows, 'slab', axis=0, tiled=True)]
    dot_general x18 -> x0, matrix products: 24.8 us -> none  [the longest x8 7.55 us: back_tile(): lax.dot_general(row_tiles[tile_idx], res_block, (((0,), (0,)), ((), ())),...]
    dynamic_slice x40 -> x0, local copies, waits for them, and re-layouts: 19.4 us -> none  [the longest x8 5.2 us: back_tile(): block_id = tile_block[tile_idx]]
    ppermute x0 -> x5, waiting for transfers between devices: none -> 17.2 us  [the longest x1 16.3 us: body(): other = lax.ppermute(residual_lines, 'trans', [(1, 0)])]
    ppermute x0 -> x5, starting transfers between devices: none -> 5.78 us  [the longest x1 2.49 us: body(): sums = sums + lax.ppermute(first, 'trans', [(0, 1)]).astype(F32)]
    pallas_call x0 -> x2, Pallas kernels: none -> 4.1 us  [the longest x1 2.13 us: body(): pl.pallas_call(project_kernel, out_shape=(jax.ShapeDtypeStruct(sent, F32)...]
  transfers between devices with their start and end apart: 1 -> 5, of which waited for: 1 -> 2; matrix products, arithmetic and copies ran while one was open for 0% -> 0% of each run, Pallas kernels for 0% -> 0%
where the time goes in v1:
time: 36 us; the launch traced here: 35.4 us
  waiting for transfers between devices  17.2 us (48%)
  local copies, waits for them, and re-layouts  6.52 us (18%)
  starting transfers between devices  5.78 us (16%)
  Pallas kernels  4.1 us (11%)
  between operations  1.54 us (4%)
    ppermute x1, waiting for transfers between devices, body(): other = lax.ppermute(residual_lines, 'trans', [(1, 0)])  16.3 us
    unnamed x30, local copies, waits for them, and re-layouts  5.91 us
    ppermute x1, starting transfers between devices, body(): sums = sums + lax.ppermute(first, 'trans', [(0, 1)]).astype(F32)  2.49 us
    pallas_call x1, Pallas kernels, body(): pl.pallas_call(project_kernel, out_shape=(jax.ShapeDtypeStruct(sent, F32)...  2.13 us
    ppermute x3, starting transfers between devices, body(): lax.ppermute(jnp.concatenate([partial.astype(BF16), weights], axis=0), ('...  2 us
    pallas_call x1, Pallas kernels, body(): pl.pallas_call(update_kernel, out_shape=(jax.ShapeDtypeStruct(volume.shap...  1.98 us
    ppermute x1, starting transfers between devices, body(): other = lax.ppermute(residual_lines, 'trans', [(1, 0)])  1.29 us
    ppermute x1, waiting for transfers between devices, body(): sums = sums + lax.ppermute(first, 'trans', [(0, 1)]).astype(F32)  0.89 us
  transfers between devices with their start and end apart: 5, of which 2 were waited for; matrix products, arithmetic and copies ran while one was open for 0% of the time, Pallas kernels for 0%

profile of v1, /device:TPU:0, one launch (start us, length us, event | category | flops | bytes accessed | tf_op | source)
XLA Modules:
  0.0 35.4 jit_solution(12819606284674841795)
XLA Ops:
  1.3 0.1 pad_add_fusion.place_ref
  1.4 0.0 copy-start
  1.4 1.0 %copy-done = f32[128,1024]{1,0:T(8,128)S(1)} copy-done((f32[128,1024]{1,0:T(8,128)S(1)}, f32[128,1024]{1,0:T(8,128)}, u32[]{:S(2)}) %copy-start) | copy-done | bytes 524312
  2.4 0.0 copy-start.3
  2.4 0.7 %copy-done.3 = f32[4,1024]{1,0:T(4,128)S(1)} copy-done((f32[4,1024]{1,0:T(4,128)S(1)}, f32[4,1024]{1,0:T(4,128)}, u32[]{:S(2)}) %copy-start.3) | copy-done | bytes 16408
  3.1 0.0 copy-start.5
  3.1 0.7 %copy-done.5 = f32[4,1024]{1,0:T(4,128)S(1)} copy-done((f32[4,1024]{1,0:T(4,128)S(1)}, f32[4,1024]{1,0:T(4,128)}, u32[]{:S(2)}) %copy-start.5) | copy-done | bytes 16408
  3.8 0.0 copy-start.7
  3.8 0.7 %copy-done.7 = bf16[8,2,128]{2,1,0:T(2,128)(2,1)S(1)} copy-done((bf16[8,2,128]{2,1,0:T(2,128)(2,1)S(1)}, bf16[8,2,128]{2,1,0:T(2,128)(2,1)}, u32[]{:S(2)}) %copy-start.7) | copy-done | bytes 4120
  4.5 0.0 copy-start.9
  4.5 0.7 %copy-done.9 = f32[2,1,1024]{2,1,0:T(1,128)S(1)} copy-done((f32[2,1,1024]{2,1,0:T(1,128)S(1)}, f32[2,1,1024]{2,1,0:T(1,128)}, u32[]{:S(2)}) %copy-start.9) | copy-done | bytes 8216
  5.2 0.0 copy-start.10
  5.2 0.7 %copy-done.10 = f32[2,1,1024]{2,1,0:T(1,128)S(1)} copy-done((f32[2,1,1024]{2,1,0:T(1,128)S(1)}, f32[2,1,1024]{2,1,0:T(1,128)}, u32[]{:S(2)}) %copy-start.10) | copy-done | bytes 8216
  5.9 0.0 copy-start.11
  5.9 0.7 %copy-done.11 = s32[8]{0:T(128)S(1)} copy-done((s32[8]{0:T(128)S(1)}, s32[8]{0:T(128)}, u32[]{:S(2)}) %copy-start.11) | copy-done | bytes 56
  6.6 0.0 copy-start.13
  6.6 0.7 %copy-done.13 = s32[8]{0:T(128)S(1)} copy-done((s32[8]{0:T(128)S(1)}, s32[8]{0:T(128)}, u32[]{:S(2)}) %copy-start.13) | copy-done | bytes 56
  7.2 2.1 %project.1 = (f32[288,128]{1,0:T(8,128)S(1)}, bf16[288,128]{1,0:T(8,128)(2,1)S(1)}, bf16[4,144,1024]{2,1,0:T(8,128)(2,1)S(1)}) custom-call(s32[8]{0:T(128)S(1)} %copy-done.11, s32[8]{0:T(128)S(1)} %copy-done.13, s32[1]{0:T(128)S(6)} %copy.13.count_ref, s32[2]{0:T(128)S(1)} %pad_add_fusion.place_ref, f32[128,1024]{1,0:T(8,128)S(1)} %copy-done, ...), custom_call_target="tpu_custom_call" | custom-call | tf_op jit(solution)/shard_map/project/pallas_call | solution.py:156
  9.4 0.0 copy-start.1
  9.4 0.0 copy-start.2
  9.4 0.0 copy-start.4
  9.4 0.0 copy-start.6
  9.4 0.0 copy-start.8
  9.4 0.0 copy-start.12
  9.4 0.0 copy-start.14
  9.4 2.5 %collective-permute-start = (bf16[288,128]{1,0:T(8,128)(2,1)S(1)}, bf16[288,128]{1,0:T(8,128)(2,1)S(1)}, u32[]{:S(2)}, u32[]{:S(2)}) collective-permute-start(bf16[288,128]{1,0:T(8,128)(2,1)S(1)} %get-tuple-element.7), channel_id=1, source_target_pairs={{0,1},{2,3},{4,5},{6,7},{8,9},{10,11},{12,13},{14,15},{16,17},{18,... | collective-permute-start | bytes 221192 | tf_op jit(solution)/shard_map/ppermute | solution.py:169
  11.9 0.9 %collective-permute-done = bf16[288,128]{1,0:T(8,128)(2,1)S(1)} collective-permute-done((bf16[288,128]{1,0:T(8,128)(2,1)S(1)}, bf16[288,128]{1,0:T(8,128)(2,1)S(1)}, u32[]{:S(2)}, u32[]{:S(2)}) %collective-permute-start) | collective-permute-done | bytes 73760 | tf_op jit(solution)/shard_map/ppermute | solution.py:169
  12.9 0.7 %collective-permute-start.1 = (bf16[288,128]{1,0:T(8,128)(2,1)S(1)}, bf16[288,128]{1,0:T(8,128)(2,1)S(1)}, u32[]{:S(2)}, u32[]{:S(2)}) collective-permute-start(bf16[288,128]{1,0:T(8,128)(2,1)S(1)} %pad_maximum_fusion.2), channel_id=1, source_target_pairs={{1,3},{3,1},{5,7},{7,5},{9,11},{11,9},{13,15},{15,13},{17,19},{19,... | collective-permute-start | bytes 221192 | tf_op jit(solution)/shard_map/ppermute | solution.py:174
  13.6 0.0 collective-permute-done.1
  13.6 0.7 %collective-permute-start.2 = (bf16[320,128]{1,0:T(8,128)(2,1)S(1)}, bf16[320,128]{1,0:T(8,128)(2,1)S(1)}, u32[]{:S(2)}, u32[]{:S(2)}) collective-permute-start(bf16[320,128]{1,0:T(8,128)(2,1)S(1)} %pad_maximum_fusion.1), channel_id=1, source_target_pairs={{1,5},{3,7},{5,1},{7,3},{9,13},{11,15},{13,9},{15,11},{17,21},{19,... | collective-permute-start | bytes 245768 | tf_op jit(solution)/shard_map/ppermute | solution.py:174
  14.3 0.0 collective-permute-done.2
  14.4 0.7 %collective-permute-start.3 = (bf16[384,128]{1,0:T(8,128)(2,1)S(1)}, bf16[384,128]{1,0:T(8,128)(2,1)S(1)}, u32[]{:S(2)}, u32[]{:S(2)}) collective-permute-start(bf16[384,128]{1,0:T(8,128)(2,1)S(1)} %pad_maximum_fusion), channel_id=1, source_target_pairs={{1,9},{3,11},{5,13},{7,15},{9,1},{11,3},{13,5},{15,7},{17,25},{19,... | collective-permute-start | bytes 294920 | tf_op jit(solution)/shard_map/ppermute | solution.py:174
  15.1 0.0 collective-permute-done.3
  15.1 0.1 multiply_convert_fusion.res_ref
  15.2 1.3 %collective-permute-start.4 = (bf16[256,128]{1,0:T(8,128)(2,1)S(1)}, bf16[256,128]{1,0:T(8,128)(2,1)S(1)}, u32[]{:S(2)}, u32[]{:S(2)}) collective-permute-start(bf16[256,128]{1,0:T(8,128)(2,1)S(1)} %multiply_convert_fusion.res_ref), channel_id=1, source_target_pairs={{1,0},{3,2},{5,4},{7,6},{9,8},{11,10},{13,12},{15,14},{17,16},{19,... | collective-permute-start | bytes 196616 | tf_op jit(solution)/shard_map/ppermute | solution.py:181
  16.5 16.3 %collective-permute-done.4.got_ref = bf16[256,128]{1,0:T(8,128)(2,1)S(1)} collective-permute-done((bf16[256,128]{1,0:T(8,128)(2,1)S(1)}, bf16[256,128]{1,0:T(8,128)(2,1)S(1)}, u32[]{:S(2)}, u32[]{:S(2)}) %collective-permute-start.4) | collective-permute-done | bytes 65568 | tf_op jit(solution)/shard_map/ppermute | solution.py:181
  32.8 0.0 copy-done.1
  32.8 0.0 copy-done.2
  32.8 0.0 copy-done.4
  32.8 0.0 copy-done.6
  32.8 0.0 copy-done.8
  32.9 0.0 copy-done.12
  32.9 0.0 copy-done.14
  32.9 2.0 %update.1 = (f32[128,1024]{1,0:T(8,128)}, bf16[2,1,1024]{2,1,0:T(2,128)(2,1)S(1)}) custom-call(s32[8]{0:T(128)S(1)} %copy-done.12, s32[8]{0:T(128)S(1)} %copy-done.14, s32[1]{0:T(128)S(6)} %copy.13.count_ref, s32[2]{0:T(128)S(1)} %pad_add_fusion.place_ref, f32[128,1024]{1,0:T(8,128)S(1)} %copy-done.1, f32[128,1024]{1,0:T(8,128)S(1)} %copy-done.2, ...), custom_call_target="tpu_custom_call" | custom-call | tf_op jit(solution)/shard_map/update/pallas_call | solution.py:182
  34.8 0.6 %copy.12 = bf16[2,1,1024]{2,0,1:T(2,128)(2,1)} copy(bf16[2,1,1024]{2,1,0:T(2,128)(2,1)S(1)} %get-tuple-element.9) | data formatting | bytes 8192 | tf_op jit(solution)/shard_map/update/pallas_call | solution.py:182
  (11 shorter events, 0.2 us)
Async XLA Ops:
  1.4 1.0 %copy-start = (f32[128,1024]{1,0:T(8,128)S(1)}, f32[128,1024]{1,0:T(8,128)}, u32[]{:S(2)}) copy-start(f32[128,1024]{1,0:T(8,128)} %vol_ref.3) | copy-start | bytes 1572868
  2.4 0.7 %copy-start.3 = (f32[4,1024]{1,0:T(4,128)S(1)}, f32[4,1024]{1,0:T(4,128)}, u32[]{:S(2)}) copy-start(f32[4,1024]{1,0:T(4,128)} %pos_ref.3) | copy-start | bytes 49156
  3.1 0.7 %copy-start.5 = (f32[4,1024]{1,0:T(4,128)S(1)}, f32[4,1024]{1,0:T(4,128)}, u32[]{:S(2)}) copy-start(f32[4,1024]{1,0:T(4,128)} %wid_ref.3) | copy-start | bytes 49156
  3.8 0.7 %copy-start.7 = (bf16[8,2,128]{2,1,0:T(2,128)(2,1)S(1)}, bf16[8,2,128]{2,1,0:T(2,128)(2,1)}, u32[]{:S(2)}) copy-start(bf16[8,2,128]{2,1,0:T(2,128)(2,1)} %tiles_ref.3) | copy-start | bytes 12292
  4.5 0.7 %copy-start.9 = (f32[2,1,1024]{2,1,0:T(1,128)S(1)}, f32[2,1,1024]{2,1,0:T(1,128)}, u32[]{:S(2)}) copy-start(f32[2,1,1024]{2,1,0:T(1,128)} %meas_ref.1) | copy-start | bytes 24580
  5.2 0.7 %copy-start.10 = (f32[2,1,1024]{2,1,0:T(1,128)S(1)}, f32[2,1,1024]{2,1,0:T(1,128)}, u32[]{:S(2)}) copy-start(f32[2,1,1024]{2,1,0:T(1,128)} %rw_ref.1) | copy-start | bytes 24580
  5.9 0.7 %copy-start.11 = (s32[8]{0:T(128)S(1)}, s32[8]{0:T(128)}, u32[]{:S(2)}) copy-start(s32[8]{0:T(128)} %view_ref.3) | copy-start | bytes 100
  6.6 0.7 %copy-start.13 = (s32[8]{0:T(128)S(1)}, s32[8]{0:T(128)}, u32[]{:S(2)}) copy-start(s32[8]{0:T(128)} %block_ref.3) | copy-start | bytes 100
  9.4 23.5 %copy-start.1 = (f32[128,1024]{1,0:T(8,128)S(1)}, f32[128,1024]{1,0:T(8,128)}, u32[]{:S(2)}) copy-start(f32[128,1024]{1,0:T(8,128)} %vol_ref.3) | copy-start | bytes 1572868
  9.4 23.4 %copy-start.2 = (f32[128,1024]{1,0:T(8,128)S(1)}, f32[128,1024]{1,0:T(8,128)}, u32[]{:S(2)}) copy-start(f32[128,1024]{1,0:T(8,128)} %cw_ref.1) | copy-start | bytes 1572868
  9.4 23.4 %copy-start.4 = (f32[4,1024]{1,0:T(4,128)S(1)}, f32[4,1024]{1,0:T(4,128)}, u32[]{:S(2)}) copy-start(f32[4,1024]{1,0:T(4,128)} %pos_ref.3) | copy-start | bytes 49156
  9.4 23.4 %copy-start.6 = (f32[4,1024]{1,0:T(4,128)S(1)}, f32[4,1024]{1,0:T(4,128)}, u32[]{:S(2)}) copy-start(f32[4,1024]{1,0:T(4,128)} %wid_ref.3) | copy-start | bytes 49156
  9.4 23.4 %copy-start.8 = (bf16[8,2,128]{2,1,0:T(2,128)(2,1)S(1)}, bf16[8,2,128]{2,1,0:T(2,128)(2,1)}, u32[]{:S(2)}) copy-start(bf16[8,2,128]{2,1,0:T(2,128)(2,1)} %tiles_ref.3) | copy-start | bytes 12292
  9.4 23.4 %copy-start.12 = (s32[8]{0:T(128)S(1)}, s32[8]{0:T(128)}, u32[]{:S(2)}) copy-start(s32[8]{0:T(128)} %view_ref.3) | copy-start | bytes 100
  9.4 23.4 %copy-start.14 = (s32[8]{0:T(128)S(1)}, s32[8]{0:T(128)}, u32[]{:S(2)}) copy-start(s32[8]{0:T(128)} %block_ref.3) | copy-start | bytes 100
  9.4 3.4 %collective-permute-start = (bf16[288,128]{1,0:T(8,128)(2,1)S(1)}, bf16[288,128]{1,0:T(8,128)(2,1)S(1)}, u32[]{:S(2)}, u32[]{:S(2)}) collective-permute-start(bf16[288,128]{1,0:T(8,128)(2,1)S(1)} %get-tuple-element.7), channel_id=1, source_target_pairs={{0,1},{2,3},{4,5},{6,7},{8,9},{10,11},{12,13},{14,15},{16,17},{18,... | collective-permute-start | bytes 221192 | tf_op jit(solution)/shard_map/ppermute | solution.py:169
  12.9 0.7 %collective-permute-start.1 = (bf16[288,128]{1,0:T(8,128)(2,1)S(1)}, bf16[288,128]{1,0:T(8,128)(2,1)S(1)}, u32[]{:S(2)}, u32[]{:S(2)}) collective-permute-start(bf16[288,128]{1,0:T(8,128)(2,1)S(1)} %pad_maximum_fusion.2), channel_id=1, source_target_pairs={{1,3},{3,1},{5,7},{7,5},{9,11},{11,9},{13,15},{15,13},{17,19},{19,... | collective-permute-start | bytes 221192 | tf_op jit(solution)/shard_map/ppermute | solution.py:174
  13.6 0.7 %collective-permute-start.2 = (bf16[320,128]{1,0:T(8,128)(2,1)S(1)}, bf16[320,128]{1,0:T(8,128)(2,1)S(1)}, u32[]{:S(2)}, u32[]{:S(2)}) collective-permute-start(bf16[320,128]{1,0:T(8,128)(2,1)S(1)} %pad_maximum_fusion.1), channel_id=1, source_target_pairs={{1,5},{3,7},{5,1},{7,3},{9,13},{11,15},{13,9},{15,11},{17,21},{19,... | collective-permute-start | bytes 245768 | tf_op jit(solution)/shard_map/ppermute | solution.py:174
  14.4 0.7 %collective-permute-start.3 = (bf16[384,128]{1,0:T(8,128)(2,1)S(1)}, bf16[384,128]{1,0:T(8,128)(2,1)S(1)}, u32[]{:S(2)}, u32[]{:S(2)}) collective-permute-start(bf16[384,128]{1,0:T(8,128)(2,1)S(1)} %pad_maximum_fusion), channel_id=1, source_target_pairs={{1,9},{3,11},{5,13},{7,15},{9,1},{11,3},{13,5},{15,7},{17,25},{19,... | collective-permute-start | bytes 294920 | tf_op jit(solution)/shard_map/ppermute | solution.py:174
  15.2 17.6 %collective-permute-start.4 = (bf16[256,128]{1,0:T(8,128)(2,1)S(1)}, bf16[256,128]{1,0:T(8,128)(2,1)S(1)}, u32[]{:S(2)}, u32[]{:S(2)}) collective-permute-start(bf16[256,128]{1,0:T(8,128)(2,1)S(1)} %multiply_convert_fusion.res_ref), channel_id=1, source_target_pairs={{1,0},{3,2},{5,4},{7,6},{9,8},{11,10},{13,12},{15,14},{17,16},{19,... | collective-permute-start | bytes 196616 | tf_op jit(solution)/shard_map/ppermute | solution.py:181

commit v2 on v1

v2 whole, which is shorter than its diff:
```python
import jax
import jax.numpy as jnp
from jax import lax
from jax.experimental import pallas as pl
from jax.experimental.pallas import tpu as pltpu
from jax.sharding import PartitionSpec as P

LANES = 128
WINDOW = 144
F32 = jnp.float32
BF16 = jnp.bfloat16


def parity(index):
    for shift in (8, 4, 2, 1):
        index = index ^ (index >> shift)
    return index & 1


def my_place():
    slab, trans = lax.axis_index("slab"), lax.axis_index("trans")
    return slab, trans, trans ^ parity(slab)


def segment_of(pos, width, n_seg):
    first = jnp.floor((pos - width - 0.5) * (1.0 / LANES))
    return jnp.clip(first, 0.0, n_seg - 1.0)


def repeated_tiles(tiles_ref, count_ref, n_seg):
    n_slots, tile_rows, depth = tiles_ref.shape
    tiles = tiles_ref[...].astype(F32)
    rows = []
    for s in range(n_slots):
        live = (s < count_ref[0]).astype(F32)
        for r in range(tile_rows):
            rows.append(jnp.broadcast_to(tiles[s, r : r + 1, :] * live, (n_seg, depth)))
    return jnp.concatenate(rows, axis=0).astype(BF16)


def line_of(detector_row, view, shared_views, own_rows, half_lines):
    owner = detector_row // own_rows
    inside = (owner * shared_views + view % shared_views) * own_rows + detector_row % own_rows
    return (view // shared_views) * half_lines + inside


def rows_of(line, n_seg):
    return pl.ds(pl.multiple_of(line * n_seg, n_seg), n_seg)


def folded(ref, i, j, n_seg):
    return jnp.concatenate([ref[i, j : j + 1, a * LANES : (a + 1) * LANES] for a in range(n_seg)], axis=0)


def project_kernel(
    view_hbm, block_hbm, vol_hbm, pos_hbm, wid_hbm, meas_hbm, rw_hbm, tiles_hbm, count_ref,
    keep_ref, send_ref, win_ref, mask_ref, wide_ref,
    view_ref, block_ref, vol_ref, pos_ref, wid_ref, meas_ref, rw_ref, tiles_ref, sum_ref, terms_ref, sems,
):
    inputs = (pos_hbm, wid_hbm, vol_hbm, tiles_hbm, view_hbm, block_hbm, meas_hbm, rw_hbm)
    holders = (pos_ref, wid_ref, vol_ref, tiles_ref, view_ref, block_ref, meas_ref, rw_ref)
    copies = [pltpu.make_async_copy(a, b, sems.at[i]) for i, (a, b) in enumerate(zip(inputs, holders))]
    for copy in copies:
        copy.start()
    n_views, cols = pos_ref.shape
    n_slots, tile_rows, _ = tiles_ref.shape
    shared_views, own_rows, det_cols = meas_ref.shape
    n_seg = det_cols // LANES
    slab, trans, half = my_place()
    slot_rows = tile_rows * n_seg
    half_rows = keep_ref.shape[0]
    half_lines = half_rows // n_seg
    sum_ref[...] = jnp.zeros_like(sum_ref)
    terms_ref[:, LANES:] = jnp.zeros((terms_ref.shape[0], LANES), F32)
    seg_ids = lax.broadcasted_iota(jnp.int32, (n_seg, cols), 0).astype(F32)
    offsets = lax.broadcasted_iota(jnp.int32, (WINDOW, cols), 0).astype(F32)
    copies[0].wait()
    copies[1].wait()
    for v in range(n_views):
        pos, wid = pos_ref[v : v + 1, :], wid_ref[v : v + 1, :]
        seg = segment_of(pos, wid, n_seg)
        mask_ref[v] = (seg_ids == seg).astype(F32)
        distance = jnp.abs(offsets + (seg * LANES + 0.5 - pos)) * (1.0 / wid)
        win_ref[v] = jnp.maximum(0.0, 1.0 - distance).astype(BF16)
    for copy in copies[2:]:
        copy.wait()
    tiles = repeated_tiles(tiles_ref, count_ref, n_seg)
    wide_ref[...] = tiles
    rows = jnp.dot(tiles, vol_ref[...].astype(BF16), preferred_element_type=F32)
    for s in range(n_slots):
        view = view_ref[s]
        mask = mask_ref[view]
        spread = rows[s * slot_rows : (s + 1) * slot_rows] * jnp.concatenate([mask] * tile_rows, axis=0)
        terms_ref[s * slot_rows : (s + 1) * slot_rows, :WINDOW] = lax.dot_general(
            spread.astype(BF16), win_ref[view], (((1,), (1,)), ((), ())), preferred_element_type=F32
        )
    over = pltpu.roll(terms_ref[:, LANES:], 1, 0)
    row_ids = lax.broadcasted_iota(jnp.int32, over.shape, 0)
    totals = terms_ref[:, :LANES] + jnp.where(row_ids % n_seg == 0, 0.0, over)
    for s in range(n_slots):
        for r in range(tile_rows):
            k = (s * tile_rows + r) * n_seg
            line = line_of(block_ref[s] * tile_rows + r, view_ref[s], shared_views, own_rows, half_lines)
            at = rows_of(line, n_seg)
            sum_ref[at, :] = sum_ref[at, :] + totals[k : k + n_seg]
    for i in range(shared_views):
        for j in range(own_rows):
            line = line_of(slab * own_rows + j, trans * shared_views + i, shared_views, own_rows, half_lines)
            at = rows_of(line, n_seg)
            sum_ref[at, :] = sum_ref[at, :] - folded(meas_ref, i, j, n_seg)
    keep_ref[...] = sum_ref[pl.ds(pl.multiple_of(half * half_rows, n_seg), half_rows), :]
    away = sum_ref[pl.ds(pl.multiple_of((1 - half) * half_rows, n_seg), half_rows), :]
    weights = [folded(rw_ref, i, j, n_seg) for i in range(shared_views) for j in range(own_rows)]
    send_ref[...] = jnp.concatenate([away] + weights, axis=0).astype(BF16)


def update_kernel(
    view_ref, block_ref, vol_ref, cw_ref, wide_ref, win_ref, mask_ref, res_ref, got_ref,
    upd_hbm, out_ref,
    val_ref, near_ref, back_ref, upd_ref, sems,
):
    n_views, n_seg, cols = mask_ref.shape
    n_slots = view_ref.shape[0]
    shared_views, own_rows, _ = out_ref.shape
    tile_rows = near_ref.shape[0] // (n_slots * n_seg)
    slab, trans, half = my_place()
    slot_rows = tile_rows * n_seg
    half_rows = res_ref.shape[0]
    half_lines = half_rows // n_seg
    val_ref[pl.ds(pl.multiple_of(half * half_rows, n_seg), half_rows), :] = res_ref[...].astype(F32)
    val_ref[pl.ds(pl.multiple_of((1 - half) * half_rows, n_seg), half_rows), :] = got_ref[...].astype(F32)

    def taken(detector_row, view):
        return val_ref[rows_of(line_of(detector_row, view, shared_views, own_rows, half_lines), n_seg), :]

    seg_ids = lax.broadcasted_iota(jnp.int32, (n_seg, LANES), 0)
    for s in range(n_slots):
        for r in range(tile_rows):
            k = (s * tile_rows + r) * n_seg
            line = taken(block_ref[s] * tile_rows + r, view_ref[s])
            near_ref[k : k + n_seg, :LANES] = line
            near_ref[k : k + n_seg, LANES:] = jnp.where(seg_ids == n_seg - 1, 0.0, pltpu.roll(line, n_seg - 1, 0))
    near = near_ref[:, :WINDOW].astype(BF16)
    for s in range(n_slots):
        view = view_ref[s]
        mask = mask_ref[view]
        part = jnp.dot(near[s * slot_rows : (s + 1) * slot_rows], win_ref[view], preferred_element_type=F32)
        back_ref[s * slot_rows : (s + 1) * slot_rows, :] = (part * jnp.concatenate([mask] * tile_rows, axis=0)).astype(BF16)
    n_parts = sems.shape[0]
    width = cols // n_parts
    copies = []
    for p in range(n_parts):
        at = slice(p * width, (p + 1) * width)
        gradient = lax.dot_general(
            wide_ref[...], back_ref[:, at], (((0,), (0,)), ((), ())), preferred_element_type=F32
        )
        upd_ref[:, at] = vol_ref[:, at] + 0.9 * cw_ref[:, at] * gradient
        copies.append(pltpu.make_async_copy(upd_ref.at[:, at], upd_hbm.at[:, at], sems.at[p]))
        copies[-1].start()
    for i in range(shared_views):
        for j in range(own_rows):
            line = taken(slab * own_rows + j, trans * shared_views + i).astype(BF16)
            for a in range(n_seg):
                out_ref[i, j : j + 1, a * LANES : (a + 1) * LANES] = line[a : a + 1]
    for copy in copies:
        copy.wait()


def exchange(array, slab_mask, n_slab, n_trans):
    pairs = []
    for i in range(n_slab):
        for k in range(n_trans):
            pairs.append((i * n_trans + k, (i ^ slab_mask) * n_trans + (k ^ parity(slab_mask))))
    return lax.ppermute(array, ("slab", "trans"), pairs)


def in_order(blocks, index):
    step = 1
    while step < len(blocks):
        odd = (index & step) != 0
        blocks = [jnp.where(odd, blocks[q ^ step], blocks[q]) for q in range(len(blocks))]
        step *= 2
    return blocks


def body(
    volume, col_weight, foot_pos, foot_width, measured, row_weight, row_tiles, tile_view_index, tile_block, tile_count
):
    n_views = foot_pos.shape[0]
    shared_views, own_rows, det_cols = measured.shape
    n_slots, tile_rows, depth = row_tiles.shape
    n_slab, n_trans = lax.axis_size("slab"), lax.axis_size("trans")
    assert n_trans == 2 and n_slab & (n_slab - 1) == 0
    n_seg = det_cols // LANES
    cols = volume.shape[1]
    half_rows = n_slab * shared_views * own_rows * n_seg
    own = shared_views * own_rows * n_seg
    all_rows = n_slots * tile_rows * n_seg
    smem, vmem = pl.BlockSpec(memory_space=pltpu.SMEM), pl.BlockSpec(memory_space=pltpu.VMEM)
    hbm = pl.BlockSpec(memory_space=pltpu.HBM)
    params = pltpu.CompilerParams(vmem_limit_bytes=32 * 1024 * 1024)
    keep, send, windows, masks, wide = pl.pallas_call(
        project_kernel,
        out_shape=(
            jax.ShapeDtypeStruct((half_rows, LANES), F32),
            jax.ShapeDtypeStruct((half_rows + own, LANES), BF16),
            jax.ShapeDtypeStruct((n_views, WINDOW, cols), BF16),
            jax.ShapeDtypeStruct((n_views, n_seg, cols), F32),
            jax.ShapeDtypeStruct((all_rows, depth), BF16),
        ),
        in_specs=[hbm] * 8 + [smem],
        out_specs=(vmem,) * 5,
        scratch_shapes=[
            pltpu.SMEM(tile_view_index.shape, jnp.int32),
            pltpu.SMEM(tile_block.shape, jnp.int32),
            pltpu.VMEM(volume.shape, F32),
            pltpu.VMEM(foot_pos.shape, F32),
            pltpu.VMEM(foot_width.shape, F32),
            pltpu.VMEM(measured.shape, F32),
            pltpu.VMEM(row_weight.shape, F32),
            pltpu.VMEM(row_tiles.shape, BF16),
            pltpu.VMEM((n_trans * half_rows, LANES), F32),
            pltpu.VMEM((all_rows, 2 * LANES), F32),
            pltpu.SemaphoreType.DMA((8,)),
        ],
        compiler_params=params,
        name="project",
    )(
        *[
            pltpu.with_memory_space_constraint(array, pltpu.HBM)
            for array in (tile_view_index, tile_block, volume, foot_pos, foot_width, measured, row_weight, row_tiles)
        ],
        tile_count,
    )

    slab, trans, half = my_place()
    got = lax.ppermute(send, "trans", [(0, 1), (1, 0)])
    partial = keep + got[:half_rows].astype(F32)
    weights = jnp.where(half == trans, send[half_rows:], got[half_rows:])
    bit = 1
    while bit < n_slab:
        radix = 2 if (n_slab // bit).bit_length() % 2 == 0 else 4
        sent = jnp.concatenate([partial.astype(BF16), weights], axis=0)
        arrived = [exchange(sent, m * bit, n_slab, n_trans) for m in range(1, radix)]
        for other in arrived:
            partial = partial + other[:half_rows].astype(F32)
        blocks = [weights] + [other[half_rows:] for other in arrived]
        weights = jnp.concatenate(in_order(blocks, slab // bit), axis=0)
        bit *= radix
    residual_lines = (-partial * weights.astype(F32)).astype(BF16)
    other_lines = lax.ppermute(residual_lines, "trans", [(0, 1), (1, 0)])

    n_parts = 4
    return pl.pallas_call(
        update_kernel,
        out_shape=(
            jax.ShapeDtypeStruct(volume.shape, F32),
            jax.ShapeDtypeStruct(measured.shape, BF16),
        ),
        in_specs=[smem] * 2 + [vmem] * 7,
        out_specs=(hbm, vmem),
        scratch_shapes=[
            pltpu.VMEM((n_trans * half_rows, LANES), F32),
            pltpu.VMEM((all_rows, 2 * LANES), F32),
            pltpu.VMEM((all_rows, cols), BF16),
            pltpu.VMEM(volume.shape, F32),
            pltpu.SemaphoreType.DMA((n_parts,)),
        ],
        compiler_params=params,
        name="update",
    )(tile_view_index, tile_block, volume, col_weight, wide, windows, masks, residual_lines, other_lines)


def solution(mesh):
    in_specs = (
        P(("groups", "slab"), "trans"),
        P(("groups", "slab"), "trans"),
        P(None, "trans"),
        P(None, "trans"),
        P(("groups", "trans"), "slab", None),
        P(("groups", "trans"), "slab", None),
        P(("groups", "slab"), None, None),
        P(("groups", "slab")),
        P(("groups", "slab")),
        P(("groups", "slab")),
    )
    out_specs = (P(("groups", "slab"), "trans"), P(("groups", "trans"), "slab", None))
    return jax.shard_map(body, mesh=mesh, in_specs=in_specs, out_specs=out_specs, check_vma=False)
```

time: 36 us -> 22.5 us (0.62)
  waiting for transfers between devices: 17.2 us -> 7.94 us
  local copies, waits for them, and re-layouts: 6.52 us -> 0.61 us
  starting transfers between devices: 5.78 us -> 7.92 us
    ppermute x5 -> x6, waiting for transfers between devices: 17.2 us -> 7.94 us  [the longest x4 5.98 us: exchange(): return lax.ppermute(array, ('slab', 'trans'), pairs)]
    unnamed x30 -> x8, local copies, waits for them, and re-layouts: 5.91 us -> 0.02 us
    ppermute x5 -> x6, starting transfers between devices: 5.78 us -> 7.92 us  [the longest x4 7.23 us: exchange(): return lax.ppermute(array, ('slab', 'trans'), pairs)]
  transfers between devices with their start and end apart: 5 -> 6, of which waited for: 2 -> 5; matrix products, arithmetic and copies ran while one was open for 0% -> 0% of each run, Pallas kernels for 0% -> 0%
where the time goes in v2:
time: 22.5 us; the launch traced here: 22.2 us
  waiting for transfers between devices  7.94 us (35%)
  starting transfers between devices  7.92 us (35%)
  Pallas kernels  4.15 us (18%)
  between operations  1.47 us (7%)
  local copies, waits for them, and re-layouts  0.61 us (3%)
    ppermute x4, starting transfers between devices, exchange(): return lax.ppermute(array, ('slab', 'trans'), pairs)  7.23 us
    ppermute x4, waiting for transfers between devices, exchange(): return lax.ppermute(array, ('slab', 'trans'), pairs)  5.98 us
    pallas_call x1, Pallas kernels, body(): pl.pallas_call(project_kernel, out_shape=(jax.ShapeDtypeStruct((half_rows...  2.2 us
    pallas_call x1, Pallas kernels, body(): pl.pallas_call(update_kernel, out_shape=(jax.ShapeDtypeStruct(volume.shap...  1.95 us
    ppermute x1, waiting for transfers between devices, body(): other_lines = lax.ppermute(residual_lines, 'trans', [(0, 1), (1, 0)])  1.09 us
    ppermute x1, waiting for transfers between devices, body(): got = lax.ppermute(send, 'trans', [(0, 1), (1, 0)])  0.87 us
    pallas_call x1, local copies, waits for them, and re-layouts, body(): pl.pallas_call(update_kernel, out_shape=(jax.ShapeDtypeStruct(volume.shap...  0.6 us
    ppermute x1, starting transfers between devices, body(): got = lax.ppermute(send, 'trans', [(0, 1), (1, 0)])  0.51 us
  transfers between devices with their start and end apart: 6, of which 5 were waited for; matrix products, arithmetic and copies ran while one was open for 0% of the time, Pallas kernels for 0%

profile of v2, /device:TPU:0, one launch (start us, length us, event | category | flops | bytes accessed | tf_op | source)
XLA Modules:
  0.0 22.2 jit_solution(10758388648522354666)
XLA Ops:
  0.6 0.0 copy-start.3
  0.6 0.0 copy-start.2
  0.7 0.0 copy-start
  0.7 0.0 copy-start.1
  1.4 2.2 %project.1 = (f32[128,128]{1,0:T(8,128)S(1)}, bf16[144,128]{1,0:T(8,128)(2,1)S(1)}, bf16[4,144,1024]{2,1,0:T(8,128)(2,1)S(1)}, f32[4,8,1024]{2,1,0:T(8,128)S(1)}, bf16[128,128]{1,0:T(8,128)(2,1)S(1)}) custom-call(s32[8]{0:T(128)} %view_ref.1, s32[8]{0:T(128)} %block_ref.1, f32[128,1024]{1,0:T(8,128)} %vol_ref.1, f32[4,1024]{1,0:T(4,128)} %pos_hbm.1, ...), custom_call_target="tpu_custom_call" | custom-call | tf_op jit(solution)/shard_map/project/pallas_call | solution.py:202
  3.6 0.5 %collective-permute-start = (bf16[144,128]{1,0:T(8,128)(2,1)S(1)}, bf16[144,128]{1,0:T(8,128)(2,1)S(1)}, u32[]{:S(2)}, u32[]{:S(2)}) collective-permute-start(bf16[144,128]{1,0:T(8,128)(2,1)S(1)} %get-tuple-element.11), channel_id=1, source_target_pairs={{0,1},{1,0},{2,3},{3,2},{4,5},{5,4},{6,7},{7,6},{8,9},{9,8},{10,11... | collective-permute-start | bytes 110600 | tf_op jit(solution)/shard_map/ppermute | solution.py:237
  4.1 0.9 %collective-permute-done = bf16[144,128]{1,0:T(8,128)(2,1)S(1)} collective-permute-done((bf16[144,128]{1,0:T(8,128)(2,1)S(1)}, bf16[144,128]{1,0:T(8,128)(2,1)S(1)}, u32[]{:S(2)}, u32[]{:S(2)}) %collective-permute-start) | collective-permute-done | bytes 36896 | tf_op jit(solution)/shard_map/ppermute | solution.py:237
  5.0 2.7 %collective-permute-start.1 = (bf16[144,128]{1,0:T(8,128)(2,1)S(1)}, bf16[144,128]{1,0:T(8,128)(2,1)S(1)}, u32[]{:S(2)}, u32[]{:S(2)}) collective-permute-start(bf16[144,128]{1,0:T(8,128)(2,1)S(1)} %pad_maximum_fusion.1), channel_id=1, source_target_pairs={{0,3},{1,2},{2,1},{3,0},{4,7},{5,6},{6,5},{7,4},{8,11},{9,10},{10,... | collective-permute-start | bytes 110600 | tf_op jit(solution)/shard_map/ppermute | solution.py:174
  7.7 1.6 %collective-permute-done.1 = bf16[144,128]{1,0:T(8,128)(2,1)S(1)} collective-permute-done((bf16[144,128]{1,0:T(8,128)(2,1)S(1)}, bf16[144,128]{1,0:T(8,128)(2,1)S(1)}, u32[]{:S(2)}, u32[]{:S(2)}) %collective-permute-start.1) | collective-permute-done | bytes 36896 | tf_op jit(solution)/shard_map/ppermute | solution.py:174
  9.4 4.2 %collective-permute-start.4 = (bf16[160,128]{1,0:T(8,128)(2,1)S(1)}, bf16[160,128]{1,0:T(8,128)(2,1)S(1)}, u32[]{:S(2)}, u32[]{:S(2)}) collective-permute-start(bf16[160,128]{1,0:T(8,128)(2,1)S(1)} %pad_maximum_fusion), channel_id=1, source_target_pairs={{0,12},{1,13},{2,14},{3,15},{4,8},{5,9},{6,10},{7,11},{8,4},{9,5},... | collective-permute-start | bytes 122888 | tf_op jit(solution)/shard_map/ppermute | solution.py:174
  13.6 0.0 collective-permute-start.3
  13.6 0.4 %collective-permute-start.2 = (bf16[160,128]{1,0:T(8,128)(2,1)S(1)}, bf16[160,128]{1,0:T(8,128)(2,1)S(1)}, u32[]{:S(2)}, u32[]{:S(2)}) collective-permute-start(bf16[160,128]{1,0:T(8,128)(2,1)S(1)} %pad_maximum_fusion), channel_id=1, source_target_pairs={{0,5},{1,4},{2,7},{3,6},{4,1},{5,0},{6,3},{7,2},{8,13},{9,12},{10,... | collective-permute-start | bytes 122888 | tf_op jit(solution)/shard_map/ppermute | solution.py:174
  14.0 1.7 %collective-permute-done.4 = bf16[160,128]{1,0:T(8,128)(2,1)S(1)} collective-permute-done((bf16[160,128]{1,0:T(8,128)(2,1)S(1)}, bf16[160,128]{1,0:T(8,128)(2,1)S(1)}, u32[]{:S(2)}, u32[]{:S(2)}) %collective-permute-start.4) | collective-permute-done | bytes 40992 | tf_op jit(solution)/shard_map/ppermute | solution.py:174
  15.6 2.7 %collective-permute-done.3 = bf16[160,128]{1,0:T(8,128)(2,1)S(1)} collective-permute-done((bf16[160,128]{1,0:T(8,128)(2,1)S(1)}, bf16[160,128]{1,0:T(8,128)(2,1)S(1)}, u32[]{:S(2)}, u32[]{:S(2)}) %collective-permute-start.3) | collective-permute-done | bytes 40992 | tf_op jit(solution)/shard_map/ppermute | solution.py:174
  18.3 0.0 collective-permute-done.2
  18.4 0.2 collective-permute-start.5
  18.6 1.1 %collective-permute-done.5.got_ref = bf16[128,128]{1,0:T(8,128)(2,1)S(1)} collective-permute-done((bf16[128,128]{1,0:T(8,128)(2,1)S(1)}, bf16[128,128]{1,0:T(8,128)(2,1)S(1)}, u32[]{:S(2)}, u32[]{:S(2)}) %collective-permute-start.5) | collective-permute-done | bytes 32800 | tf_op jit(solution)/shard_map/ppermute | solution.py:251
  19.7 0.0 copy-done.3
  19.7 0.0 copy-done.2
  19.7 0.0 copy-done
  19.7 0.0 copy-done.1
  19.7 2.0 %update.1 = (f32[128,1024]{1,0:T(8,128)}, bf16[2,1,1024]{2,1,0:T(2,128)(2,1)S(1)}) custom-call(s32[8]{0:T(128)S(1)} %copy-done.2, s32[8]{0:T(128)S(1)} %copy-done.3, f32[128,1024]{1,0:T(8,128)S(1)} %copy-done, f32[128,1024]{1,0:T(8,128)S(1)} %copy-done.1, bf16[128,128]{1,0:T(8,128)(2,1)S(1)} %get-tuple-element.7.wide_ref, ...), custom_call_target="tpu_custom_call" | custom-call | tf_op jit(solution)/shard_map/update/pallas_call | solution.py:254
  21.6 0.6 %copy.12 = bf16[2,1,1024]{2,0,1:T(2,128)(2,1)} copy(bf16[2,1,1024]{2,1,0:T(2,128)(2,1)S(1)} %get-tuple-element.13) | data formatting | bytes 8192 | tf_op jit(solution)/shard_map/update/pallas_call | solution.py:254
  (9 shorter events, 0.1 us)
Async XLA Ops:
  0.6 19.0 %copy-start.3 = (s32[8]{0:T(128)S(1)}, s32[8]{0:T(128)}, u32[]{:S(2)}) copy-start(s32[8]{0:T(128)} %block_ref.1) | copy-start | bytes 100
  0.6 19.0 %copy-start.2 = (s32[8]{0:T(128)S(1)}, s32[8]{0:T(128)}, u32[]{:S(2)}) copy-start(s32[8]{0:T(128)} %view_ref.1) | copy-start | bytes 100
  0.7 19.0 %copy-start = (f32[128,1024]{1,0:T(8,128)S(1)}, f32[128,1024]{1,0:T(8,128)}, u32[]{:S(2)}) copy-start(f32[128,1024]{1,0:T(8,128)} %vol_ref.1) | copy-start | bytes 1572868
  0.7 19.0 %copy-start.1 = (f32[128,1024]{1,0:T(8,128)S(1)}, f32[128,1024]{1,0:T(8,128)}, u32[]{:S(2)}) copy-start(f32[128,1024]{1,0:T(8,128)} %cw_ref.1) | copy-start | bytes 1572868
  3.6 1.4 %collective-permute-start = (bf16[144,128]{1,0:T(8,128)(2,1)S(1)}, bf16[144,128]{1,0:T(8,128)(2,1)S(1)}, u32[]{:S(2)}, u32[]{:S(2)}) collective-permute-start(bf16[144,128]{1,0:T(8,128)(2,1)S(1)} %get-tuple-element.11), channel_id=1, source_target_pairs={{0,1},{1,0},{2,3},{3,2},{4,5},{5,4},{6,7},{7,6},{8,9},{9,8},{10,11... | collective-permute-start | bytes 110600 | tf_op jit(solution)/shard_map/ppermute | solution.py:237
  5.0 4.3 %collective-permute-start.1 = (bf16[144,128]{1,0:T(8,128)(2,1)S(1)}, bf16[144,128]{1,0:T(8,128)(2,1)S(1)}, u32[]{:S(2)}, u32[]{:S(2)}) collective-permute-start(bf16[144,128]{1,0:T(8,128)(2,1)S(1)} %pad_maximum_fusion.1), channel_id=1, source_target_pairs={{0,3},{1,2},{2,1},{3,0},{4,7},{5,6},{6,5},{7,4},{8,11},{9,10},{10,... | collective-permute-start | bytes 110600 | tf_op jit(solution)/shard_map/ppermute | solution.py:174
  9.4 6.2 %collective-permute-start.4 = (bf16[160,128]{1,0:T(8,128)(2,1)S(1)}, bf16[160,128]{1,0:T(8,128)(2,1)S(1)}, u32[]{:S(2)}, u32[]{:S(2)}) collective-permute-start(bf16[160,128]{1,0:T(8,128)(2,1)S(1)} %pad_maximum_fusion), channel_id=1, source_target_pairs={{0,12},{1,13},{2,14},{3,15},{4,8},{5,9},{6,10},{7,11},{8,4},{9,5},... | collective-permute-start | bytes 122888 | tf_op jit(solution)/shard_map/ppermute | solution.py:174
  13.6 4.7 %collective-permute-start.3 = (bf16[160,128]{1,0:T(8,128)(2,1)S(1)}, bf16[160,128]{1,0:T(8,128)(2,1)S(1)}, u32[]{:S(2)}, u32[]{:S(2)}) collective-permute-start(bf16[160,128]{1,0:T(8,128)(2,1)S(1)} %pad_maximum_fusion), channel_id=1, source_target_pairs={{0,9},{1,8},{2,11},{3,10},{4,13},{5,12},{6,15},{7,14},{8,1},{9,0},... | collective-permute-start | bytes 122888 | tf_op jit(solution)/shard_map/ppermute | solution.py:174
  13.6 4.7 %collective-permute-start.2 = (bf16[160,128]{1,0:T(8,128)(2,1)S(1)}, bf16[160,128]{1,0:T(8,128)(2,1)S(1)}, u32[]{:S(2)}, u32[]{:S(2)}) collective-permute-start(bf16[160,128]{1,0:T(8,128)(2,1)S(1)} %pad_maximum_fusion), channel_id=1, source_target_pairs={{0,5},{1,4},{2,7},{3,6},{4,1},{5,0},{6,3},{7,2},{8,13},{9,12},{10,... | collective-permute-start | bytes 122888 | tf_op jit(solution)/shard_map/ppermute | solution.py:174
  18.4 1.3 %collective-permute-start.5 = (bf16[128,128]{1,0:T(8,128)(2,1)S(1)}, bf16[128,128]{1,0:T(8,128)(2,1)S(1)}, u32[]{:S(2)}, u32[]{:S(2)}) collective-permute-start(bf16[128,128]{1,0:T(8,128)(2,1)S(1)} %multiply_convert_fusion.res_ref), channel_id=1, source_target_pairs={{0,1},{1,0},{2,3},{3,2},{4,5},{5,4},{6,7},{7,6},{8,9},{9,8},{10,11... | collective-permute-start | bytes 98312 | tf_op jit(solution)/shard_map/ppermute | solution.py:251

commit v3 on v2

v3 whole, which is shorter than its diff:
```python
import jax
import jax.numpy as jnp
from jax import lax
from jax.experimental import pallas as pl
from jax.experimental.pallas import tpu as pltpu
from jax.sharding import PartitionSpec as P

LANES = 128
WINDOW = 144
GROUP = 8
META = 16
F32 = jnp.float32
BF16 = jnp.bfloat16


def iota(shape, dim):
    return lax.broadcasted_iota(jnp.int32, shape, dim)


def segment_of(pos, width, n_seg):
    first = jnp.floor((pos - width - 0.5) * (1.0 / LANES))
    return jnp.clip(first, 0.0, n_seg - 1.0)


def slot_vector(values, repeat, index):
    result = jnp.full(index.shape, values[0], jnp.int32)
    for s in range(1, len(values)):
        result = jnp.where(index >= s * repeat, values[s], result)
    return result


def slot_lines(view_ref, block_ref, count_ref, index, tile_rows, n_views, own_rows):
    n_slots = view_ref.shape[0]
    view = slot_vector([view_ref[s] for s in range(n_slots)], tile_rows, index)
    block = slot_vector([block_ref[s] for s in range(n_slots)], tile_rows, index)
    detector_row = block * tile_rows + index % tile_rows
    line = (detector_row // own_rows * n_views + view) * own_rows + detector_row % own_rows
    return jnp.where(index // tile_rows < count_ref[0], line, -1)


def project_kernel(
    view_hbm, vol_hbm, pos_hbm, wid_hbm, meas_hbm, rw_hbm, tiles_hbm,
    own_ref, send_ref, win_ref, key_ref, flat_ref,
    view_ref, vol_ref, pos_ref, wid_ref, meas_ref, rw_ref, tiles_ref, spread_ref, sems,
):
    inputs = (pos_hbm, wid_hbm, vol_hbm, tiles_hbm, view_hbm, meas_hbm, rw_hbm)
    holders = (pos_ref, wid_ref, vol_ref, tiles_ref, view_ref, meas_ref, rw_ref)
    copies = [pltpu.make_async_copy(a, b, sems.at[i]) for i, (a, b) in enumerate(zip(inputs, holders))]
    for copy in copies:
        copy.start()
    n_views, cols = pos_ref.shape
    n_slots, tile_rows, _ = tiles_ref.shape
    shared_views, own_rows, det_cols = meas_ref.shape
    n_seg = det_cols // LANES
    slot_rows = n_slots * tile_rows
    own_lines = n_views * own_rows
    trans = lax.axis_index("trans")
    offsets = iota((WINDOW, cols), 0).astype(F32)
    copies[0].wait()
    copies[1].wait()
    segments = []
    for v in range(n_views):
        pos, wid = pos_ref[v : v + 1, :], wid_ref[v : v + 1, :]
        seg = segment_of(pos, wid, n_seg)
        segments.append(seg + float(v * n_seg))
        distance = jnp.abs(offsets + (seg * LANES + 0.5 - pos)) * (1.0 / wid)
        win_ref[v] = jnp.maximum(0.0, 1.0 - distance).astype(BF16)
    for copy in copies[2:]:
        copy.wait()
    views = slot_vector([view_ref[s] for s in range(n_slots)], tile_rows, iota((slot_rows, cols), 0))
    key = jnp.broadcast_to(segments[0], (slot_rows, cols))
    for v in range(1, n_views):
        key = jnp.where(views == v, segments[v], key)
    key_ref[...] = key
    tiles = tiles_ref[...].astype(F32)
    flat = jnp.concatenate([tiles[s, r : r + 1, :] for s in range(n_slots) for r in range(tile_rows)], axis=0)
    flat = flat.astype(BF16)
    flat_ref[...] = flat
    rows = jnp.dot(flat, vol_ref[...].astype(BF16), preferred_element_type=F32)
    sums = jnp.zeros((n_seg * slot_rows, WINDOW), F32)
    for v in range(n_views):
        for a in range(n_seg):
            spread_ref[v, a * slot_rows : (a + 1) * slot_rows, :] = jnp.where(key == v * n_seg + a, rows, 0.0).astype(BF16)
        sums = sums + lax.dot_general(
            spread_ref[v], win_ref[v], (((1,), (1,)), ((), ())), preferred_element_type=F32
        )
    edge = WINDOW - LANES
    own_ref[: n_seg * slot_rows, :] = sums[:, :LANES]
    own_ref[slot_rows : n_seg * slot_rows, :edge] += sums[: (n_seg - 1) * slot_rows, LANES:]
    lines = own_ref.shape[0] // n_seg - slot_rows
    place = iota((lines, det_cols), 0)
    block = jnp.zeros((lines, det_cols), F32)
    for i in range(shared_views):
        for j in range(own_rows):
            at = (trans * shared_views + i) * own_rows + j
            block = jnp.where(place == at, rw_ref[i, j : j + 1, :], block)
            block = jnp.where(place == own_lines + at, meas_ref[i, j : j + 1, :], block)
    for a in range(n_seg):
        at = n_seg * slot_rows + a * lines
        own_ref[at : at + lines, :] = block[:, a * LANES : (a + 1) * LANES]
    send_ref[...] = own_ref[...].astype(BF16)


def join_kernel(view_ref, block_ref, count_ref, own_ref, got_ref, out_ref, *, tile_rows, n_views, own_rows):
    n_rows = own_ref.shape[0]
    out_ref[:n_rows, :] = (own_ref[...] + got_ref[...].astype(F32)).astype(BF16)
    shape = (META, LANES)
    index = iota(shape, 1) % (view_ref.shape[0] * tile_rows)
    line = slot_lines(view_ref, block_ref, count_ref, index, tile_rows, n_views, own_rows)
    part = jnp.where(iota(shape, 0) == 0, line & 127, line >> 7)
    out_ref[n_rows:, :] = part.astype(F32).astype(BF16)


def gather_kernel(*refs, masks, slot_rows, own_lines, n_seg):
    payloads, (part_ref, send_ref, all_ref) = refs[:-3], refs[-3:]
    slab, trans = lax.axis_index("slab"), lax.axis_index("trans")
    lines = part_ref.shape[0] // 2
    depth = all_ref.shape[0]
    n_sources = len(payloads)
    block_lines = (payloads[0].shape[0] - META) // n_seg - slot_rows
    first_block = n_sources * slot_rows
    lane = iota((1, depth), 1)
    sum_line = jnp.full((1, depth), -1, jnp.int32)
    weight_line = sum_line
    if first_block + n_sources * block_lines < depth:
        used = first_block + n_sources * block_lines
        all_ref[used:, :] = jnp.zeros((depth - used, all_ref.shape[1]), F32)
    for j, ref in enumerate(payloads):
        values = ref[...].astype(F32)
        mask = jnp.where(trans == 0, masks[j][0], masks[j][1])
        taken = mask >= 0
        meta = values[n_seg * (slot_rows + block_lines) :]
        line = (meta[0:1, :] + 128.0 * meta[1:2, :]).astype(jnp.int32)
        line = jnp.concatenate([line] * (depth // LANES), axis=1)
        here = (lane >= j * slot_rows) & (lane < (j + 1) * slot_rows)
        sum_line = jnp.where(here & taken, line, sum_line)
        at = first_block + j * block_lines
        inside = lane - at
        base = (slab ^ mask) * own_lines
        weights = (inside >= 0) & (inside < own_lines) & taken
        weight_line = jnp.where(weights, base + inside, weight_line)
        measured = (inside >= own_lines) & (inside < 2 * own_lines) & taken
        sum_line = jnp.where(measured, base + inside - own_lines, sum_line)
        for a in range(n_seg):
            lanes = slice(a * LANES, (a + 1) * LANES)
            all_ref[j * slot_rows : (j + 1) * slot_rows, lanes] = values[a * slot_rows : (a + 1) * slot_rows]
            start = n_seg * slot_rows + a * block_lines
            all_ref[at : at + block_lines, lanes] = values[start : start + block_lines]
    ids = iota((lines, depth), 0)
    sign = jnp.where(lane >= first_block, -1.0, 1.0)
    chosen = jnp.concatenate(
        [jnp.where(ids == sum_line, sign, 0.0), jnp.where(ids == weight_line, 1.0, 0.0)], axis=0
    )
    part = jnp.dot(chosen.astype(BF16), all_ref[...].astype(BF16), preferred_element_type=F32)
    part_ref[...] = part
    send_ref[...] = part.astype(BF16)


def update_kernel(
    view_ref, block_ref, count_ref, vol_ref, cw_ref, flat_ref, win_ref, key_ref, part_ref, got_ref,
    upd_hbm, out_hbm,
    val_ref, near_ref, upd_ref, out_ref, sems, out_sem,
):
    n_views, _, cols = win_ref.shape
    own_rows, shared_views, det_cols = out_ref.shape
    n_seg = det_cols // LANES
    slot_rows = key_ref.shape[0]
    tile_rows = slot_rows // view_ref.shape[0]
    slab, trans = lax.axis_index("slab"), lax.axis_index("trans")
    lines = part_ref.shape[0] // 2
    total = part_ref[...] + got_ref[...].astype(F32)
    residual = (-total[:lines] * total[lines:]).astype(BF16)
    val_ref[...] = residual.astype(F32)
    line = slot_lines(view_ref, block_ref, count_ref, iota((slot_rows, lines), 0), tile_rows, n_views, own_rows)
    chosen = jnp.where(iota((slot_rows, lines), 1) == line, 1.0, 0.0).astype(BF16)
    near = jnp.dot(chosen, residual, preferred_element_type=F32).astype(BF16)
    for a in range(n_seg):
        at = slice(a * slot_rows, (a + 1) * slot_rows)
        near_ref[at, :LANES] = near[:, a * LANES : (a + 1) * LANES]
        if a + 1 < n_seg:
            near_ref[at, LANES:] = near[:, (a + 1) * LANES : (a + 2) * LANES]
        else:
            near_ref[at, LANES:] = jnp.zeros((slot_rows, LANES), BF16)
    n_parts = sems.shape[0]
    width = cols // n_parts
    copies = []
    for p in range(n_parts):
        at = slice(p * width, (p + 1) * width)
        key = key_ref[:, at]
        back = jnp.zeros((slot_rows, width), F32)
        for v in range(n_views):
            part = jnp.dot(near_ref[:, :WINDOW], win_ref[v, :, at], preferred_element_type=F32)
            for a in range(n_seg):
                back = jnp.where(key == v * n_seg + a, part[a * slot_rows : (a + 1) * slot_rows], back)
        gradient = lax.dot_general(
            flat_ref[...], back.astype(BF16), (((0,), (0,)), ((), ())), preferred_element_type=F32
        )
        upd_ref[:, at] = vol_ref[:, at] + 0.9 * cw_ref[:, at] * gradient
        copies.append(pltpu.make_async_copy(upd_ref.at[:, at], upd_hbm.at[:, at], sems.at[p]))
        copies[-1].start()
    for i in range(shared_views):
        for j in range(own_rows):
            line = (slab * n_views + trans * shared_views + i) * own_rows + j
            out_ref[j, i : i + 1, :] = val_ref[pl.ds(line, 1), :].astype(BF16)
    copies.append(pltpu.make_async_copy(out_ref, out_hbm, out_sem))
    copies[-1].start()
    for copy in copies:
        copy.wait()


def exchange(array, masks, n_slab):
    pairs = []
    for i in range(n_slab):
        for k, mask in enumerate(masks):
            pairs.append(((i ^ mask) * len(masks) + k, i * len(masks) + k))
    return lax.ppermute(array, ("slab", "trans"), pairs)


def direct_masks(n_group):
    far = list(range(n_group // 2, n_group))
    near = list(range(1, n_group // 2))
    return [(near[j] if j < len(near) else None, mask) for j, mask in enumerate(far)]


def body(
    volume, col_weight, foot_pos, foot_width, measured, row_weight, row_tiles, tile_view_index, tile_block, tile_count
):
    n_views, cols = foot_pos.shape
    shared_views, own_rows, det_cols = measured.shape
    n_slots, tile_rows, depth = row_tiles.shape
    n_slab, n_trans = lax.axis_size("slab"), lax.axis_size("trans")
    assert n_trans == 2 and n_slab & (n_slab - 1) == 0 and n_slab > 1
    n_seg = det_cols // LANES
    slot_rows = n_slots * tile_rows
    own_lines = n_views * own_rows
    lines = n_slab * own_lines
    block_lines = -(-2 * own_lines // 8) * 8
    first_rows = n_seg * (slot_rows + block_lines)
    smem, vmem = pl.BlockSpec(memory_space=pltpu.SMEM), pl.BlockSpec(memory_space=pltpu.VMEM)
    hbm = pl.BlockSpec(memory_space=pltpu.HBM)
    params = pltpu.CompilerParams(vmem_limit_bytes=32 * 1024 * 1024)
    near = (tile_view_index, volume, foot_pos, foot_width, measured, row_weight, row_tiles)
    own, send, windows, key, flat = pl.pallas_call(
        project_kernel,
        out_shape=(
            jax.ShapeDtypeStruct((first_rows, LANES), F32),
            jax.ShapeDtypeStruct((first_rows, LANES), BF16),
            jax.ShapeDtypeStruct((n_views, WINDOW, cols), BF16),
            jax.ShapeDtypeStruct((slot_rows, cols), F32),
            jax.ShapeDtypeStruct((slot_rows, depth), BF16),
        ),
        in_specs=[hbm] * 7,
        out_specs=(vmem,) * 5,
        scratch_shapes=[
            pltpu.SMEM(tile_view_index.shape, jnp.int32),
            pltpu.VMEM(volume.shape, F32),
            pltpu.VMEM(foot_pos.shape, F32),
            pltpu.VMEM(foot_width.shape, F32),
            pltpu.VMEM(measured.shape, F32),
            pltpu.VMEM(row_weight.shape, F32),
            pltpu.VMEM(row_tiles.shape, BF16),
            pltpu.VMEM((n_views, n_seg * slot_rows, cols), BF16),
            pltpu.SemaphoreType.DMA((7,)),
        ],
        compiler_params=params,
        name="project",
    )(*[pltpu.with_memory_space_constraint(array, pltpu.HBM) for array in near])

    swap = [(0, 1), (1, 0)]
    got = lax.ppermute(send, "trans", swap)
    tile_count, own = lax.optimization_barrier((tile_count, own))

    def join(*args):
        join_kernel(*args, tile_rows=tile_rows, n_views=n_views, own_rows=own_rows)

    payload = pl.pallas_call(
        join,
        out_shape=jax.ShapeDtypeStruct((first_rows + META, LANES), BF16),
        in_specs=[smem] * 3 + [vmem] * 2,
        out_specs=vmem,
        compiler_params=params,
        name="join",
    )(tile_view_index, tile_block, tile_count, own, got)

    n_group = min(GROUP, n_slab)
    steps = direct_masks(n_group)
    arrived = [exchange(payload, (1 if a is None else a, b), n_slab) for a, b in steps]
    masks = [(0, -1)] + [(-1 if a is None else a, b) for a, b in steps]

    def gather(*refs):
        gather_kernel(*refs, masks=masks, slot_rows=slot_rows, own_lines=own_lines, n_seg=n_seg)

    part_shape = (2 * lines, det_cols)
    all_depth = -(-len(masks) * (slot_rows + block_lines) // LANES) * LANES
    part, send = pl.pallas_call(
        gather,
        out_shape=(jax.ShapeDtypeStruct(part_shape, F32), jax.ShapeDtypeStruct(part_shape, BF16)),
        in_specs=[vmem] * len(masks),
        out_specs=(vmem,) * 2,
        scratch_shapes=[pltpu.VMEM((all_depth, det_cols), F32)],
        compiler_params=params,
        name="gather",
    )(payload, *arrived)
    bit = n_group
    while bit < n_slab:
        part = part + exchange(send, (bit, bit), n_slab).astype(F32)
        send = part.astype(BF16)
        bit *= 2
    other = lax.ppermute(send, "trans", swap)

    n_parts = 4
    updated, residual = pl.pallas_call(
        update_kernel,
        out_shape=(
            jax.ShapeDtypeStruct(volume.shape, F32),
            jax.ShapeDtypeStruct((own_rows, shared_views, det_cols), BF16),
        ),
        in_specs=[smem] * 3 + [vmem] * 7,
        out_specs=(hbm, hbm),
        scratch_shapes=[
            pltpu.VMEM((lines, det_cols), F32),
            pltpu.VMEM((n_seg * slot_rows, 2 * LANES), BF16),
            pltpu.VMEM(volume.shape, F32),
            pltpu.VMEM((own_rows, shared_views, det_cols), BF16),
            pltpu.SemaphoreType.DMA((n_parts,)),
            pltpu.SemaphoreType.DMA(()),
        ],
        compiler_params=params,
        name="update",
    )(tile_view_index, tile_block, tile_count, volume, col_weight, flat, windows, key, part, other)
    return updated, jnp.transpose(residual, (1, 0, 2))


def solution(mesh):
    in_specs = (
        P(("groups", "slab"), "trans"),
        P(("groups", "slab"), "trans"),
        P(None, "trans"),
        P(None, "trans"),
        P(("groups", "trans"), "slab", None),
        P(("groups", "trans"), "slab", None),
        P(("groups", "slab"), None, None),
        P(("groups", "slab")),
        P(("groups", "slab")),
        P(("groups", "slab")),
    )
    out_specs = (P(("groups", "slab"), "trans"), P(("groups", "trans"), "slab", None))
    return jax.shard_map(body, mesh=mesh, in_specs=in_specs, out_specs=out_specs, check_vma=False)
```

time: 22.5 us -> 22.1 us (0.982)
  waiting for transfers between devices: 7.94 us -> 3.49 us
  starting transfers between devices: 7.92 us -> 10 us
  local copies, waits for them, and re-layouts: 0.61 us -> 1.97 us
  Pallas kernels: 4.15 us -> 5.11 us
    ppermute x4, waiting for transfers between devices: 5.98 us -> 2.27 us  [exchange(): return lax.ppermute(array, ('slab', 'trans'), pairs)]
    ppermute x2, starting transfers between devices: 0.7 us -> 3.64 us  [the longest x1 3.12 us: body(): other = lax.ppermute(send, 'trans', swap)]
    unnamed x8 -> x10, local copies, waits for them, and re-layouts: 0.02 us -> 1.97 us
    ppermute x4, starting transfers between devices: 7.23 us -> 6.39 us  [exchange(): return lax.ppermute(array, ('slab', 'trans'), pairs)]
    ppermute x2, waiting for transfers between devices: 1.96 us -> 1.22 us  [the longest x1 0.99 us: body(): other = lax.ppermute(send, 'trans', swap)]
    pallas_call x1 -> x0, local copies, waits for them, and re-layouts: 0.6 us -> none  [body(): pl.pallas_call(update_kernel, out_shape=(jax.ShapeDtypeStruct(volume.shap...]
    pallas_call x1 -> x3, Pallas kernels: 2.2 us -> 2.71 us  [the longest x1 1.96 us: body(): pl.pallas_call(project_kernel, out_shape=(jax.ShapeDtypeStruct((first_row...]
    pallas_call x1, Pallas kernels: 1.95 us -> 2.4 us  [body(): pl.pallas_call(update_kernel, out_shape=(jax.ShapeDtypeStruct(volume.shap...]
where the time goes in v3:
time: 22.1 us; the launch traced here: 21.9 us
  starting transfers between devices  10 us (45%)
  Pallas kernels  5.11 us (23%)
  waiting for transfers between devices  3.49 us (16%)
  local copies, waits for them, and re-layouts  1.97 us (9%)
  between operations  1.33 us (6%)
    ppermute x4, starting transfers between devices, exchange(): return lax.ppermute(array, ('slab', 'trans'), pairs)  6.39 us
    ppermute x1, starting transfers between devices, body(): other = lax.ppermute(send, 'trans', swap)  3.12 us
    pallas_call x1, Pallas kernels, body(): pl.pallas_call(update_kernel, out_shape=(jax.ShapeDtypeStruct(volume.shap...  2.4 us
    ppermute x4, waiting for transfers between devices, exchange(): return lax.ppermute(array, ('slab', 'trans'), pairs)  2.27 us
    unnamed x10, local copies, waits for them, and re-layouts  1.97 us
    pallas_call x1, Pallas kernels, body(): pl.pallas_call(project_kernel, out_shape=(jax.ShapeDtypeStruct((first_row...  1.96 us
    ppermute x1, waiting for transfers between devices, body(): other = lax.ppermute(send, 'trans', swap)  0.99 us
    pallas_call x1, Pallas kernels, body(): pl.pallas_call(join, out_shape=jax.ShapeDtypeStruct((first_rows + META, L...  0.57 us
  transfers between devices with their start and end apart: 6, of which 5 were waited for; matrix products, arithmetic and copies ran while one was open for 0% of the time, Pallas kernels for 0%

profile of v3, /device:TPU:0, one launch (start us, length us, event | category | flops | bytes accessed | tf_op | source)
XLA Modules:
  0.0 21.9 jit_solution(5730820984927302747)
XLA Ops:
  0.6 0.0 copy-start
  0.6 0.0 copy-start.1
  0.7 2.0 %project.1 = (f32[192,128]{1,0:T(8,128)S(1)}, bf16[192,128]{1,0:T(8,128)(2,1)S(1)}, bf16[4,144,1024]{2,1,0:T(8,128)(2,1)S(1)}, f32[16,1024]{1,0:T(8,128)S(1)}, bf16[16,128]{1,0:T(8,128)(2,1)S(1)}) custom-call(s32[8]{0:T(128)} %view_ref.1, f32[128,1024]{1,0:T(8,128)} %vol_ref.1, f32[4,1024]{1,0:T(4,128)} %pos_hbm.1, f32[4,1024]{1,0:T(4,128)} %wid_hbm.1, ...), custom_call_target="tpu_custom_call" | custom-call | tf_op jit(solution)/shard_map/project/pallas_call | solution.py:243
  2.6 0.5 %collective-permute-start = (bf16[192,128]{1,0:T(8,128)(2,1)S(1)}, bf16[192,128]{1,0:T(8,128)(2,1)S(1)}, u32[]{:S(2)}, u32[]{:S(2)}) collective-permute-start(bf16[192,128]{1,0:T(8,128)(2,1)S(1)} %get-tuple-element.19), channel_id=1, source_target_pairs={{0,1},{1,0},{2,3},{3,2},{4,5},{5,4},{6,7},{7,6},{8,9},{9,8},{10,11... | collective-permute-start | bytes 147464 | tf_op jit(solution)/shard_map/ppermute | solution.py:270
  3.8 0.2 %collective-permute-done.args_4_ = bf16[192,128]{1,0:T(8,128)(2,1)S(1)} collective-permute-done((bf16[192,128]{1,0:T(8,128)(2,1)S(1)}, bf16[192,128]{1,0:T(8,128)(2,1)S(1)}, u32[]{:S(2)}, u32[]{:S(2)}) %collective-permute-start) | collective-permute-done | bytes 49184 | tf_op jit(solution)/shard_map/ppermute | solution.py:270
  4.0 0.0 copy-start.2
  4.0 0.7 %copy-done.2 = s32[8]{0:T(128)S(1)} copy-done((s32[8]{0:T(128)S(1)}, s32[8]{0:T(128)}, u32[]{:S(2)}) %copy-start.2) | copy-done | bytes 56
  4.7 0.0 copy-start.4
  4.7 0.7 %copy-done.4 = s32[8]{0:T(128)S(1)} copy-done((s32[8]{0:T(128)S(1)}, s32[8]{0:T(128)}, u32[]{:S(2)}) %copy-start.4) | copy-done | bytes 56
  5.3 0.6 %join.1.refs_0_ = bf16[208,128]{1,0:T(8,128)(2,1)S(1)} custom-call(s32[8]{0:T(128)S(1)} %copy-done.2, s32[8]{0:T(128)S(1)} %copy-done.4, s32[1]{0:T(128)S(6)} %copy.12.args_2_.count_ref, f32[192,128]{1,0:T(8,128)S(1)} %get-tuple-element.18.args_3_, bf16[192,128]{1,0:T(8,128)(2,1)S(1)} %collective-permute-done.args_4_), custom_call_target="tpu_custom_call" | custom-call | tf_op jit(solution)/shard_map/join/pallas_call | solution.py:276
  5.9 2.9 %collective-permute-start.4 = (bf16[208,128]{1,0:T(8,128)(2,1)S(1)}, bf16[208,128]{1,0:T(8,128)(2,1)S(1)}, u32[]{:S(2)}, u32[]{:S(2)}) collective-permute-start(bf16[208,128]{1,0:T(8,128)(2,1)S(1)} %join.1.refs_0_), channel_id=1, source_target_pairs={{2,0},{15,1},{0,2},{13,3},{6,4},{11,5},{4,6},{9,7},{10,8},{7,9},{8... | collective-permute-start | bytes 159752 | tf_op jit(solution)/shard_map/ppermute | solution.py:216
  8.8 1.5 %collective-permute-start.3 = (bf16[208,128]{1,0:T(8,128)(2,1)S(1)}, bf16[208,128]{1,0:T(8,128)(2,1)S(1)}, u32[]{:S(2)}, u32[]{:S(2)}) collective-permute-start(bf16[208,128]{1,0:T(8,128)(2,1)S(1)} %join.1.refs_0_), channel_id=1, source_target_pairs={{6,0},{13,1},{4,2},{15,3},{2,4},{9,5},{0,6},{11,7},{14,8},{5,9},{1... | collective-permute-start | bytes 159752 | tf_op jit(solution)/shard_map/ppermute | solution.py:216
  10.3 0.0 collective-permute-start.2
  10.4 1.9 %collective-permute-start.1 = (bf16[208,128]{1,0:T(8,128)(2,1)S(1)}, bf16[208,128]{1,0:T(8,128)(2,1)S(1)}, u32[]{:S(2)}, u32[]{:S(2)}) collective-permute-start(bf16[208,128]{1,0:T(8,128)(2,1)S(1)} %join.1.refs_0_), channel_id=1, source_target_pairs={{2,0},{9,1},{0,2},{11,3},{6,4},{13,5},{4,6},{15,7},{10,8},{1,9},{8... | collective-permute-start | bytes 159752 | tf_op jit(solution)/shard_map/ppermute | solution.py:216
  12.3 0.0 collective-permute-done.4.refs_4_
  12.3 1.7 %collective-permute-done.3.refs_3_ = bf16[208,128]{1,0:T(8,128)(2,1)S(1)} collective-permute-done((bf16[208,128]{1,0:T(8,128)(2,1)S(1)}, bf16[208,128]{1,0:T(8,128)(2,1)S(1)}, u32[]{:S(2)}, u32[]{:S(2)}) %collective-permute-start.3) | collective-permute-done | bytes 53280 | tf_op jit(solution)/shard_map/ppermute | solution.py:216
  14.0 0.5 %collective-permute-done.2.refs_2_ = bf16[208,128]{1,0:T(8,128)(2,1)S(1)} collective-permute-done((bf16[208,128]{1,0:T(8,128)(2,1)S(1)}, bf16[208,128]{1,0:T(8,128)(2,1)S(1)}, u32[]{:S(2)}, u32[]{:S(2)}) %collective-permute-start.2) | collective-permute-done | bytes 53280 | tf_op jit(solution)/shard_map/ppermute | solution.py:216
  14.5 0.1 collective-permute-done.1.refs_1_
  14.6 0.2 gather.1
  14.8 3.1 %collective-permute-start.5 = (bf16[64,1024]{1,0:T(8,128)(2,1)S(1)}, bf16[64,1024]{1,0:T(8,128)(2,1)S(1)}, u32[]{:S(2)}, u32[]{:S(2)}) collective-permute-start(bf16[64,1024]{1,0:T(8,128)(2,1)S(1)} %get-tuple-element.21), channel_id=1, source_target_pairs={{0,1},{1,0},{2,3},{3,2},{4,5},{5,4},{6,7},{7,6},{8,9},{9,8},{10,11... | collective-permute-start | bytes 393224 | tf_op jit(solution)/shard_map/ppermute | solution.py:309
  17.9 1.0 %collective-permute-done.5.got_ref = bf16[64,1024]{1,0:T(8,128)(2,1)S(1)} collective-permute-done((bf16[64,1024]{1,0:T(8,128)(2,1)S(1)}, bf16[64,1024]{1,0:T(8,128)(2,1)S(1)}, u32[]{:S(2)}, u32[]{:S(2)}) %collective-permute-start.5) | collective-permute-done | bytes 131104 | tf_op jit(solution)/shard_map/ppermute | solution.py:309
  18.9 0.0 copy-done
  18.9 0.0 copy-done.1
  18.9 0.0 copy-start.3
  18.9 0.7 %copy-done.3 = s32[8]{0:T(128)S(1)} copy-done((s32[8]{0:T(128)S(1)}, s32[8]{0:T(128)}, u32[]{:S(2)}) %copy-start.3) | copy-done | bytes 56
  19.5 2.4 %update.1 = (f32[128,1024]{1,0:T(8,128)}, bf16[1,2,1024]{2,1,0:T(2,128)(2,1)}) custom-call(s32[8]{0:T(128)S(1)} %copy-done.3, s32[8]{0:T(128)S(1)} %copy-done.4, s32[1]{0:T(128)S(6)} %copy.12.args_2_.count_ref, f32[128,1024]{1,0:T(8,128)S(1)} %copy-done, f32[128,1024]{1,0:T(8,128)S(1)} %copy-done.1, bf16[16,128]{1,0:T(8,128)(2,1)S(1)} %get-tuple-element.15.flat_ref, ...), custom_call_target="tpu_custom_call" | custom-call | tf_op jit(solution)/shard_map/update/pallas_call | solution.py:312
Async XLA Ops:
  0.6 18.2 %copy-start = (f32[128,1024]{1,0:T(8,128)S(1)}, f32[128,1024]{1,0:T(8,128)}, u32[]{:S(2)}) copy-start(f32[128,1024]{1,0:T(8,128)} %vol_ref.1) | copy-start | bytes 1572868
  0.6 18.2 %copy-start.1 = (f32[128,1024]{1,0:T(8,128)S(1)}, f32[128,1024]{1,0:T(8,128)}, u32[]{:S(2)}) copy-start(f32[128,1024]{1,0:T(8,128)} %cw_ref.1) | copy-start | bytes 1572868
  2.6 1.4 %collective-permute-start = (bf16[192,128]{1,0:T(8,128)(2,1)S(1)}, bf16[192,128]{1,0:T(8,128)(2,1)S(1)}, u32[]{:S(2)}, u32[]{:S(2)}) collective-permute-start(bf16[192,128]{1,0:T(8,128)(2,1)S(1)} %get-tuple-element.19), channel_id=1, source_target_pairs={{0,1},{1,0},{2,3},{3,2},{4,5},{5,4},{6,7},{7,6},{8,9},{9,8},{10,11... | collective-permute-start | bytes 147464 | tf_op jit(solution)/shard_map/ppermute | solution.py:270
  4.0 0.7 %copy-start.2 = (s32[8]{0:T(128)S(1)}, s32[8]{0:T(128)}, u32[]{:S(2)}) copy-start(s32[8]{0:T(128)} %view_ref.1) | copy-start | bytes 100
  4.7 0.7 %copy-start.4 = (s32[8]{0:T(128)S(1)}, s32[8]{0:T(128)}, u32[]{:S(2)}) copy-start(s32[8]{0:T(128)} %block_ref.1) | copy-start | bytes 100
  5.9 6.4 %collective-permute-start.4 = (bf16[208,128]{1,0:T(8,128)(2,1)S(1)}, bf16[208,128]{1,0:T(8,128)(2,1)S(1)}, u32[]{:S(2)}, u32[]{:S(2)}) collective-permute-start(bf16[208,128]{1,0:T(8,128)(2,1)S(1)} %join.1.refs_0_), channel_id=1, source_target_pairs={{2,0},{15,1},{0,2},{13,3},{6,4},{11,5},{4,6},{9,7},{10,8},{7,9},{8... | collective-permute-start | bytes 159752 | tf_op jit(solution)/shard_map/ppermute | solution.py:216
  8.8 5.2 %collective-permute-start.3 = (bf16[208,128]{1,0:T(8,128)(2,1)S(1)}, bf16[208,128]{1,0:T(8,128)(2,1)S(1)}, u32[]{:S(2)}, u32[]{:S(2)}) collective-permute-start(bf16[208,128]{1,0:T(8,128)(2,1)S(1)} %join.1.refs_0_), channel_id=1, source_target_pairs={{6,0},{13,1},{4,2},{15,3},{2,4},{9,5},{0,6},{11,7},{14,8},{5,9},{1... | collective-permute-start | bytes 159752 | tf_op jit(solution)/shard_map/ppermute | solution.py:216
  10.3 4.1 %collective-permute-start.2 = (bf16[208,128]{1,0:T(8,128)(2,1)S(1)}, bf16[208,128]{1,0:T(8,128)(2,1)S(1)}, u32[]{:S(2)}, u32[]{:S(2)}) collective-permute-start(bf16[208,128]{1,0:T(8,128)(2,1)S(1)} %join.1.refs_0_), channel_id=1, source_target_pairs={{4,0},{11,1},{6,2},{9,3},{0,4},{15,5},{2,6},{13,7},{12,8},{3,9},{1... | collective-permute-start | bytes 159752 | tf_op jit(solution)/shard_map/ppermute | solution.py:216
  10.4 4.2 %collective-permute-start.1 = (bf16[208,128]{1,0:T(8,128)(2,1)S(1)}, bf16[208,128]{1,0:T(8,128)(2,1)S(1)}, u32[]{:S(2)}, u32[]{:S(2)}) collective-permute-start(bf16[208,128]{1,0:T(8,128)(2,1)S(1)} %join.1.refs_0_), channel_id=1, source_target_pairs={{2,0},{9,1},{0,2},{11,3},{6,4},{13,5},{4,6},{15,7},{10,8},{1,9},{8... | collective-permute-start | bytes 159752 | tf_op jit(solution)/shard_map/ppermute | solution.py:216
  14.8 4.1 %collective-permute-start.5 = (bf16[64,1024]{1,0:T(8,128)(2,1)S(1)}, bf16[64,1024]{1,0:T(8,128)(2,1)S(1)}, u32[]{:S(2)}, u32[]{:S(2)}) collective-permute-start(bf16[64,1024]{1,0:T(8,128)(2,1)S(1)} %get-tuple-element.21), channel_id=1, source_target_pairs={{0,1},{1,0},{2,3},{3,2},{4,5},{5,4},{6,7},{7,6},{8,9},{9,8},{10,11... | collective-permute-start | bytes 393224 | tf_op jit(solution)/shard_map/ppermute | solution.py:309
  18.9 0.7 %copy-start.3 = (s32[8]{0:T(128)S(1)}, s32[8]{0:T(128)}, u32[]{:S(2)}) copy-start(s32[8]{0:T(128)} %view_ref.1) | copy-start | bytes 100

commit v4 on v3

--- a/solution.py
+++ b/solution.py
@@ -29,22 +29,22 @@
     return result
 
 
-def slot_lines(view_ref, block_ref, count_ref, index, tile_rows, n_views, own_rows):
-    n_slots = view_ref.shape[0]
-    view = slot_vector([view_ref[s] for s in range(n_slots)], tile_rows, index)
-    block = slot_vector([block_ref[s] for s in range(n_slots)], tile_rows, index)
-    detector_row = block * tile_rows + index % tile_rows
-    line = (detector_row // own_rows * n_views + view) * own_rows + detector_row % own_rows
-    return jnp.where(index // tile_rows < count_ref[0], line, -1)
+def slot_lines(view_ref, block_ref, tile_rows, n_views, own_rows):
+    lines = []
+    for s in range(view_ref.shape[0]):
+        for r in range(tile_rows):
+            detector_row = block_ref[s] * tile_rows + r
+            lines.append((detector_row // own_rows * n_views + view_ref[s]) * own_rows + detector_row % own_rows)
+    return lines
 
 
 def project_kernel(
-    view_hbm, vol_hbm, pos_hbm, wid_hbm, meas_hbm, rw_hbm, tiles_hbm,
-    own_ref, send_ref, win_ref, key_ref, flat_ref,
-    view_ref, vol_ref, pos_ref, wid_ref, meas_ref, rw_ref, tiles_ref, spread_ref, sems,
+    view_hbm, block_hbm, vol_hbm, pos_hbm, wid_hbm, meas_hbm, rw_hbm, tiles_hbm,
+    own_ref, send_ref, win_ref, key_ref, flat_ref, across_ref, down_ref,
+    view_ref, block_ref, vol_ref, pos_ref, wid_ref, meas_ref, rw_ref, tiles_ref, spread_ref, sems,
 ):
-    inputs = (pos_hbm, wid_hbm, vol_hbm, tiles_hbm, view_hbm, meas_hbm, rw_hbm)
-    holders = (pos_ref, wid_ref, vol_ref, tiles_ref, view_ref, meas_ref, rw_ref)
+    inputs = (pos_hbm, wid_hbm, vol_hbm, tiles_hbm, view_hbm, block_hbm, meas_hbm, rw_hbm)
+    holders = (pos_ref, wid_ref, vol_ref, tiles_ref, view_ref, block_ref, meas_ref, rw_ref)
     copies = [pltpu.make_async_copy(a, b, sems.at[i]) for i, (a, b) in enumerate(zip(inputs, holders))]
     for copy in copies:
         copy.start()
@@ -67,6 +67,9 @@
         win_ref[v] = jnp.maximum(0.0, 1.0 - distance).astype(BF16)
     for copy in copies[2:]:
         copy.wait()
+    numbers = slot_lines(view_ref, block_ref, tile_rows, n_views, own_rows)
+    across_ref[...] = slot_vector(numbers, 1, iota(across_ref.shape, 1) & (slot_rows - 1))
+    down_ref[...] = slot_vector(numbers, 1, iota(down_ref.shape, 0))
     views = slot_vector([view_ref[s] for s in range(n_slots)], tile_rows, iota((slot_rows, cols), 0))
     key = jnp.broadcast_to(segments[0], (slot_rows, cols))
     for v in range(1, n_views):
@@ -101,12 +104,12 @@
     send_ref[...] = own_ref[...].astype(BF16)
 
 
-def join_kernel(view_ref, block_ref, count_ref, own_ref, got_ref, out_ref, *, tile_rows, n_views, own_rows):
+def join_kernel(count_ref, across_ref, own_ref, got_ref, out_ref, *, tile_rows, slot_rows):
     n_rows = own_ref.shape[0]
     out_ref[:n_rows, :] = (own_ref[...] + got_ref[...].astype(F32)).astype(BF16)
     shape = (META, LANES)
-    index = iota(shape, 1) % (view_ref.shape[0] * tile_rows)
-    line = slot_lines(view_ref, block_ref, count_ref, index, tile_rows, n_views, own_rows)
+    live = (iota((1, LANES), 1) & (slot_rows - 1)) < count_ref[0] * tile_rows
+    line = jnp.where(live, across_ref[0:1, :], -1)
     part = jnp.where(iota(shape, 0) == 0, line & 127, line >> 7)
     out_ref[n_rows:, :] = part.astype(F32).astype(BF16)
 
@@ -157,21 +160,22 @@
 
 
 def update_kernel(
-    view_ref, block_ref, count_ref, vol_ref, cw_ref, flat_ref, win_ref, key_ref, part_ref, got_ref,
+    count_ref, down_ref, vol_ref, cw_ref, flat_ref, win_ref, key_ref, part_ref, got_ref,
     upd_hbm, out_hbm,
     val_ref, near_ref, upd_ref, out_ref, sems, out_sem,
+    *, tile_rows,
 ):
     n_views, _, cols = win_ref.shape
     own_rows, shared_views, det_cols = out_ref.shape
     n_seg = det_cols // LANES
     slot_rows = key_ref.shape[0]
-    tile_rows = slot_rows // view_ref.shape[0]
     slab, trans = lax.axis_index("slab"), lax.axis_index("trans")
     lines = part_ref.shape[0] // 2
     total = part_ref[...] + got_ref[...].astype(F32)
     residual = (-total[:lines] * total[lines:]).astype(BF16)
     val_ref[...] = residual.astype(F32)
-    line = slot_lines(view_ref, block_ref, count_ref, iota((slot_rows, lines), 0), tile_rows, n_views, own_rows)
+    live = iota((slot_rows, 1), 0) < count_ref[0] * tile_rows
+    line = jnp.where(live, down_ref[:, 0:1], -1)
     chosen = jnp.where(iota((slot_rows, lines), 1) == line, 1.0, 0.0).astype(BF16)
     near = jnp.dot(chosen, residual, preferred_element_type=F32).astype(BF16)
     for a in range(n_seg):
@@ -217,9 +221,12 @@
 
 
 def direct_masks(n_group):
-    far = list(range(n_group // 2, n_group))
-    near = list(range(1, n_group // 2))
-    return [(near[j] if j < len(near) else None, mask) for j, mask in enumerate(far)]
+    half = n_group // 2
+    near = list(range(1, half + 1))
+    far = list(range(half + 1, n_group))
+    if len(far) == 3:
+        far = [far[1], far[0], far[2]]
+    return list(zip(near, far + [None]))
 
 
 def body(
@@ -230,6 +237,7 @@
     n_slots, tile_rows, depth = row_tiles.shape
     n_slab, n_trans = lax.axis_size("slab"), lax.axis_size("trans")
     assert n_trans == 2 and n_slab & (n_slab - 1) == 0 and n_slab > 1
+    assert LANES % (n_slots * tile_rows) == 0
     n_seg = det_cols // LANES
     slot_rows = n_slots * tile_rows
     own_lines = n_views * own_rows
@@ -239,8 +247,8 @@
     smem, vmem = pl.BlockSpec(memory_space=pltpu.SMEM), pl.BlockSpec(memory_space=pltpu.VMEM)
     hbm = pl.BlockSpec(memory_space=pltpu.HBM)
     params = pltpu.CompilerParams(vmem_limit_bytes=32 * 1024 * 1024)
-    near = (tile_view_index, volume, foot_pos, foot_width, measured, row_weight, row_tiles)
-    own, send, windows, key, flat = pl.pallas_call(
+    near = (tile_view_index, tile_block, volume, foot_pos, foot_width, measured, row_weight, row_tiles)
+    own, send, windows, key, flat, across, down = pl.pallas_call(
         project_kernel,
         out_shape=(
             jax.ShapeDtypeStruct((first_rows, LANES), F32),
@@ -248,11 +256,14 @@
             jax.ShapeDtypeStruct((n_views, WINDOW, cols), BF16),
             jax.ShapeDtypeStruct((slot_rows, cols), F32),
             jax.ShapeDtypeStruct((slot_rows, depth), BF16),
+            jax.ShapeDtypeStruct((8, LANES), jnp.int32),
+            jax.ShapeDtypeStruct((slot_rows, LANES), jnp.int32),
         ),
-        in_specs=[hbm] * 7,
-        out_specs=(vmem,) * 5,
+        in_specs=[hbm] * 8,
+        out_specs=(vmem,) * 7,
         scratch_shapes=[
             pltpu.SMEM(tile_view_index.shape, jnp.int32),
+            pltpu.SMEM(tile_block.shape, jnp.int32),
             pltpu.VMEM(volume.shape, F32),
             pltpu.VMEM(foot_pos.shape, F32),
             pltpu.VMEM(foot_width.shape, F32),
@@ -260,7 +271,7 @@
             pltpu.VMEM(row_weight.shape, F32),
             pltpu.VMEM(row_tiles.shape, BF16),
             pltpu.VMEM((n_views, n_seg * slot_rows, cols), BF16),
-            pltpu.SemaphoreType.DMA((7,)),
+            pltpu.SemaphoreType.DMA((8,)),
         ],
         compiler_params=params,
         name="project",
@@ -271,21 +282,21 @@
     tile_count, own = lax.optimization_barrier((tile_count, own))
 
     def join(*args):
-        join_kernel(*args, tile_rows=tile_rows, n_views=n_views, own_rows=own_rows)
+        join_kernel(*args, tile_rows=tile_rows, slot_rows=slot_rows)
 
     payload = pl.pallas_call(
         join,
         out_shape=jax.ShapeDtypeStruct((first_rows + META, LANES), BF16),
-        in_specs=[smem] * 3 + [vmem] * 2,
+        in_specs=[smem] + [vmem] * 3,
         out_specs=vmem,
         compiler_params=params,
         name="join",
-    )(tile_view_index, tile_block, tile_count, own, got)
+    )(tile_count, across, own, got)
 
     n_group = min(GROUP, n_slab)
     steps = direct_masks(n_group)
-    arrived = [exchange(payload, (1 if a is None else a, b), n_slab) for a, b in steps]
-    masks = [(0, -1)] + [(-1 if a is None else a, b) for a, b in steps]
+    arrived = [exchange(payload, (a, 1 if b is None else b), n_slab) for a, b in steps]
+    masks = [(-1, 0)] + [(a, -1 if b is None else b) for a, b in steps]
 
     def gather(*refs):
         gather_kernel(*refs, masks=masks, slot_rows=slot_rows, own_lines=own_lines, n_seg=n_seg)
@@ -308,14 +319,17 @@
         bit *= 2
     other = lax.ppermute(send, "trans", swap)
 
+    def update(*refs):
+        update_kernel(*refs, tile_rows=tile_rows)
+
     n_parts = 4
     updated, residual = pl.pallas_call(
-        update_kernel,
+        update,
         out_shape=(
             jax.ShapeDtypeStruct(volume.shape, F32),
             jax.ShapeDtypeStruct((own_rows, shared_views, det_cols), BF16),
         ),
-        in_specs=[smem] * 3 + [vmem] * 7,
+        in_specs=[smem] + [vmem] * 8,
         out_specs=(hbm, hbm),
         scratch_shapes=[
             pltpu.VMEM((lines, det_cols), F32),
@@ -327,7 +341,7 @@
         ],
         compiler_params=params,
         name="update",
-    )(tile_view_index, tile_block, tile_count, volume, col_weight, flat, windows, key, part, other)
+    )(tile_count, down, volume, col_weight, flat, windows, key, part, other)
     return updated, jnp.transpose(residual, (1, 0, 2))
 
 

time: 22.1 us -> 19.5 us (0.88)
  waiting for transfers between devices: 3.49 us -> 5.86 us
  local copies, waits for them, and re-layouts: 1.97 us -> 0.01 us
  starting transfers between devices: 10 us -> 8.08 us
  Pallas kernels: 5.11 us -> 4.09 us
    ppermute x1, starting transfers between devices: 3.12 us -> 0.07 us  [body(): other = lax.ppermute(send, 'trans', swap)]
    ppermute x4, waiting for transfers between devices: 2.27 us -> 4.29 us  [exchange(): return lax.ppermute(array, ('slab', 'trans'), pairs)]
    unnamed x10 -> x4, local copies, waits for them, and re-layouts: 1.97 us -> 0.01 us
    ppermute x4, starting transfers between devices: 6.39 us -> 7.49 us  [exchange(): return lax.ppermute(array, ('slab', 'trans'), pairs)]
    pallas_call x1, Pallas kernels: 0.57 us -> 0.02 us  [body(): pl.pallas_call(join, out_shape=jax.ShapeDtypeStruct((first_rows + META, L...]
    pallas_call x1, Pallas kernels: 2.4 us -> 1.91 us  [body(): pl.pallas_call(update, out_shape=(jax.ShapeDtypeStruct(volume.shape, F32)...]
    ppermute x1, waiting for transfers between devices: 0.99 us -> 1.33 us  [body(): other = lax.ppermute(send, 'trans', swap)]
  transfers between devices with their start and end apart: 6 -> 6, of which waited for: 5 -> 4; matrix products, arithmetic and copies ran while one was open for 0% -> 0% of each run, Pallas kernels for 0% -> 0%
where the time goes in v4:
time: 19.5 us; the launch traced here: 19.4 us
  starting transfers between devices  8.08 us (41%)
  waiting for transfers between devices  5.86 us (30%)
  Pallas kernels  4.09 us (21%)
  between operations  1.33 us (7%)
    ppermute x4, starting transfers between devices, exchange(): return lax.ppermute(array, ('slab', 'trans'), pairs)  7.49 us
    ppermute x4, waiting for transfers between devices, exchange(): return lax.ppermute(array, ('slab', 'trans'), pairs)  4.29 us
    pallas_call x1, Pallas kernels, body(): pl.pallas_call(project_kernel, out_shape=(jax.ShapeDtypeStruct((first_row...  1.98 us
    pallas_call x1, Pallas kernels, body(): pl.pallas_call(update, out_shape=(jax.ShapeDtypeStruct(volume.shape, F32)...  1.91 us
    ppermute x1, waiting for transfers between devices, body(): other = lax.ppermute(send, 'trans', swap)  1.33 us
    ppermute x1, starting transfers between devices, body(): got = lax.ppermute(send, 'trans', swap)  0.52 us
  transfers between devices with their start and end apart: 6, of which 4 were waited for; matrix products, arithmetic and copies ran while one was open for 0% of the time, Pallas kernels for 0%

profile of v4, /device:TPU:0, one launch (start us, length us, event | category | flops | bytes accessed | tf_op | source)
XLA Modules:
  0.0 19.4 jit_solution(11063157446891277540)
XLA Ops:
  0.6 0.0 copy-start
  0.6 0.0 copy-start.1
  0.7 2.0 %project.1 = (f32[192,128]{1,0:T(8,128)S(1)}, bf16[192,128]{1,0:T(8,128)(2,1)S(1)}, bf16[4,144,1024]{2,1,0:T(8,128)(2,1)S(1)}, f32[16,1024]{1,0:T(8,128)S(1)}, b...) custom-call(s32[8]{0:T(128)} %view_hbm.1, s32[8]{0:T(128)} %block_hbm.1, ...), custom_call_target="tpu_custom_call" | custom-call | tf_op jit(solution)/shard_map/project/pallas_call | solution.py:251
  2.6 0.5 %collective-permute-start = (bf16[192,128]{1,0:T(8,128)(2,1)S(1)}, bf16[192,128]{1,0:T(8,128)(2,1)S(1)}, u32[]{:S(2)}, u32[]{:S(2)}) collective-permute-start(bf16[192,128]{1,0:T(8,128)(2,1)S(1)} %get-tuple-element.23), channel_id=1, source_target_pairs={{0,1},{1,0},{2,3},{3,2},{4,5},{5,4},{6,7},{7,6},{8,9},{9,8},{10,11... | collective-permute-start | bytes 147464 | tf_op jit(solution)/shard_map/ppermute | solution.py:281
  3.8 0.2 %collective-permute-done.args_3_ = bf16[192,128]{1,0:T(8,128)(2,1)S(1)} collective-permute-done((bf16[192,128]{1,0:T(8,128)(2,1)S(1)}, bf16[192,128]{1,0:T(8,128)(2,1)S(1)}, u32[]{:S(2)}, u32[]{:S(2)}) %collective-permute-start) | collective-permute-done | bytes 49184 | tf_op jit(solution)/shard_map/ppermute | solution.py:281
  4.1 4.0 %collective-permute-start.4 = (bf16[208,128]{1,0:T(8,128)(2,1)S(1)}, bf16[208,128]{1,0:T(8,128)(2,1)S(1)}, u32[]{:S(2)}, u32[]{:S(2)}) collective-permute-start(bf16[208,128]{1,0:T(8,128)(2,1)S(1)} %join.1.refs_0_), channel_id=1, source_target_pairs={{8,0},{3,1},{10,2},{1,3},{12,4},{7,5},{14,6},{5,7},{0,8},{11,9},{2... | collective-permute-start | bytes 159752 | tf_op jit(solution)/shard_map/ppermute | solution.py:220
  8.1 2.5 %collective-permute-start.3 = (bf16[208,128]{1,0:T(8,128)(2,1)S(1)}, bf16[208,128]{1,0:T(8,128)(2,1)S(1)}, u32[]{:S(2)}, u32[]{:S(2)}) collective-permute-start(bf16[208,128]{1,0:T(8,128)(2,1)S(1)} %join.1.refs_0_), channel_id=1, source_target_pairs={{6,0},{15,1},{4,2},{13,3},{2,4},{11,5},{0,6},{9,7},{14,8},{7,9},{1... | collective-permute-start | bytes 159752 | tf_op jit(solution)/shard_map/ppermute | solution.py:220
  10.6 0.5 %collective-permute-start.2 = (bf16[208,128]{1,0:T(8,128)(2,1)S(1)}, bf16[208,128]{1,0:T(8,128)(2,1)S(1)}, u32[]{:S(2)}, u32[]{:S(2)}) collective-permute-start(bf16[208,128]{1,0:T(8,128)(2,1)S(1)} %join.1.refs_0_), channel_id=1, source_target_pairs={{4,0},{11,1},{6,2},{9,3},{0,4},{15,5},{2,6},{13,7},{12,8},{3,9},{1... | collective-permute-start | bytes 159752 | tf_op jit(solution)/shard_map/ppermute | solution.py:220
  11.0 0.5 %collective-permute-start.1 = (bf16[208,128]{1,0:T(8,128)(2,1)S(1)}, bf16[208,128]{1,0:T(8,128)(2,1)S(1)}, u32[]{:S(2)}, u32[]{:S(2)}) collective-permute-start(bf16[208,128]{1,0:T(8,128)(2,1)S(1)} %join.1.refs_0_), channel_id=1, source_target_pairs={{2,0},{13,1},{0,2},{15,3},{6,4},{9,5},{4,6},{11,7},{10,8},{5,9},{8... | collective-permute-start | bytes 159752 | tf_op jit(solution)/shard_map/ppermute | solution.py:220
  11.5 0.0 collective-permute-done.4.refs_4_
  11.6 2.0 %collective-permute-done.3.refs_3_ = bf16[208,128]{1,0:T(8,128)(2,1)S(1)} collective-permute-done((bf16[208,128]{1,0:T(8,128)(2,1)S(1)}, bf16[208,128]{1,0:T(8,128)(2,1)S(1)}, u32[]{:S(2)}, u32[]{:S(2)}) %collective-permute-start.3) | collective-permute-done | bytes 53280 | tf_op jit(solution)/shard_map/ppermute | solution.py:220
  13.5 2.3 %collective-permute-done.2.refs_2_ = bf16[208,128]{1,0:T(8,128)(2,1)S(1)} collective-permute-done((bf16[208,128]{1,0:T(8,128)(2,1)S(1)}, bf16[208,128]{1,0:T(8,128)(2,1)S(1)}, u32[]{:S(2)}, u32[]{:S(2)}) %collective-permute-start.2) | collective-permute-done | bytes 53280 | tf_op jit(solution)/shard_map/ppermute | solution.py:220
  15.8 0.0 collective-permute-done.1.refs_1_
  15.8 0.2 gather.1
  16.0 0.1 collective-permute-start.5
  16.1 1.3 %collective-permute-done.5.refs_8_ = bf16[64,1024]{1,0:T(8,128)(2,1)S(1)} collective-permute-done((bf16[64,1024]{1,0:T(8,128)(2,1)S(1)}, bf16[64,1024]{1,0:T(8,128)(2,1)S(1)}, u32[]{:S(2)}, u32[]{:S(2)}) %collective-permute-start.5) | collective-permute-done | bytes 131104 | tf_op jit(solution)/shard_map/ppermute | solution.py:320
  17.4 0.0 copy-done
  17.4 0.0 copy-done.1
  17.5 1.9 %update.1 = (f32[128,1024]{1,0:T(8,128)}, bf16[1,2,1024]{2,1,0:T(2,128)(2,1)}) custom-call(s32[1]{0:T(128)S(6)} %copy.12.args_0_.refs_0_, s32[16,128]{1,0:T(8,128)S(1)} %get-tuple-element.17.refs_1_, f32[128,1024]{1,0:T(8,128)S(1)} %copy-done, f32[128,1024]{1,0:T(8,128)S(1)} %copy-done.1, bf16[16,128]{1,0:T(8,128)(2,1)S(1)} %get-tuple-element.18.refs_4_, ...), custom_call_target="tpu_custom_call" | custom-call | tf_op jit(solution)/shard_map/update/pallas_call | solution.py:326
  (1 shorter events, 0.0 us)
Async XLA Ops:
  0.6 16.8 %copy-start = (f32[128,1024]{1,0:T(8,128)S(1)}, f32[128,1024]{1,0:T(8,128)}, u32[]{:S(2)}) copy-start(f32[128,1024]{1,0:T(8,128)} %refs_2_.1) | copy-start | bytes 1572868
  0.6 16.8 %copy-start.1 = (f32[128,1024]{1,0:T(8,128)S(1)}, f32[128,1024]{1,0:T(8,128)}, u32[]{:S(2)}) copy-start(f32[128,1024]{1,0:T(8,128)} %refs_3_.1) | copy-start | bytes 1572868
  2.6 1.4 %collective-permute-start = (bf16[192,128]{1,0:T(8,128)(2,1)S(1)}, bf16[192,128]{1,0:T(8,128)(2,1)S(1)}, u32[]{:S(2)}, u32[]{:S(2)}) collective-permute-start(bf16[192,128]{1,0:T(8,128)(2,1)S(1)} %get-tuple-element.23), channel_id=1, source_target_pairs={{0,1},{1,0},{2,3},{3,2},{4,5},{5,4},{6,7},{7,6},{8,9},{9,8},{10,11... | collective-permute-start | bytes 147464 | tf_op jit(solution)/shard_map/ppermute | solution.py:281
  4.1 7.5 %collective-permute-start.4 = (bf16[208,128]{1,0:T(8,128)(2,1)S(1)}, bf16[208,128]{1,0:T(8,128)(2,1)S(1)}, u32[]{:S(2)}, u32[]{:S(2)}) collective-permute-start(bf16[208,128]{1,0:T(8,128)(2,1)S(1)} %join.1.refs_0_), channel_id=1, source_target_pairs={{8,0},{3,1},{10,2},{1,3},{12,4},{7,5},{14,6},{5,7},{0,8},{11,9},{2... | collective-permute-start | bytes 159752 | tf_op jit(solution)/shard_map/ppermute | solution.py:220
  8.1 5.5 %collective-permute-start.3 = (bf16[208,128]{1,0:T(8,128)(2,1)S(1)}, bf16[208,128]{1,0:T(8,128)(2,1)S(1)}, u32[]{:S(2)}, u32[]{:S(2)}) collective-permute-start(bf16[208,128]{1,0:T(8,128)(2,1)S(1)} %join.1.refs_0_), channel_id=1, source_target_pairs={{6,0},{15,1},{4,2},{13,3},{2,4},{11,5},{0,6},{9,7},{14,8},{7,9},{1... | collective-permute-start | bytes 159752 | tf_op jit(solution)/shard_map/ppermute | solution.py:220
  10.6 5.3 %collective-permute-start.2 = (bf16[208,128]{1,0:T(8,128)(2,1)S(1)}, bf16[208,128]{1,0:T(8,128)(2,1)S(1)}, u32[]{:S(2)}, u32[]{:S(2)}) collective-permute-start(bf16[208,128]{1,0:T(8,128)(2,1)S(1)} %join.1.refs_0_), channel_id=1, source_target_pairs={{4,0},{11,1},{6,2},{9,3},{0,4},{15,5},{2,6},{13,7},{12,8},{3,9},{1... | collective-permute-start | bytes 159752 | tf_op jit(solution)/shard_map/ppermute | solution.py:220
  11.0 4.8 %collective-permute-start.1 = (bf16[208,128]{1,0:T(8,128)(2,1)S(1)}, bf16[208,128]{1,0:T(8,128)(2,1)S(1)}, u32[]{:S(2)}, u32[]{:S(2)}) collective-permute-start(bf16[208,128]{1,0:T(8,128)(2,1)S(1)} %join.1.refs_0_), channel_id=1, source_target_pairs={{2,0},{13,1},{0,2},{15,3},{6,4},{9,5},{4,6},{11,7},{10,8},{5,9},{8... | collective-permute-start | bytes 159752 | tf_op jit(solution)/shard_map/ppermute | solution.py:220
  16.0 1.4 %collective-permute-start.5 = (bf16[64,1024]{1,0:T(8,128)(2,1)S(1)}, bf16[64,1024]{1,0:T(8,128)(2,1)S(1)}, u32[]{:S(2)}, u32[]{:S(2)}) collective-permute-start(bf16[64,1024]{1,0:T(8,128)(2,1)S(1)} %get-tuple-element.25), channel_id=1, source_target_pairs={{0,1},{1,0},{2,3},{3,2},{4,5},{5,4},{6,7},{7,6},{8,9},{9,8},{10,11... | collective-permute-start | bytes 393224 | tf_op jit(solution)/shard_map/ppermute | solution.py:320

commit v5 on v4

--- a/solution.py
+++ b/solution.py
@@ -43,8 +43,8 @@
     own_ref, send_ref, win_ref, key_ref, flat_ref, across_ref, down_ref,
     view_ref, block_ref, vol_ref, pos_ref, wid_ref, meas_ref, rw_ref, tiles_ref, spread_ref, sems,
 ):
-    inputs = (pos_hbm, wid_hbm, vol_hbm, tiles_hbm, view_hbm, block_hbm, meas_hbm, rw_hbm)
-    holders = (pos_ref, wid_ref, vol_ref, tiles_ref, view_ref, block_ref, meas_ref, rw_ref)
+    inputs = (pos_hbm, wid_hbm, vol_hbm, view_hbm, block_hbm, tiles_hbm, meas_hbm, rw_hbm)
+    holders = (pos_ref, wid_ref, vol_ref, view_ref, block_ref, tiles_ref, meas_ref, rw_ref)
     copies = [pltpu.make_async_copy(a, b, sems.at[i]) for i, (a, b) in enumerate(zip(inputs, holders))]
     for copy in copies:
         copy.start()
@@ -60,36 +60,40 @@
     copies[1].wait()
     segments = []
     for v in range(n_views):
+        segments.append(segment_of(pos_ref[v : v + 1, :], wid_ref[v : v + 1, :], n_seg))
+
+    def window(v):
         pos, wid = pos_ref[v : v + 1, :], wid_ref[v : v + 1, :]
-        seg = segment_of(pos, wid, n_seg)
-        segments.append(seg + float(v * n_seg))
-        distance = jnp.abs(offsets + (seg * LANES + 0.5 - pos)) * (1.0 / wid)
+        distance = jnp.abs(offsets + (segments[v] * LANES + 0.5 - pos)) * (1.0 / wid)
         win_ref[v] = jnp.maximum(0.0, 1.0 - distance).astype(BF16)
+
+    first_views = n_views // 2
+    for v in range(first_views):
+        window(v)
     for copy in copies[2:]:
         copy.wait()
-    numbers = slot_lines(view_ref, block_ref, tile_rows, n_views, own_rows)
-    across_ref[...] = slot_vector(numbers, 1, iota(across_ref.shape, 1) & (slot_rows - 1))
-    down_ref[...] = slot_vector(numbers, 1, iota(down_ref.shape, 0))
-    views = slot_vector([view_ref[s] for s in range(n_slots)], tile_rows, iota((slot_rows, cols), 0))
-    key = jnp.broadcast_to(segments[0], (slot_rows, cols))
-    for v in range(1, n_views):
-        key = jnp.where(views == v, segments[v], key)
-    key_ref[...] = key
     tiles = tiles_ref[...].astype(F32)
     flat = jnp.concatenate([tiles[s, r : r + 1, :] for s in range(n_slots) for r in range(tile_rows)], axis=0)
     flat = flat.astype(BF16)
     flat_ref[...] = flat
     rows = jnp.dot(flat, vol_ref[...].astype(BF16), preferred_element_type=F32)
+    views = slot_vector([view_ref[s] for s in range(n_slots)], tile_rows, iota((slot_rows, cols), 0))
+    key = jnp.broadcast_to(segments[0], (slot_rows, cols))
+    for v in range(1, n_views):
+        key = jnp.where(views == v, segments[v] + float(v * n_seg), key)
+    key_ref[...] = key
     sums = jnp.zeros((n_seg * slot_rows, WINDOW), F32)
     for v in range(n_views):
         for a in range(n_seg):
             spread_ref[v, a * slot_rows : (a + 1) * slot_rows, :] = jnp.where(key == v * n_seg + a, rows, 0.0).astype(BF16)
+        if v >= first_views:
+            window(v)
         sums = sums + lax.dot_general(
             spread_ref[v], win_ref[v], (((1,), (1,)), ((), ())), preferred_element_type=F32
         )
-    edge = WINDOW - LANES
-    own_ref[: n_seg * slot_rows, :] = sums[:, :LANES]
-    own_ref[slot_rows : n_seg * slot_rows, :edge] += sums[: (n_seg - 1) * slot_rows, LANES:]
+    numbers = slot_lines(view_ref, block_ref, tile_rows, n_views, own_rows)
+    across_ref[...] = slot_vector(numbers, 1, iota(across_ref.shape, 1) & (slot_rows - 1))
+    down_ref[...] = slot_vector(numbers, 1, iota(down_ref.shape, 0))
     lines = own_ref.shape[0] // n_seg - slot_rows
     place = iota((lines, det_cols), 0)
     block = jnp.zeros((lines, det_cols), F32)
@@ -101,23 +105,31 @@
     for a in range(n_seg):
         at = n_seg * slot_rows + a * lines
         own_ref[at : at + lines, :] = block[:, a * LANES : (a + 1) * LANES]
+    edge = WINDOW - LANES
+    own_ref[: n_seg * slot_rows, :] = sums[:, :LANES]
+    own_ref[slot_rows : n_seg * slot_rows, :edge] += sums[: (n_seg - 1) * slot_rows, LANES:]
     send_ref[...] = own_ref[...].astype(BF16)
 
 
-def join_kernel(count_ref, across_ref, own_ref, got_ref, out_ref, *, tile_rows, slot_rows):
+def join_kernel(count_ref, across_ref, down_ref, own_ref, got_ref, out_ref, wanted_ref, *, tile_rows, own_lines):
     n_rows = own_ref.shape[0]
+    slot_rows = down_ref.shape[0]
     out_ref[:n_rows, :] = (own_ref[...] + got_ref[...].astype(F32)).astype(BF16)
     shape = (META, LANES)
-    live = (iota((1, LANES), 1) & (slot_rows - 1)) < count_ref[0] * tile_rows
+    live_rows = count_ref[0] * tile_rows
+    live = (iota((1, LANES), 1) & (slot_rows - 1)) < live_rows
     line = jnp.where(live, across_ref[0:1, :], -1)
     part = jnp.where(iota(shape, 0) == 0, line & 127, line >> 7)
     out_ref[n_rows:, :] = part.astype(F32).astype(BF16)
-
-
-def gather_kernel(*refs, masks, slot_rows, own_lines, n_seg):
+    wanted_ref[:slot_rows, :] = jnp.where(iota((slot_rows, LANES), 0) < live_rows, down_ref[...], -2)
+    shape = (wanted_ref.shape[0] - slot_rows, LANES)
+    index = iota(shape, 0)
+    wanted_ref[slot_rows:, :] = jnp.where(index < own_lines, lax.axis_index("slab") * own_lines + index, -2)
+
+
+def gather_kernel(ids_ref, *refs, masks, slot_rows, own_lines, n_seg):
     payloads, (part_ref, send_ref, all_ref) = refs[:-3], refs[-3:]
     slab, trans = lax.axis_index("slab"), lax.axis_index("trans")
-    lines = part_ref.shape[0] // 2
     depth = all_ref.shape[0]
     n_sources = len(payloads)
     block_lines = (payloads[0].shape[0] - META) // n_seg - slot_rows
@@ -149,7 +161,7 @@
             all_ref[j * slot_rows : (j + 1) * slot_rows, lanes] = values[a * slot_rows : (a + 1) * slot_rows]
             start = n_seg * slot_rows + a * block_lines
             all_ref[at : at + block_lines, lanes] = values[start : start + block_lines]
-    ids = iota((lines, depth), 0)
+    ids = jnp.concatenate([ids_ref[...]] * (depth // LANES), axis=1)
     sign = jnp.where(lane >= first_block, -1.0, 1.0)
     chosen = jnp.concatenate(
         [jnp.where(ids == sum_line, sign, 0.0), jnp.where(ids == weight_line, 1.0, 0.0)], axis=0
@@ -159,25 +171,33 @@
     send_ref[...] = part.astype(BF16)
 
 
+def pick_kernel(ids_ref, part_ref, out_ref, send_ref):
+    lines = part_ref.shape[0] // 2
+    ids = jnp.concatenate([ids_ref[...]] * (-(-lines // LANES)), axis=1)[:, :lines]
+    chosen = (iota(ids.shape, 1) == ids).astype(F32)
+    for half in range(2):
+        part = part_ref[half * lines : (half + 1) * lines, :]
+        rows = slice(half * ids.shape[0], (half + 1) * ids.shape[0])
+        picked = jnp.dot(chosen, part, preferred_element_type=F32, precision=lax.Precision.HIGHEST)
+        out_ref[rows, :] = picked
+        send_ref[rows, :] = picked.astype(BF16)
+
+
 def update_kernel(
-    count_ref, down_ref, vol_ref, cw_ref, flat_ref, win_ref, key_ref, part_ref, got_ref,
+    vol_ref, cw_ref, flat_ref, win_ref, key_ref, part_ref, got_ref,
     upd_hbm, out_hbm,
     val_ref, near_ref, upd_ref, out_ref, sems, out_sem,
-    *, tile_rows,
 ):
     n_views, _, cols = win_ref.shape
     own_rows, shared_views, det_cols = out_ref.shape
     n_seg = det_cols // LANES
     slot_rows = key_ref.shape[0]
-    slab, trans = lax.axis_index("slab"), lax.axis_index("trans")
+    trans = lax.axis_index("trans")
     lines = part_ref.shape[0] // 2
     total = part_ref[...] + got_ref[...].astype(F32)
-    residual = (-total[:lines] * total[lines:]).astype(BF16)
-    val_ref[...] = residual.astype(F32)
-    live = iota((slot_rows, 1), 0) < count_ref[0] * tile_rows
-    line = jnp.where(live, down_ref[:, 0:1], -1)
-    chosen = jnp.where(iota((slot_rows, lines), 1) == line, 1.0, 0.0).astype(BF16)
-    near = jnp.dot(chosen, residual, preferred_element_type=F32).astype(BF16)
+    residual = -total[:lines] * total[lines:]
+    near = residual[:slot_rows].astype(BF16)
+    val_ref[...] = residual[slot_rows:]
     for a in range(n_seg):
         at = slice(a * slot_rows, (a + 1) * slot_rows)
         near_ref[at, :LANES] = near[:, a * LANES : (a + 1) * LANES]
@@ -185,29 +205,26 @@
             near_ref[at, LANES:] = near[:, (a + 1) * LANES : (a + 2) * LANES]
         else:
             near_ref[at, LANES:] = jnp.zeros((slot_rows, LANES), BF16)
-    n_parts = sems.shape[0]
-    width = cols // n_parts
-    copies = []
-    for p in range(n_parts):
-        at = slice(p * width, (p + 1) * width)
-        key = key_ref[:, at]
-        back = jnp.zeros((slot_rows, width), F32)
-        for v in range(n_views):
-            part = jnp.dot(near_ref[:, :WINDOW], win_ref[v, :, at], preferred_element_type=F32)
-            for a in range(n_seg):
-                back = jnp.where(key == v * n_seg + a, part[a * slot_rows : (a + 1) * slot_rows], back)
-        gradient = lax.dot_general(
-            flat_ref[...], back.astype(BF16), (((0,), (0,)), ((), ())), preferred_element_type=F32
-        )
-        upd_ref[:, at] = vol_ref[:, at] + 0.9 * cw_ref[:, at] * gradient
-        copies.append(pltpu.make_async_copy(upd_ref.at[:, at], upd_hbm.at[:, at], sems.at[p]))
-        copies[-1].start()
     for i in range(shared_views):
         for j in range(own_rows):
-            line = (slab * n_views + trans * shared_views + i) * own_rows + j
+            line = (trans * shared_views + i) * own_rows + j
             out_ref[j, i : i + 1, :] = val_ref[pl.ds(line, 1), :].astype(BF16)
-    copies.append(pltpu.make_async_copy(out_ref, out_hbm, out_sem))
-    copies[-1].start()
+    copies = [pltpu.make_async_copy(out_ref, out_hbm, out_sem)]
+    copies[0].start()
+    key = key_ref[...]
+    back = jnp.zeros((slot_rows, cols), F32)
+    for v in range(n_views):
+        part = jnp.dot(near_ref[:, :WINDOW], win_ref[v], preferred_element_type=F32)
+        for a in range(n_seg):
+            back = jnp.where(key == v * n_seg + a, part[a * slot_rows : (a + 1) * slot_rows], back)
+    gradient = lax.dot_general(flat_ref[...], back.astype(BF16), (((0,), (0,)), ((), ())), preferred_element_type=F32)
+    n_parts = sems.shape[0]
+    depth = gradient.shape[0] // n_parts
+    for p in range(n_parts):
+        at = slice(p * depth, (p + 1) * depth)
+        upd_ref[at, :] = vol_ref[at, :] + cw_ref[at, :] * gradient[at]
+        copies.append(pltpu.make_async_copy(upd_ref.at[at, :], upd_hbm.at[at, :], sems.at[p]))
+        copies[-1].start()
     for copy in copies:
         copy.wait()
 
@@ -220,13 +237,14 @@
     return lax.ppermute(array, ("slab", "trans"), pairs)
 
 
-def direct_masks(n_group):
+def direct_steps(n_group):
     half = n_group // 2
-    near = list(range(1, half + 1))
-    far = list(range(half + 1, n_group))
-    if len(far) == 3:
-        far = [far[1], far[0], far[2]]
-    return list(zip(near, far + [None]))
+    near = [(mask, True) for mask in range(half, 0, -1)]
+    far = [(1, False)] + [(mask, True) for mask in range(n_group - 1, half, -1)]
+    if n_group == 8:
+        near = [(mask, True) for mask in (4, 1, 2, 3)]
+        far = [(1, False), (7, True), (5, True), (6, True)]
+    return list(zip(near, far))
 
 
 def body(
@@ -281,58 +299,71 @@
     got = lax.ppermute(send, "trans", swap)
     tile_count, own = lax.optimization_barrier((tile_count, own))
 
-    def join(*args):
-        join_kernel(*args, tile_rows=tile_rows, slot_rows=slot_rows)
-
-    payload = pl.pallas_call(
+    def join(*refs):
+        join_kernel(*refs, tile_rows=tile_rows, own_lines=own_lines)
+
+    n_wanted = slot_rows + -(-own_lines // 8) * 8
+    payload, wanted = pl.pallas_call(
         join,
-        out_shape=jax.ShapeDtypeStruct((first_rows + META, LANES), BF16),
-        in_specs=[smem] + [vmem] * 3,
-        out_specs=vmem,
+        out_shape=(
+            jax.ShapeDtypeStruct((first_rows + META, LANES), BF16),
+            jax.ShapeDtypeStruct((n_wanted, LANES), jnp.int32),
+        ),
+        in_specs=[smem] + [vmem] * 4,
+        out_specs=(vmem,) * 2,
         compiler_params=params,
         name="join",
-    )(tile_count, across, own, got)
+    )(tile_count, across, down, own, got)
 
     n_group = min(GROUP, n_slab)
-    steps = direct_masks(n_group)
-    arrived = [exchange(payload, (a, 1 if b is None else b), n_slab) for a, b in steps]
-    masks = [(-1, 0)] + [(a, -1 if b is None else b) for a, b in steps]
+    steps = direct_steps(n_group)
+    arrived = [exchange(payload, [mask for mask, _ in step], n_slab) for step in steps]
+    masks = [[mask if used else -1 for mask, used in step] for step in steps]
 
     def gather(*refs):
-        gather_kernel(*refs, masks=masks, slot_rows=slot_rows, own_lines=own_lines, n_seg=n_seg)
-
-    part_shape = (2 * lines, det_cols)
-    all_depth = -(-len(masks) * (slot_rows + block_lines) // LANES) * LANES
+        gather_kernel(*refs, masks=[(-1, 0)] + masks, slot_rows=slot_rows, own_lines=own_lines, n_seg=n_seg)
+
+    whole = n_group == n_slab
+    ids = wanted if whole else jnp.broadcast_to(jnp.arange(lines, dtype=jnp.int32)[:, None], (lines, LANES))
+    part_shape = (2 * ids.shape[0], det_cols)
+    all_depth = -(-(1 + len(steps)) * (slot_rows + block_lines) // LANES) * LANES
     part, send = pl.pallas_call(
         gather,
         out_shape=(jax.ShapeDtypeStruct(part_shape, F32), jax.ShapeDtypeStruct(part_shape, BF16)),
-        in_specs=[vmem] * len(masks),
+        in_specs=[vmem] * (2 + len(steps)),
         out_specs=(vmem,) * 2,
         scratch_shapes=[pltpu.VMEM((all_depth, det_cols), F32)],
         compiler_params=params,
         name="gather",
-    )(payload, *arrived)
-    bit = n_group
-    while bit < n_slab:
-        part = part + exchange(send, (bit, bit), n_slab).astype(F32)
-        send = part.astype(BF16)
-        bit *= 2
+    )(ids, payload, *arrived)
+    if not whole:
+        bit = n_group
+        while bit < n_slab:
+            part = part + exchange(part.astype(BF16), (bit, bit), n_slab).astype(F32)
+            bit *= 2
+        part_shape = (2 * n_wanted, det_cols)
+        part, send = pl.pallas_call(
+            pick_kernel,
+            out_shape=(jax.ShapeDtypeStruct(part_shape, F32), jax.ShapeDtypeStruct(part_shape, BF16)),
+            in_specs=[vmem] * 2,
+            out_specs=(vmem,) * 2,
+            compiler_params=params,
+            name="pick",
+        )(wanted, part)
+    scaled, send = lax.optimization_barrier((0.9 * col_weight, send))
     other = lax.ppermute(send, "trans", swap)
 
-    def update(*refs):
-        update_kernel(*refs, tile_rows=tile_rows)
-
-    n_parts = 4
+    n_parts = 2
     updated, residual = pl.pallas_call(
-        update,
+        update_kernel,
         out_shape=(
             jax.ShapeDtypeStruct(volume.shape, F32),
             jax.ShapeDtypeStruct((own_rows, shared_views, det_cols), BF16),
         ),
-        in_specs=[smem] + [vmem] * 8,
+        in_specs=[vmem] * 7,
         out_specs=(hbm, hbm),
         scratch_shapes=[
-            pltpu.VMEM((lines, det_cols), F32),
+            pltpu.VMEM((n_wanted - slot_rows, det_cols), F32),
             pltpu.VMEM((n_seg * slot_rows, 2 * LANES), BF16),
             pltpu.VMEM(volume.shape, F32),
             pltpu.VMEM((own_rows, shared_views, det_cols), BF16),
@@ -341,7 +372,7 @@
         ],
         compiler_params=params,
         name="update",
-    )(tile_count, down, volume, col_weight, flat, windows, key, part, other)
+    )(volume, scaled, flat, windows, key, part, other)
     return updated, jnp.transpose(residual, (1, 0, 2))
 
 

time: 19.5 us -> 17.6 us (0.903)
  waiting for transfers between devices: 5.86 us -> 2.52 us
  other arithmetic: 0 us -> 1.09 us
  starting transfers between devices: 8.08 us -> 8.94 us
  Pallas kernels: 4.09 us -> 3.46 us
    ppermute x4, waiting for transfers between devices: 4.29 us -> 1.34 us  [exchange(): return lax.ppermute(array, ('slab', 'trans'), pairs)]
    mul x0 -> x1, other arithmetic: none -> 1.09 us  [body(): scaled, send = lax.optimization_barrier((0.9 * col_weight, send))]
    ppermute x1, starting transfers between devices: 0.07 us -> 0.93 us  [body(): other = lax.ppermute(send, 'trans', swap)]
    pallas_call x2, Pallas kernels: 1.93 us -> 1.42 us  [the longest x1 1.4 us: body(): pl.pallas_call(update_kernel, out_shape=(jax.ShapeDtypeStruct(volume.shap...]
    ppermute x1, waiting for transfers between devices: 1.33 us -> 0.94 us  [body(): other = lax.ppermute(send, 'trans', swap)]
  transfers between devices with their start and end apart: 6 -> 6, of which waited for: 4 -> 3; matrix products, arithmetic and copies ran while one was open for 0% -> 6% of each run, Pallas kernels for 0% -> 0%
where the time goes in v5:
time: 17.6 us; the launch traced here: 17.4 us
  starting transfers between devices  8.94 us (51%)
  Pallas kernels  3.46 us (20%)
  waiting for transfers between devices  2.52 us (14%)
  between operations  1.35 us (8%)
  other arithmetic  1.09 us (6%)
    ppermute x4, starting transfers between devices, exchange(): return lax.ppermute(array, ('slab', 'trans'), pairs)  7.49 us
    pallas_call x1, Pallas kernels, body(): pl.pallas_call(project_kernel, out_shape=(jax.ShapeDtypeStruct((first_row...  1.86 us
    pallas_call x1, Pallas kernels, body(): pl.pallas_call(update_kernel, out_shape=(jax.ShapeDtypeStruct(volume.shap...  1.4 us
    ppermute x4, waiting for transfers between devices, exchange(): return lax.ppermute(array, ('slab', 'trans'), pairs)  1.34 us
    mul x1, other arithmetic, body(): scaled, send = lax.optimization_barrier((0.9 * col_weight, send))  1.09 us
    ppermute x1, waiting for transfers between devices, body(): other = lax.ppermute(send, 'trans', swap)  0.94 us
    ppermute x1, starting transfers between devices, body(): other = lax.ppermute(send, 'trans', swap)  0.93 us
    ppermute x1, starting transfers between devices, body(): got = lax.ppermute(send, 'trans', swap)  0.52 us
  transfers between devices with their start and end apart: 6, of which 3 were waited for; matrix products, arithmetic and copies ran while one was open for 6% of the time, Pallas kernels for 0%

profile of v5, /device:TPU:0, one launch (start us, length us, event | category | flops | bytes accessed | tf_op | source)
XLA Modules:
  0.0 17.4 jit_solution(13042471352853260248)
XLA Ops:
  0.6 0.0 copy-start
  0.6 1.9 %project.1 = (f32[192,128]{1,0:T(8,128)S(1)}, bf16[192,128]{1,0:T(8,128)(2,1)S(1)}, bf16[4,144,1024]{2,1,0:T(8,128)(2,1)S(1)}, f32[16,1024]{1,0:T(8,128)S(1)}, b...) custom-call(s32[8]{0:T(128)} %view_hbm.1, s32[8]{0:T(128)} %block_hbm.1, ...), custom_call_target="tpu_custom_call" | custom-call | tf_op jit(solution)/shard_map/project/pallas_call | solution.py:269
  2.5 0.5 %collective-permute-start = (bf16[192,128]{1,0:T(8,128)(2,1)S(1)}, bf16[192,128]{1,0:T(8,128)(2,1)S(1)}, u32[]{:S(2)}, u32[]{:S(2)}) collective-permute-start(bf16[192,128]{1,0:T(8,128)(2,1)S(1)} %get-tuple-element.24), channel_id=1, source_target_pairs={{0,1},{1,0},{2,3},{3,2},{4,5},{5,4},{6,7},{7,6},{8,9},{9,8},{10,11... | collective-permute-start | bytes 147464 | tf_op jit(solution)/shard_map/ppermute | solution.py:299
  3.7 0.2 %collective-permute-done.refs_4_ = bf16[192,128]{1,0:T(8,128)(2,1)S(1)} collective-permute-done((bf16[192,128]{1,0:T(8,128)(2,1)S(1)}, bf16[192,128]{1,0:T(8,128)(2,1)S(1)}, u32[]{:S(2)}, u32[]{:S(2)}) %collective-permute-start) | collective-permute-done | bytes 49184 | tf_op jit(solution)/shard_map/ppermute | solution.py:299
  3.9 3.9 %collective-permute-start.4 = (bf16[208,128]{1,0:T(8,128)(2,1)S(1)}, bf16[208,128]{1,0:T(8,128)(2,1)S(1)}, u32[]{:S(2)}, u32[]{:S(2)}) collective-permute-start(bf16[208,128]{1,0:T(8,128)(2,1)S(1)} %get-tuple-element.26.refs_1_), channel_id=1, source_target_pairs={{6,0},{13,1},{4,2},{15,3},{2,4},{9,5},{0,6},{11,7},{14,8},{5,9},{1... | collective-permute-start | bytes 159752 | tf_op jit(solution)/shard_map/ppermute | solution.py:237
  7.8 0.4 %collective-permute-start.3 = (bf16[208,128]{1,0:T(8,128)(2,1)S(1)}, bf16[208,128]{1,0:T(8,128)(2,1)S(1)}, u32[]{:S(2)}, u32[]{:S(2)}) collective-permute-start(bf16[208,128]{1,0:T(8,128)(2,1)S(1)} %get-tuple-element.26.refs_1_), channel_id=1, source_target_pairs={{4,0},{11,1},{6,2},{9,3},{0,4},{15,5},{2,6},{13,7},{12,8},{3,9},{1... | collective-permute-start | bytes 159752 | tf_op jit(solution)/shard_map/ppermute | solution.py:237
  8.3 0.2 %collective-permute-start.2 = (bf16[208,128]{1,0:T(8,128)(2,1)S(1)}, bf16[208,128]{1,0:T(8,128)(2,1)S(1)}, u32[]{:S(2)}, u32[]{:S(2)}) collective-permute-start(bf16[208,128]{1,0:T(8,128)(2,1)S(1)} %get-tuple-element.26.refs_1_), channel_id=1, source_target_pairs={{2,0},{15,1},{0,2},{13,3},{6,4},{11,5},{4,6},{9,7},{10,8},{7,9},{8... | collective-permute-start | bytes 159752 | tf_op jit(solution)/shard_map/ppermute | solution.py:237
  8.5 2.9 %collective-permute-start.1 = (bf16[208,128]{1,0:T(8,128)(2,1)S(1)}, bf16[208,128]{1,0:T(8,128)(2,1)S(1)}, u32[]{:S(2)}, u32[]{:S(2)}) collective-permute-start(bf16[208,128]{1,0:T(8,128)(2,1)S(1)} %get-tuple-element.26.refs_1_), channel_id=1, source_target_pairs={{8,0},{3,1},{10,2},{1,3},{12,4},{7,5},{14,6},{5,7},{0,8},{11,9},{2... | collective-permute-start | bytes 159752 | tf_op jit(solution)/shard_map/ppermute | solution.py:237
  11.4 1.1 %broadcast_multiply_fusion.cw_ref = f32[128,1024]{1,0:T(8,128)S(1)} fusion(f32[128,1024]{1,0:T(8,128)} %param.11), kind=kLoop, calls=%fused_computation | loop fusion | flops 131072 | bytes 1048576 | tf_op jit(solution)/shard_map/mul | solution.py:353
  12.5 0.0 collective-permute-done.4.refs_5_
  12.5 0.0 collective-permute-done.3.refs_4_
  12.5 0.0 collective-permute-done.2.refs_3_
  12.6 1.3 %collective-permute-done.1.refs_2_ = bf16[208,128]{1,0:T(8,128)(2,1)S(1)} collective-permute-done((bf16[208,128]{1,0:T(8,128)(2,1)S(1)}, bf16[208,128]{1,0:T(8,128)(2,1)S(1)}, u32[]{:S(2)}, u32[]{:S(2)}) %collective-permute-start.1) | collective-permute-done | bytes 53280 | tf_op jit(solution)/shard_map/ppermute | solution.py:237
  13.9 0.2 %gather.1 = (f32[48,1024]{1,0:T(8,128)S(1)}, bf16[48,1024]{1,0:T(8,128)(2,1)S(1)}) custom-call(s32[24,128]{1,0:T(8,128)S(1)} %get-tuple-element.25.refs_0_, bf16[208,128]{1,0:T(8,128)(2,1)S(1)} %get-tuple-element.26.refs_1_, bf16[208,128]{1,0:T(8,128)(2,1)S(1)} %collective-permute-done.1.refs_2_, bf16[208,128]{1,0:T(8,128)(2,1)S(1)} %collective-permute-done.2.refs_3_, ...), custom_call_target="tpu_custom_call" | custom-call | tf_op jit(solution)/shard_map/gather/pallas_call | solution.py:330
  14.1 0.9 %collective-permute-start.5 = (bf16[48,1024]{1,0:T(8,128)(2,1)S(1)}, bf16[48,1024]{1,0:T(8,128)(2,1)S(1)}, u32[]{:S(2)}, u32[]{:S(2)}) collective-permute-start(bf16[48,1024]{1,0:T(8,128)(2,1)S(1)} %get-tuple-element.33), channel_id=1, source_target_pairs={{0,1},{1,0},{2,3},{3,2},{4,5},{5,4},{6,7},{7,6},{8,9},{9,8},{10,11... | collective-permute-start | bytes 294920 | tf_op jit(solution)/shard_map/ppermute | solution.py:354
  15.0 0.9 %collective-permute-done.5.got_ref = bf16[48,1024]{1,0:T(8,128)(2,1)S(1)} collective-permute-done((bf16[48,1024]{1,0:T(8,128)(2,1)S(1)}, bf16[48,1024]{1,0:T(8,128)(2,1)S(1)}, u32[]{:S(2)}, u32[]{:S(2)}) %collective-permute-start.5) | collective-permute-done | bytes 98336 | tf_op jit(solution)/shard_map/ppermute | solution.py:354
  16.0 0.0 copy-done
  16.0 1.4 %update.1 = (f32[128,1024]{1,0:T(8,128)}, bf16[1,2,1024]{2,1,0:T(2,128)(2,1)}) custom-call(f32[128,1024]{1,0:T(8,128)S(1)} %copy-done, f32[128,1024]{1,0:T(8,128)S(1)} %broadcast_multiply_fusion.cw_ref, bf16[16,128]{1,0:T(8,128)(2,1)S(1)} %get-tuple-element.29.flat_ref, bf16[4,144,1024]{2,1,0:T(8,128)(2,1)S(1)} %get-tuple-element.30.win_ref, ...), custom_call_target="tpu_custom_call" | custom-call | tf_op jit(solution)/shard_map/update/pallas_call | solution.py:357
  (1 shorter events, 0.0 us)
Async XLA Ops:
  0.6 15.3 %copy-start = (f32[128,1024]{1,0:T(8,128)S(1)}, f32[128,1024]{1,0:T(8,128)}, u32[]{:S(2)}) copy-start(f32[128,1024]{1,0:T(8,128)} %vol_ref.1) | copy-start | bytes 1572868
  2.5 1.4 %collective-permute-start = (bf16[192,128]{1,0:T(8,128)(2,1)S(1)}, bf16[192,128]{1,0:T(8,128)(2,1)S(1)}, u32[]{:S(2)}, u32[]{:S(2)}) collective-permute-start(bf16[192,128]{1,0:T(8,128)(2,1)S(1)} %get-tuple-element.24), channel_id=1, source_target_pairs={{0,1},{1,0},{2,3},{3,2},{4,5},{5,4},{6,7},{7,6},{8,9},{9,8},{10,11... | collective-permute-start | bytes 147464 | tf_op jit(solution)/shard_map/ppermute | solution.py:299
  3.9 8.6 %collective-permute-start.4 = (bf16[208,128]{1,0:T(8,128)(2,1)S(1)}, bf16[208,128]{1,0:T(8,128)(2,1)S(1)}, u32[]{:S(2)}, u32[]{:S(2)}) collective-permute-start(bf16[208,128]{1,0:T(8,128)(2,1)S(1)} %get-tuple-element.26.refs_1_), channel_id=1, source_target_pairs={{6,0},{13,1},{4,2},{15,3},{2,4},{9,5},{0,6},{11,7},{14,8},{5,9},{1... | collective-permute-start | bytes 159752 | tf_op jit(solution)/shard_map/ppermute | solution.py:237
  7.8 4.7 %collective-permute-start.3 = (bf16[208,128]{1,0:T(8,128)(2,1)S(1)}, bf16[208,128]{1,0:T(8,128)(2,1)S(1)}, u32[]{:S(2)}, u32[]{:S(2)}) collective-permute-start(bf16[208,128]{1,0:T(8,128)(2,1)S(1)} %get-tuple-element.26.refs_1_), channel_id=1, source_target_pairs={{4,0},{11,1},{6,2},{9,3},{0,4},{15,5},{2,6},{13,7},{12,8},{3,9},{1... | collective-permute-start | bytes 159752 | tf_op jit(solution)/shard_map/ppermute | solution.py:237
  8.3 4.3 %collective-permute-start.2 = (bf16[208,128]{1,0:T(8,128)(2,1)S(1)}, bf16[208,128]{1,0:T(8,128)(2,1)S(1)}, u32[]{:S(2)}, u32[]{:S(2)}) collective-permute-start(bf16[208,128]{1,0:T(8,128)(2,1)S(1)} %get-tuple-element.26.refs_1_), channel_id=1, source_target_pairs={{2,0},{15,1},{0,2},{13,3},{6,4},{11,5},{4,6},{9,7},{10,8},{7,9},{8... | collective-permute-start | bytes 159752 | tf_op jit(solution)/shard_map/ppermute | solution.py:237
  8.5 5.4 %collective-permute-start.1 = (bf16[208,128]{1,0:T(8,128)(2,1)S(1)}, bf16[208,128]{1,0:T(8,128)(2,1)S(1)}, u32[]{:S(2)}, u32[]{:S(2)}) collective-permute-start(bf16[208,128]{1,0:T(8,128)(2,1)S(1)} %get-tuple-element.26.refs_1_), channel_id=1, source_target_pairs={{8,0},{3,1},{10,2},{1,3},{12,4},{7,5},{14,6},{5,7},{0,8},{11,9},{2... | collective-permute-start | bytes 159752 | tf_op jit(solution)/shard_map/ppermute | solution.py:237
  14.1 1.9 %collective-permute-start.5 = (bf16[48,1024]{1,0:T(8,128)(2,1)S(1)}, bf16[48,1024]{1,0:T(8,128)(2,1)S(1)}, u32[]{:S(2)}, u32[]{:S(2)}) collective-permute-start(bf16[48,1024]{1,0:T(8,128)(2,1)S(1)} %get-tuple-element.33), channel_id=1, source_target_pairs={{0,1},{1,0},{2,3},{3,2},{4,5},{5,4},{6,7},{7,6},{8,9},{9,8},{10,11... | collective-permute-start | bytes 294920 | tf_op jit(solution)/shard_map/ppermute | solution.py:354

commit v6 on v5

--- a/solution.py
+++ b/solution.py
@@ -8,7 +8,7 @@
 LANES = 128
 WINDOW = 144
 GROUP = 8
-META = 16
+META = 8
 F32 = jnp.float32
 BF16 = jnp.bfloat16
 
@@ -211,19 +211,23 @@
             out_ref[j, i : i + 1, :] = val_ref[pl.ds(line, 1), :].astype(BF16)
     copies = [pltpu.make_async_copy(out_ref, out_hbm, out_sem)]
     copies[0].start()
-    key = key_ref[...]
-    back = jnp.zeros((slot_rows, cols), F32)
-    for v in range(n_views):
-        part = jnp.dot(near_ref[:, :WINDOW], win_ref[v], preferred_element_type=F32)
-        for a in range(n_seg):
-            back = jnp.where(key == v * n_seg + a, part[a * slot_rows : (a + 1) * slot_rows], back)
-    gradient = lax.dot_general(flat_ref[...], back.astype(BF16), (((0,), (0,)), ((), ())), preferred_element_type=F32)
     n_parts = sems.shape[0]
-    depth = gradient.shape[0] // n_parts
-    for p in range(n_parts):
-        at = slice(p * depth, (p + 1) * depth)
-        upd_ref[at, :] = vol_ref[at, :] + cw_ref[at, :] * gradient[at]
-        copies.append(pltpu.make_async_copy(upd_ref.at[at, :], upd_hbm.at[at, :], sems.at[p]))
+    width = cols // n_parts
+    spans = [slice(p * width, (p + 1) * width) for p in range(n_parts)]
+    near_all = near_ref[:, :WINDOW]
+    parts = [[jnp.dot(near_all, win_ref[v, :, at], preferred_element_type=F32) for v in range(n_views)] for at in spans]
+    gradients = []
+    for p, at in enumerate(spans):
+        key = key_ref[:, at]
+        back = jnp.zeros((slot_rows, width), F32)
+        for v in range(n_views):
+            for a in range(n_seg):
+                back = jnp.where(key == v * n_seg + a, parts[p][v][a * slot_rows : (a + 1) * slot_rows], back)
+        gradient = lax.dot_general(
+            flat_ref[...], back.astype(BF16), (((0,), (0,)), ((), ())), preferred_element_type=F32
+        )
+        upd_ref[:, at] = vol_ref[:, at] + cw_ref[:, at] * gradient
+        copies.append(pltpu.make_async_copy(upd_ref.at[:, at], upd_hbm.at[:, at], sems.at[p]))
         copies[-1].start()
     for copy in copies:
         copy.wait()
@@ -242,7 +246,7 @@
     near = [(mask, True) for mask in range(half, 0, -1)]
     far = [(1, False)] + [(mask, True) for mask in range(n_group - 1, half, -1)]
     if n_group == 8:
-        near = [(mask, True) for mask in (4, 1, 2, 3)]
+        near = [(mask, True) for mask in (4, 1, 3, 2)]
         far = [(1, False), (7, True), (5, True), (6, True)]
     return list(zip(near, far))
 

time: 17.6 us -> 17.4 us (0.989)
  no operation moved by 1% of the time
where the time goes in v6:
time: 17.4 us; the launch traced here: 17.2 us
  starting transfers between devices  8.98 us (52%)
  Pallas kernels  3.38 us (19%)
  waiting for transfers between devices  2.41 us (14%)
  between operations  1.35 us (8%)
  other arithmetic  1.09 us (6%)
    ppermute x4, starting transfers between devices, exchange(): return lax.ppermute(array, ('slab', 'trans'), pairs)  7.49 us
    pallas_call x1, Pallas kernels, body(): pl.pallas_call(project_kernel, out_shape=(jax.ShapeDtypeStruct((first_row...  1.86 us
    pallas_call x1, Pallas kernels, body(): pl.pallas_call(update_kernel, out_shape=(jax.ShapeDtypeStruct(volume.shap...  1.32 us
    ppermute x4, waiting for transfers between devices, exchange(): return lax.ppermute(array, ('slab', 'trans'), pairs)  1.23 us
    mul x1, other arithmetic, body(): scaled, send = lax.optimization_barrier((0.9 * col_weight, send))  1.09 us
    ppermute x1, starting transfers between devices, body(): other = lax.ppermute(send, 'trans', swap)  0.97 us
    ppermute x1, waiting for transfers between devices, body(): other = lax.ppermute(send, 'trans', swap)  0.94 us
    ppermute x1, starting transfers between devices, body(): got = lax.ppermute(send, 'trans', swap)  0.52 us
  transfers between devices with their start and end apart: 6, of which 3 were waited for; matrix products, arithmetic and copies ran while one was open for 6% of the time, Pallas kernels for 0%

profile of v6, /device:TPU:0, one launch (start us, length us, event | category | flops | bytes accessed | tf_op | source)
XLA Modules:
  0.0 17.2 jit_solution(12275365853088769669)
XLA Ops:
  0.6 0.0 copy-start
  0.6 1.9 %project.1 = (f32[192,128]{1,0:T(8,128)S(1)}, bf16[192,128]{1,0:T(8,128)(2,1)S(1)}, bf16[4,144,1024]{2,1,0:T(8,128)(2,1)S(1)}, f32[16,1024]{1,0:T(8,128)S(1)}, b...) custom-call(s32[8]{0:T(128)} %view_hbm.1, s32[8]{0:T(128)} %block_hbm.1, ...), custom_call_target="tpu_custom_call" | custom-call | tf_op jit(solution)/shard_map/project/pallas_call | solution.py:273
  2.5 0.5 %collective-permute-start = (bf16[192,128]{1,0:T(8,128)(2,1)S(1)}, bf16[192,128]{1,0:T(8,128)(2,1)S(1)}, u32[]{:S(2)}, u32[]{:S(2)}) collective-permute-start(bf16[192,128]{1,0:T(8,128)(2,1)S(1)} %get-tuple-element.24), channel_id=1, source_target_pairs={{0,1},{1,0},{2,3},{3,2},{4,5},{5,4},{6,7},{7,6},{8,9},{9,8},{10,11... | collective-permute-start | bytes 147464 | tf_op jit(solution)/shard_map/ppermute | solution.py:303
  3.7 0.2 %collective-permute-done.refs_4_ = bf16[192,128]{1,0:T(8,128)(2,1)S(1)} collective-permute-done((bf16[192,128]{1,0:T(8,128)(2,1)S(1)}, bf16[192,128]{1,0:T(8,128)(2,1)S(1)}, u32[]{:S(2)}, u32[]{:S(2)}) %collective-permute-start) | collective-permute-done | bytes 49184 | tf_op jit(solution)/shard_map/ppermute | solution.py:303
  3.9 3.0 %collective-permute-start.4 = (bf16[200,128]{1,0:T(8,128)(2,1)S(1)}, bf16[200,128]{1,0:T(8,128)(2,1)S(1)}, u32[]{:S(2)}, u32[]{:S(2)}) collective-permute-start(bf16[200,128]{1,0:T(8,128)(2,1)S(1)} %get-tuple-element.26.refs_1_), channel_id=1, source_target_pairs={{4,0},{13,1},{6,2},{15,3},{0,4},{9,5},{2,6},{11,7},{12,8},{5,9},{1... | collective-permute-start | bytes 153608 | tf_op jit(solution)/shard_map/ppermute | solution.py:241
  6.9 1.4 %collective-permute-start.3 = (bf16[200,128]{1,0:T(8,128)(2,1)S(1)}, bf16[200,128]{1,0:T(8,128)(2,1)S(1)}, u32[]{:S(2)}, u32[]{:S(2)}) collective-permute-start(bf16[200,128]{1,0:T(8,128)(2,1)S(1)} %get-tuple-element.26.refs_1_), channel_id=1, source_target_pairs={{6,0},{11,1},{4,2},{9,3},{2,4},{15,5},{0,6},{13,7},{14,8},{3,9},{1... | collective-permute-start | bytes 153608 | tf_op jit(solution)/shard_map/ppermute | solution.py:241
  8.3 0.2 collective-permute-start.2
  8.5 3.0 %collective-permute-start.1 = (bf16[200,128]{1,0:T(8,128)(2,1)S(1)}, bf16[200,128]{1,0:T(8,128)(2,1)S(1)}, u32[]{:S(2)}, u32[]{:S(2)}) collective-permute-start(bf16[200,128]{1,0:T(8,128)(2,1)S(1)} %get-tuple-element.26.refs_1_), channel_id=1, source_target_pairs={{8,0},{3,1},{10,2},{1,3},{12,4},{7,5},{14,6},{5,7},{0,8},{11,9},{2... | collective-permute-start | bytes 153608 | tf_op jit(solution)/shard_map/ppermute | solution.py:241
  11.4 1.1 %broadcast_multiply_fusion.cw_ref = f32[128,1024]{1,0:T(8,128)S(1)} fusion(f32[128,1024]{1,0:T(8,128)} %param.11), kind=kLoop, calls=%fused_computation | loop fusion | flops 131072 | bytes 1048576 | tf_op jit(solution)/shard_map/mul | solution.py:357
  12.5 0.0 collective-permute-done.4.refs_5_
  12.5 0.0 collective-permute-done.3.refs_4_
  12.5 0.0 collective-permute-done.2.refs_3_
  12.6 1.2 %collective-permute-done.1.refs_2_ = bf16[200,128]{1,0:T(8,128)(2,1)S(1)} collective-permute-done((bf16[200,128]{1,0:T(8,128)(2,1)S(1)}, bf16[200,128]{1,0:T(8,128)(2,1)S(1)}, u32[]{:S(2)}, u32[]{:S(2)}) %collective-permute-start.1) | collective-permute-done | bytes 51232 | tf_op jit(solution)/shard_map/ppermute | solution.py:241
  13.8 0.2 %gather.1 = (f32[48,1024]{1,0:T(8,128)S(1)}, bf16[48,1024]{1,0:T(8,128)(2,1)S(1)}) custom-call(s32[24,128]{1,0:T(8,128)S(1)} %get-tuple-element.25.refs_0_, bf16[200,128]{1,0:T(8,128)(2,1)S(1)} %get-tuple-element.26.refs_1_, bf16[200,128]{1,0:T(8,128)(2,1)S(1)} %collective-permute-done.1.refs_2_, bf16[200,128]{1,0:T(8,128)(2,1)S(1)} %collective-permute-done.2.refs_3_, ...), custom_call_target="tpu_custom_call" | custom-call | tf_op jit(solution)/shard_map/gather/pallas_call | solution.py:334
  14.0 1.0 %collective-permute-start.5 = (bf16[48,1024]{1,0:T(8,128)(2,1)S(1)}, bf16[48,1024]{1,0:T(8,128)(2,1)S(1)}, u32[]{:S(2)}, u32[]{:S(2)}) collective-permute-start(bf16[48,1024]{1,0:T(8,128)(2,1)S(1)} %get-tuple-element.33), channel_id=1, source_target_pairs={{0,1},{1,0},{2,3},{3,2},{4,5},{5,4},{6,7},{7,6},{8,9},{9,8},{10,11... | collective-permute-start | bytes 294920 | tf_op jit(solution)/shard_map/ppermute | solution.py:358
  14.9 0.9 %collective-permute-done.5.got_ref = bf16[48,1024]{1,0:T(8,128)(2,1)S(1)} collective-permute-done((bf16[48,1024]{1,0:T(8,128)(2,1)S(1)}, bf16[48,1024]{1,0:T(8,128)(2,1)S(1)}, u32[]{:S(2)}, u32[]{:S(2)}) %collective-permute-start.5) | collective-permute-done | bytes 98336 | tf_op jit(solution)/shard_map/ppermute | solution.py:358
  15.9 0.0 copy-done
  15.9 1.3 %update.1 = (f32[128,1024]{1,0:T(8,128)}, bf16[1,2,1024]{2,1,0:T(2,128)(2,1)}) custom-call(f32[128,1024]{1,0:T(8,128)S(1)} %copy-done, f32[128,1024]{1,0:T(8,128)S(1)} %broadcast_multiply_fusion.cw_ref, bf16[16,128]{1,0:T(8,128)(2,1)S(1)} %get-tuple-element.29.flat_ref, bf16[4,144,1024]{2,1,0:T(8,128)(2,1)S(1)} %get-tuple-element.30.win_ref, ...), custom_call_target="tpu_custom_call" | custom-call | tf_op jit(solution)/shard_map/update/pallas_call | solution.py:361
  (1 shorter events, 0.0 us)
Async XLA Ops:
  0.6 15.3 %copy-start = (f32[128,1024]{1,0:T(8,128)S(1)}, f32[128,1024]{1,0:T(8,128)}, u32[]{:S(2)}) copy-start(f32[128,1024]{1,0:T(8,128)} %vol_ref.1) | copy-start | bytes 1572868
  2.5 1.4 %collective-permute-start = (bf16[192,128]{1,0:T(8,128)(2,1)S(1)}, bf16[192,128]{1,0:T(8,128)(2,1)S(1)}, u32[]{:S(2)}, u32[]{:S(2)}) collective-permute-start(bf16[192,128]{1,0:T(8,128)(2,1)S(1)} %get-tuple-element.24), channel_id=1, source_target_pairs={{0,1},{1,0},{2,3},{3,2},{4,5},{5,4},{6,7},{7,6},{8,9},{9,8},{10,11... | collective-permute-start | bytes 147464 | tf_op jit(solution)/shard_map/ppermute | solution.py:303
  3.9 8.6 %collective-permute-start.4 = (bf16[200,128]{1,0:T(8,128)(2,1)S(1)}, bf16[200,128]{1,0:T(8,128)(2,1)S(1)}, u32[]{:S(2)}, u32[]{:S(2)}) collective-permute-start(bf16[200,128]{1,0:T(8,128)(2,1)S(1)} %get-tuple-element.26.refs_1_), channel_id=1, source_target_pairs={{4,0},{13,1},{6,2},{15,3},{0,4},{9,5},{2,6},{11,7},{12,8},{5,9},{1... | collective-permute-start | bytes 153608 | tf_op jit(solution)/shard_map/ppermute | solution.py:241
  6.9 5.6 %collective-permute-start.3 = (bf16[200,128]{1,0:T(8,128)(2,1)S(1)}, bf16[200,128]{1,0:T(8,128)(2,1)S(1)}, u32[]{:S(2)}, u32[]{:S(2)}) collective-permute-start(bf16[200,128]{1,0:T(8,128)(2,1)S(1)} %get-tuple-element.26.refs_1_), channel_id=1, source_target_pairs={{6,0},{11,1},{4,2},{9,3},{2,4},{15,5},{0,6},{13,7},{14,8},{3,9},{1... | collective-permute-start | bytes 153608 | tf_op jit(solution)/shard_map/ppermute | solution.py:241
  8.3 4.3 %collective-permute-start.2 = (bf16[200,128]{1,0:T(8,128)(2,1)S(1)}, bf16[200,128]{1,0:T(8,128)(2,1)S(1)}, u32[]{:S(2)}, u32[]{:S(2)}) collective-permute-start(bf16[200,128]{1,0:T(8,128)(2,1)S(1)} %get-tuple-element.26.refs_1_), channel_id=1, source_target_pairs={{2,0},{15,1},{0,2},{13,3},{6,4},{11,5},{4,6},{9,7},{10,8},{7,9},{8... | collective-permute-start | bytes 153608 | tf_op jit(solution)/shard_map/ppermute | solution.py:241
  8.5 5.3 %collective-permute-start.1 = (bf16[200,128]{1,0:T(8,128)(2,1)S(1)}, bf16[200,128]{1,0:T(8,128)(2,1)S(1)}, u32[]{:S(2)}, u32[]{:S(2)}) collective-permute-start(bf16[200,128]{1,0:T(8,128)(2,1)S(1)} %get-tuple-element.26.refs_1_), channel_id=1, source_target_pairs={{8,0},{3,1},{10,2},{1,3},{12,4},{7,5},{14,6},{5,7},{0,8},{11,9},{2... | collective-permute-start | bytes 153608 | tf_op jit(solution)/shard_map/ppermute | solution.py:241
  14.0 1.9 %collective-permute-start.5 = (bf16[48,1024]{1,0:T(8,128)(2,1)S(1)}, bf16[48,1024]{1,0:T(8,128)(2,1)S(1)}, u32[]{:S(2)}, u32[]{:S(2)}) collective-permute-start(bf16[48,1024]{1,0:T(8,128)(2,1)S(1)} %get-tuple-element.33), channel_id=1, source_target_pairs={{0,1},{1,0},{2,3},{3,2},{4,5},{5,4},{6,7},{7,6},{8,9},{9,8},{10,11... | collective-permute-start | bytes 294920 | tf_op jit(solution)/shard_map/ppermute | solution.py:358

commit v7 on v6

--- a/solution.py
+++ b/solution.py
@@ -40,8 +40,8 @@
 
 def project_kernel(
     view_hbm, block_hbm, vol_hbm, pos_hbm, wid_hbm, meas_hbm, rw_hbm, tiles_hbm,
-    own_ref, send_ref, win_ref, key_ref, flat_ref, across_ref, down_ref,
-    view_ref, block_ref, vol_ref, pos_ref, wid_ref, meas_ref, rw_ref, tiles_ref, spread_ref, sems,
+    own_ref, send_ref, win_ref, key_ref, flat_ref, across_ref, down_ref, vol_ref,
+    view_ref, block_ref, pos_ref, wid_ref, meas_ref, rw_ref, tiles_ref, spread_ref, sems,
 ):
     inputs = (pos_hbm, wid_hbm, vol_hbm, view_hbm, block_hbm, tiles_hbm, meas_hbm, rw_hbm)
     holders = (pos_ref, wid_ref, vol_ref, view_ref, block_ref, tiles_ref, meas_ref, rw_ref)
@@ -70,18 +70,19 @@
     first_views = n_views // 2
     for v in range(first_views):
         window(v)
-    for copy in copies[2:]:
+    for copy in copies[3:]:
         copy.wait()
     tiles = tiles_ref[...].astype(F32)
     flat = jnp.concatenate([tiles[s, r : r + 1, :] for s in range(n_slots) for r in range(tile_rows)], axis=0)
     flat = flat.astype(BF16)
     flat_ref[...] = flat
-    rows = jnp.dot(flat, vol_ref[...].astype(BF16), preferred_element_type=F32)
     views = slot_vector([view_ref[s] for s in range(n_slots)], tile_rows, iota((slot_rows, cols), 0))
     key = jnp.broadcast_to(segments[0], (slot_rows, cols))
     for v in range(1, n_views):
         key = jnp.where(views == v, segments[v] + float(v * n_seg), key)
     key_ref[...] = key
+    copies[2].wait()
+    rows = jnp.dot(flat, vol_ref[...].astype(BF16), preferred_element_type=F32)
     sums = jnp.zeros((n_seg * slot_rows, WINDOW), F32)
     for v in range(n_views):
         for a in range(n_seg):
@@ -205,12 +206,7 @@
             near_ref[at, LANES:] = near[:, (a + 1) * LANES : (a + 2) * LANES]
         else:
             near_ref[at, LANES:] = jnp.zeros((slot_rows, LANES), BF16)
-    for i in range(shared_views):
-        for j in range(own_rows):
-            line = (trans * shared_views + i) * own_rows + j
-            out_ref[j, i : i + 1, :] = val_ref[pl.ds(line, 1), :].astype(BF16)
-    copies = [pltpu.make_async_copy(out_ref, out_hbm, out_sem)]
-    copies[0].start()
+    copies = []
     n_parts = sems.shape[0]
     width = cols // n_parts
     spans = [slice(p * width, (p + 1) * width) for p in range(n_parts)]
@@ -229,6 +225,12 @@
         upd_ref[:, at] = vol_ref[:, at] + cw_ref[:, at] * gradient
         copies.append(pltpu.make_async_copy(upd_ref.at[:, at], upd_hbm.at[:, at], sems.at[p]))
         copies[-1].start()
+    for i in range(shared_views):
+        for j in range(own_rows):
+            line = (trans * shared_views + i) * own_rows + j
+            out_ref[j, i : i + 1, :] = val_ref[pl.ds(line, 1), :].astype(BF16)
+    copies.append(pltpu.make_async_copy(out_ref, out_hbm, out_sem))
+    copies[-1].start()
     for copy in copies:
         copy.wait()
 
@@ -270,7 +272,7 @@
     hbm = pl.BlockSpec(memory_space=pltpu.HBM)
     params = pltpu.CompilerParams(vmem_limit_bytes=32 * 1024 * 1024)
     near = (tile_view_index, tile_block, volume, foot_pos, foot_width, measured, row_weight, row_tiles)
-    own, send, windows, key, flat, across, down = pl.pallas_call(
+    own, send, windows, key, flat, across, down, held = pl.pallas_call(
         project_kernel,
         out_shape=(
             jax.ShapeDtypeStruct((first_rows, LANES), F32),
@@ -280,13 +282,13 @@
             jax.ShapeDtypeStruct((slot_rows, depth), BF16),
             jax.ShapeDtypeStruct((8, LANES), jnp.int32),
             jax.ShapeDtypeStruct((slot_rows, LANES), jnp.int32),
+            jax.ShapeDtypeStruct(volume.shape, F32),
         ),
         in_specs=[hbm] * 8,
-        out_specs=(vmem,) * 7,
+        out_specs=(vmem,) * 8,
         scratch_shapes=[
             pltpu.SMEM(tile_view_index.shape, jnp.int32),
             pltpu.SMEM(tile_block.shape, jnp.int32),
-            pltpu.VMEM(volume.shape, F32),
             pltpu.VMEM(foot_pos.shape, F32),
             pltpu.VMEM(foot_width.shape, F32),
             pltpu.VMEM(measured.shape, F32),
@@ -376,7 +378,7 @@
         ],
         compiler_params=params,
         name="update",
-    )(volume, scaled, flat, windows, key, part, other)
+    )(held, scaled, flat, windows, key, part, other)
     return updated, jnp.transpose(residual, (1, 0, 2))
 
 

time: 17.4 us -> 17.4 us (level)
  no operation moved by 1% of the time
where the time goes in v7:
time: 17.4 us; the launch traced here: 17.1 us
  starting transfers between devices  8.98 us (52%)
  Pallas kernels  3.32 us (19%)
  waiting for transfers between devices  2.4 us (14%)
  between operations  1.34 us (8%)
  other arithmetic  1.09 us (6%)
    ppermute x4, starting transfers between devices, exchange(): return lax.ppermute(array, ('slab', 'trans'), pairs)  7.49 us
    pallas_call x1, Pallas kernels, body(): pl.pallas_call(project_kernel, out_shape=(jax.ShapeDtypeStruct((first_row...  1.77 us
    pallas_call x1, Pallas kernels, body(): pl.pallas_call(update_kernel, out_shape=(jax.ShapeDtypeStruct(volume.shap...  1.35 us
    ppermute x4, waiting for transfers between devices, exchange(): return lax.ppermute(array, ('slab', 'trans'), pairs)  1.23 us
    mul x1, other arithmetic, body(): scaled, send = lax.optimization_barrier((0.9 * col_weight, send))  1.09 us
    ppermute x1, starting transfers between devices, body(): other = lax.ppermute(send, 'trans', swap)  0.98 us
    ppermute x1, waiting for transfers between devices, body(): other = lax.ppermute(send, 'trans', swap)  0.94 us
    ppermute x1, starting transfers between devices, body(): got = lax.ppermute(send, 'trans', swap)  0.52 us
  transfers between devices with their start and end apart: 6, of which 3 were waited for; matrix products, arithmetic and copies ran while one was open for 6% of the time, Pallas kernels for 0%

profile of v7, /device:TPU:0, one launch (start us, length us, event | category | flops | bytes accessed | tf_op | source)
XLA Modules:
  0.0 17.1 jit_solution(17956932198655713738)
XLA Ops:
  0.6 1.8 %project.1 = (f32[192,128]{1,0:T(8,128)S(1)}, bf16[192,128]{1,0:T(8,128)(2,1)S(1)}, bf16[4,144,1024]{2,1,0:T(8,128)(2,1)S(1)}, f32[16,1024]{1,0:T(8,128)S(1)}, b...) custom-call(s32[8]{0:T(128)} %view_hbm.1, s32[8]{0:T(128)} %block_hbm.1, ...), custom_call_target="tpu_custom_call" | custom-call | tf_op jit(solution)/shard_map/project/pallas_call | solution.py:275
  2.4 0.5 %collective-permute-start = (bf16[192,128]{1,0:T(8,128)(2,1)S(1)}, bf16[192,128]{1,0:T(8,128)(2,1)S(1)}, u32[]{:S(2)}, u32[]{:S(2)}) collective-permute-start(bf16[192,128]{1,0:T(8,128)(2,1)S(1)} %get-tuple-element.26), channel_id=1, source_target_pairs={{0,1},{1,0},{2,3},{3,2},{4,5},{5,4},{6,7},{7,6},{8,9},{9,8},{10,11... | collective-permute-start | bytes 147464 | tf_op jit(solution)/shard_map/ppermute | solution.py:305
  3.6 0.2 %collective-permute-done.refs_4_ = bf16[192,128]{1,0:T(8,128)(2,1)S(1)} collective-permute-done((bf16[192,128]{1,0:T(8,128)(2,1)S(1)}, bf16[192,128]{1,0:T(8,128)(2,1)S(1)}, u32[]{:S(2)}, u32[]{:S(2)}) %collective-permute-start) | collective-permute-done | bytes 49184 | tf_op jit(solution)/shard_map/ppermute | solution.py:305
  3.8 3.0 %collective-permute-start.4 = (bf16[200,128]{1,0:T(8,128)(2,1)S(1)}, bf16[200,128]{1,0:T(8,128)(2,1)S(1)}, u32[]{:S(2)}, u32[]{:S(2)}) collective-permute-start(bf16[200,128]{1,0:T(8,128)(2,1)S(1)} %get-tuple-element.28.refs_1_), channel_id=1, source_target_pairs={{4,0},{13,1},{6,2},{15,3},{0,4},{9,5},{2,6},{11,7},{12,8},{5,9},{1... | collective-permute-start | bytes 153608 | tf_op jit(solution)/shard_map/ppermute | solution.py:243
  6.8 1.4 %collective-permute-start.3 = (bf16[200,128]{1,0:T(8,128)(2,1)S(1)}, bf16[200,128]{1,0:T(8,128)(2,1)S(1)}, u32[]{:S(2)}, u32[]{:S(2)}) collective-permute-start(bf16[200,128]{1,0:T(8,128)(2,1)S(1)} %get-tuple-element.28.refs_1_), channel_id=1, source_target_pairs={{6,0},{11,1},{4,2},{9,3},{2,4},{15,5},{0,6},{13,7},{14,8},{3,9},{1... | collective-permute-start | bytes 153608 | tf_op jit(solution)/shard_map/ppermute | solution.py:243
  8.2 0.2 collective-permute-start.2
  8.4 3.0 %collective-permute-start.1 = (bf16[200,128]{1,0:T(8,128)(2,1)S(1)}, bf16[200,128]{1,0:T(8,128)(2,1)S(1)}, u32[]{:S(2)}, u32[]{:S(2)}) collective-permute-start(bf16[200,128]{1,0:T(8,128)(2,1)S(1)} %get-tuple-element.28.refs_1_), channel_id=1, source_target_pairs={{8,0},{3,1},{10,2},{1,3},{12,4},{7,5},{14,6},{5,7},{0,8},{11,9},{2... | collective-permute-start | bytes 153608 | tf_op jit(solution)/shard_map/ppermute | solution.py:243
  11.3 1.1 %broadcast_multiply_fusion.cw_ref = f32[128,1024]{1,0:T(8,128)S(1)} fusion(f32[128,1024]{1,0:T(8,128)} %param.11), kind=kLoop, calls=%fused_computation | loop fusion | flops 131072 | bytes 1048576 | tf_op jit(solution)/shard_map/mul | solution.py:359
  12.4 0.0 collective-permute-done.4.refs_5_
  12.4 0.0 collective-permute-done.3.refs_4_
  12.4 0.0 collective-permute-done.2.refs_3_
  12.5 1.2 %collective-permute-done.1.refs_2_ = bf16[200,128]{1,0:T(8,128)(2,1)S(1)} collective-permute-done((bf16[200,128]{1,0:T(8,128)(2,1)S(1)}, bf16[200,128]{1,0:T(8,128)(2,1)S(1)}, u32[]{:S(2)}, u32[]{:S(2)}) %collective-permute-start.1) | collective-permute-done | bytes 51232 | tf_op jit(solution)/shard_map/ppermute | solution.py:243
  13.7 0.2 %gather.1 = (f32[48,1024]{1,0:T(8,128)S(1)}, bf16[48,1024]{1,0:T(8,128)(2,1)S(1)}) custom-call(s32[24,128]{1,0:T(8,128)S(1)} %get-tuple-element.27.refs_0_, bf16[200,128]{1,0:T(8,128)(2,1)S(1)} %get-tuple-element.28.refs_1_, bf16[200,128]{1,0:T(8,128)(2,1)S(1)} %collective-permute-done.1.refs_2_, bf16[200,128]{1,0:T(8,128)(2,1)S(1)} %collective-permute-done.2.refs_3_, ...), custom_call_target="tpu_custom_call" | custom-call | tf_op jit(solution)/shard_map/gather/pallas_call | solution.py:336
  13.9 1.0 %collective-permute-start.5 = (bf16[48,1024]{1,0:T(8,128)(2,1)S(1)}, bf16[48,1024]{1,0:T(8,128)(2,1)S(1)}, u32[]{:S(2)}, u32[]{:S(2)}) collective-permute-start(bf16[48,1024]{1,0:T(8,128)(2,1)S(1)} %get-tuple-element.35), channel_id=1, source_target_pairs={{0,1},{1,0},{2,3},{3,2},{4,5},{5,4},{6,7},{7,6},{8,9},{9,8},{10,11... | collective-permute-start | bytes 294920 | tf_op jit(solution)/shard_map/ppermute | solution.py:360
  14.8 0.9 %collective-permute-done.5.got_ref = bf16[48,1024]{1,0:T(8,128)(2,1)S(1)} collective-permute-done((bf16[48,1024]{1,0:T(8,128)(2,1)S(1)}, bf16[48,1024]{1,0:T(8,128)(2,1)S(1)}, u32[]{:S(2)}, u32[]{:S(2)}) %collective-permute-start.5) | collective-permute-done | bytes 98336 | tf_op jit(solution)/shard_map/ppermute | solution.py:360
  15.8 1.4 %update.1 = (f32[128,1024]{1,0:T(8,128)}, bf16[1,2,1024]{2,1,0:T(2,128)(2,1)}) custom-call(f32[128,1024]{1,0:T(8,128)S(1)} %get-tuple-element.20.vol_ref, f32[128,1024]{1,0:T(8,128)S(1)} %broadcast_multiply_fusion.cw_ref, bf16[16,128]{1,0:T(8,128)(2,1)S(1)} %get-tuple-element.31.flat_ref, bf16[4,144,1024]{2,1,0:T(8,128)(2,1)S(1)} %get-tuple-element.32.win_ref, ...), custom_call_target="tpu_custom_call" | custom-call | tf_op jit(solution)/shard_map/update/pallas_call | solution.py:363
  (1 shorter events, 0.0 us)
Async XLA Ops:
  2.4 1.4 %collective-permute-start = (bf16[192,128]{1,0:T(8,128)(2,1)S(1)}, bf16[192,128]{1,0:T(8,128)(2,1)S(1)}, u32[]{:S(2)}, u32[]{:S(2)}) collective-permute-start(bf16[192,128]{1,0:T(8,128)(2,1)S(1)} %get-tuple-element.26), channel_id=1, source_target_pairs={{0,1},{1,0},{2,3},{3,2},{4,5},{5,4},{6,7},{7,6},{8,9},{9,8},{10,11... | collective-permute-start | bytes 147464 | tf_op jit(solution)/shard_map/ppermute | solution.py:305
  3.8 8.6 %collective-permute-start.4 = (bf16[200,128]{1,0:T(8,128)(2,1)S(1)}, bf16[200,128]{1,0:T(8,128)(2,1)S(1)}, u32[]{:S(2)}, u32[]{:S(2)}) collective-permute-start(bf16[200,128]{1,0:T(8,128)(2,1)S(1)} %get-tuple-element.28.refs_1_), channel_id=1, source_target_pairs={{4,0},{13,1},{6,2},{15,3},{0,4},{9,5},{2,6},{11,7},{12,8},{5,9},{1... | collective-permute-start | bytes 153608 | tf_op jit(solution)/shard_map/ppermute | solution.py:243
  6.8 5.6 %collective-permute-start.3 = (bf16[200,128]{1,0:T(8,128)(2,1)S(1)}, bf16[200,128]{1,0:T(8,128)(2,1)S(1)}, u32[]{:S(2)}, u32[]{:S(2)}) collective-permute-start(bf16[200,128]{1,0:T(8,128)(2,1)S(1)} %get-tuple-element.28.refs_1_), channel_id=1, source_target_pairs={{6,0},{11,1},{4,2},{9,3},{2,4},{15,5},{0,6},{13,7},{14,8},{3,9},{1... | collective-permute-start | bytes 153608 | tf_op jit(solution)/shard_map/ppermute | solution.py:243
  8.2 4.3 %collective-permute-start.2 = (bf16[200,128]{1,0:T(8,128)(2,1)S(1)}, bf16[200,128]{1,0:T(8,128)(2,1)S(1)}, u32[]{:S(2)}, u32[]{:S(2)}) collective-permute-start(bf16[200,128]{1,0:T(8,128)(2,1)S(1)} %get-tuple-element.28.refs_1_), channel_id=1, source_target_pairs={{2,0},{15,1},{0,2},{13,3},{6,4},{11,5},{4,6},{9,7},{10,8},{7,9},{8... | collective-permute-start | bytes 153608 | tf_op jit(solution)/shard_map/ppermute | solution.py:243
  8.4 5.3 %collective-permute-start.1 = (bf16[200,128]{1,0:T(8,128)(2,1)S(1)}, bf16[200,128]{1,0:T(8,128)(2,1)S(1)}, u32[]{:S(2)}, u32[]{:S(2)}) collective-permute-start(bf16[200,128]{1,0:T(8,128)(2,1)S(1)} %get-tuple-element.28.refs_1_), channel_id=1, source_target_pairs={{8,0},{3,1},{10,2},{1,3},{12,4},{7,5},{14,6},{5,7},{0,8},{11,9},{2... | collective-permute-start | bytes 153608 | tf_op jit(solution)/shard_map/ppermute | solution.py:243
  13.9 1.9 %collective-permute-start.5 = (bf16[48,1024]{1,0:T(8,128)(2,1)S(1)}, bf16[48,1024]{1,0:T(8,128)(2,1)S(1)}, u32[]{:S(2)}, u32[]{:S(2)}) collective-permute-start(bf16[48,1024]{1,0:T(8,128)(2,1)S(1)} %get-tuple-element.35), channel_id=1, source_target_pairs={{0,1},{1,0},{2,3},{3,2},{4,5},{5,4},{6,7},{7,6},{8,9},{9,8},{10,11... | collective-permute-start | bytes 294920 | tf_op jit(solution)/shard_map/ppermute | solution.py:360

commit v8 on v7

--- a/solution.py
+++ b/solution.py
@@ -8,7 +8,7 @@
 LANES = 128
 WINDOW = 144
 GROUP = 8
-META = 8
+META = 16
 F32 = jnp.float32
 BF16 = jnp.bfloat16
 
@@ -176,12 +176,12 @@
     lines = part_ref.shape[0] // 2
     ids = jnp.concatenate([ids_ref[...]] * (-(-lines // LANES)), axis=1)[:, :lines]
     chosen = (iota(ids.shape, 1) == ids).astype(F32)
+    picked = []
     for half in range(2):
         part = part_ref[half * lines : (half + 1) * lines, :]
-        rows = slice(half * ids.shape[0], (half + 1) * ids.shape[0])
-        picked = jnp.dot(chosen, part, preferred_element_type=F32, precision=lax.Precision.HIGHEST)
-        out_ref[rows, :] = picked
-        send_ref[rows, :] = picked.astype(BF16)
+        picked.append(jnp.dot(chosen, part, preferred_element_type=F32, precision=lax.Precision.HIGHEST))
+    out_ref[...] = jnp.concatenate(picked, axis=0)
+    send_ref[...] = out_ref[...].astype(BF16)
 
 
 def update_kernel(
@@ -225,10 +225,9 @@
         upd_ref[:, at] = vol_ref[:, at] + cw_ref[:, at] * gradient
         copies.append(pltpu.make_async_copy(upd_ref.at[:, at], upd_hbm.at[:, at], sems.at[p]))
         copies[-1].start()
-    for i in range(shared_views):
-        for j in range(own_rows):
-            line = (trans * shared_views + i) * own_rows + j
-            out_ref[j, i : i + 1, :] = val_ref[pl.ds(line, 1), :].astype(BF16)
+    for j in range(own_rows):
+        own = [val_ref[pl.ds((trans * shared_views + i) * own_rows + j, 1), :] for i in range(shared_views)]
+        out_ref[j] = jnp.concatenate(own, axis=0).astype(BF16)
     copies.append(pltpu.make_async_copy(out_ref, out_hbm, out_sem))
     copies[-1].start()
     for copy in copies:

time: 17.4 us -> 17.5 us (level)
  no operation moved by 1% of the time
where the time goes in v8:
time: 17.5 us; the launch traced here: 17.2 us
  starting transfers between devices  9.01 us (51%)
  Pallas kernels  3.31 us (19%)
  waiting for transfers between devices  2.45 us (14%)
  between operations  1.33 us (8%)
  other arithmetic  1.09 us (6%)
    ppermute x4, starting transfers between devices, exchange(): return lax.ppermute(array, ('slab', 'trans'), pairs)  7.49 us
    pallas_call x1, Pallas kernels, body(): pl.pallas_call(project_kernel, out_shape=(jax.ShapeDtypeStruct((first_row...  1.77 us
    pallas_call x1, Pallas kernels, body(): pl.pallas_call(update_kernel, out_shape=(jax.ShapeDtypeStruct(volume.shap...  1.34 us
    ppermute x4, waiting for transfers between devices, exchange(): return lax.ppermute(array, ('slab', 'trans'), pairs)  1.28 us
    mul x1, other arithmetic, body(): scaled, send = lax.optimization_barrier((0.9 * col_weight, send))  1.09 us
    ppermute x1, starting transfers between devices, body(): other = lax.ppermute(send, 'trans', swap)  1 us
    ppermute x1, waiting for transfers between devices, body(): other = lax.ppermute(send, 'trans', swap)  0.94 us
    ppermute x1, starting transfers between devices, body(): got = lax.ppermute(send, 'trans', swap)  0.52 us
  transfers between devices with their start and end apart: 6, of which 3 were waited for; matrix products, arithmetic and copies ran while one was open for 6% of the time, Pallas kernels for 0%

profile of v8, /device:TPU:0, one launch (start us, length us, event | category | flops | bytes accessed | tf_op | source)
XLA Modules:
  0.0 17.2 jit_solution(3746215075909635057)
XLA Ops:
  0.6 1.8 %project.1 = (f32[192,128]{1,0:T(8,128)S(1)}, bf16[192,128]{1,0:T(8,128)(2,1)S(1)}, bf16[4,144,1024]{2,1,0:T(8,128)(2,1)S(1)}, f32[16,1024]{1,0:T(8,128)S(1)}, b...) custom-call(s32[8]{0:T(128)} %view_hbm.1, s32[8]{0:T(128)} %block_hbm.1, ...), custom_call_target="tpu_custom_call" | custom-call | tf_op jit(solution)/shard_map/project/pallas_call | solution.py:274
  2.4 0.5 %collective-permute-start = (bf16[192,128]{1,0:T(8,128)(2,1)S(1)}, bf16[192,128]{1,0:T(8,128)(2,1)S(1)}, u32[]{:S(2)}, u32[]{:S(2)}) collective-permute-start(bf16[192,128]{1,0:T(8,128)(2,1)S(1)} %get-tuple-element.26), channel_id=1, source_target_pairs={{0,1},{1,0},{2,3},{3,2},{4,5},{5,4},{6,7},{7,6},{8,9},{9,8},{10,11... | collective-permute-start | bytes 147464 | tf_op jit(solution)/shard_map/ppermute | solution.py:304
  3.6 0.2 %collective-permute-done.refs_4_ = bf16[192,128]{1,0:T(8,128)(2,1)S(1)} collective-permute-done((bf16[192,128]{1,0:T(8,128)(2,1)S(1)}, bf16[192,128]{1,0:T(8,128)(2,1)S(1)}, u32[]{:S(2)}, u32[]{:S(2)}) %collective-permute-start) | collective-permute-done | bytes 49184 | tf_op jit(solution)/shard_map/ppermute | solution.py:304
  3.8 3.0 %collective-permute-start.4 = (bf16[208,128]{1,0:T(8,128)(2,1)S(1)}, bf16[208,128]{1,0:T(8,128)(2,1)S(1)}, u32[]{:S(2)}, u32[]{:S(2)}) collective-permute-start(bf16[208,128]{1,0:T(8,128)(2,1)S(1)} %get-tuple-element.28.refs_1_), channel_id=1, source_target_pairs={{4,0},{13,1},{6,2},{15,3},{0,4},{9,5},{2,6},{11,7},{12,8},{5,9},{1... | collective-permute-start | bytes 159752 | tf_op jit(solution)/shard_map/ppermute | solution.py:242
  6.8 1.4 %collective-permute-start.3 = (bf16[208,128]{1,0:T(8,128)(2,1)S(1)}, bf16[208,128]{1,0:T(8,128)(2,1)S(1)}, u32[]{:S(2)}, u32[]{:S(2)}) collective-permute-start(bf16[208,128]{1,0:T(8,128)(2,1)S(1)} %get-tuple-element.28.refs_1_), channel_id=1, source_target_pairs={{6,0},{11,1},{4,2},{9,3},{2,4},{15,5},{0,6},{13,7},{14,8},{3,9},{1... | collective-permute-start | bytes 159752 | tf_op jit(solution)/shard_map/ppermute | solution.py:242
  8.2 0.2 collective-permute-start.2
  8.4 3.0 %collective-permute-start.1 = (bf16[208,128]{1,0:T(8,128)(2,1)S(1)}, bf16[208,128]{1,0:T(8,128)(2,1)S(1)}, u32[]{:S(2)}, u32[]{:S(2)}) collective-permute-start(bf16[208,128]{1,0:T(8,128)(2,1)S(1)} %get-tuple-element.28.refs_1_), channel_id=1, source_target_pairs={{8,0},{3,1},{10,2},{1,3},{12,4},{7,5},{14,6},{5,7},{0,8},{11,9},{2... | collective-permute-start | bytes 159752 | tf_op jit(solution)/shard_map/ppermute | solution.py:242
  11.3 1.1 %broadcast_multiply_fusion.cw_ref = f32[128,1024]{1,0:T(8,128)S(1)} fusion(f32[128,1024]{1,0:T(8,128)} %param.11), kind=kLoop, calls=%fused_computation | loop fusion | flops 131072 | bytes 1048576 | tf_op jit(solution)/shard_map/mul | solution.py:358
  12.4 0.0 collective-permute-done.4.refs_5_
  12.4 0.0 collective-permute-done.3.refs_4_
  12.4 0.0 collective-permute-done.2.refs_3_
  12.5 1.2 %collective-permute-done.1.refs_2_ = bf16[208,128]{1,0:T(8,128)(2,1)S(1)} collective-permute-done((bf16[208,128]{1,0:T(8,128)(2,1)S(1)}, bf16[208,128]{1,0:T(8,128)(2,1)S(1)}, u32[]{:S(2)}, u32[]{:S(2)}) %collective-permute-start.1) | collective-permute-done | bytes 53280 | tf_op jit(solution)/shard_map/ppermute | solution.py:242
  13.7 0.2 %gather.1 = (f32[48,1024]{1,0:T(8,128)S(1)}, bf16[48,1024]{1,0:T(8,128)(2,1)S(1)}) custom-call(s32[24,128]{1,0:T(8,128)S(1)} %get-tuple-element.27.refs_0_, bf16[208,128]{1,0:T(8,128)(2,1)S(1)} %get-tuple-element.28.refs_1_, bf16[208,128]{1,0:T(8,128)(2,1)S(1)} %collective-permute-done.1.refs_2_, bf16[208,128]{1,0:T(8,128)(2,1)S(1)} %collective-permute-done.2.refs_3_, ...), custom_call_target="tpu_custom_call" | custom-call | tf_op jit(solution)/shard_map/gather/pallas_call | solution.py:335
  13.9 1.0 %collective-permute-start.5 = (bf16[48,1024]{1,0:T(8,128)(2,1)S(1)}, bf16[48,1024]{1,0:T(8,128)(2,1)S(1)}, u32[]{:S(2)}, u32[]{:S(2)}) collective-permute-start(bf16[48,1024]{1,0:T(8,128)(2,1)S(1)} %get-tuple-element.35), channel_id=1, source_target_pairs={{0,1},{1,0},{2,3},{3,2},{4,5},{5,4},{6,7},{7,6},{8,9},{9,8},{10,11... | collective-permute-start | bytes 294920 | tf_op jit(solution)/shard_map/ppermute | solution.py:359
  14.9 0.9 %collective-permute-done.5.got_ref = bf16[48,1024]{1,0:T(8,128)(2,1)S(1)} collective-permute-done((bf16[48,1024]{1,0:T(8,128)(2,1)S(1)}, bf16[48,1024]{1,0:T(8,128)(2,1)S(1)}, u32[]{:S(2)}, u32[]{:S(2)}) %collective-permute-start.5) | collective-permute-done | bytes 98336 | tf_op jit(solution)/shard_map/ppermute | solution.py:359
  15.9 1.3 %update.1 = (f32[128,1024]{1,0:T(8,128)}, bf16[1,2,1024]{2,1,0:T(2,128)(2,1)}) custom-call(f32[128,1024]{1,0:T(8,128)S(1)} %get-tuple-element.20.vol_ref, f32[128,1024]{1,0:T(8,128)S(1)} %broadcast_multiply_fusion.cw_ref, bf16[16,128]{1,0:T(8,128)(2,1)S(1)} %get-tuple-element.31.flat_ref, bf16[4,144,1024]{2,1,0:T(8,128)(2,1)S(1)} %get-tuple-element.32.win_ref, ...), custom_call_target="tpu_custom_call" | custom-call | tf_op jit(solution)/shard_map/update/pallas_call | solution.py:362
  (1 shorter events, 0.0 us)
Async XLA Ops:
  2.4 1.4 %collective-permute-start = (bf16[192,128]{1,0:T(8,128)(2,1)S(1)}, bf16[192,128]{1,0:T(8,128)(2,1)S(1)}, u32[]{:S(2)}, u32[]{:S(2)}) collective-permute-start(bf16[192,128]{1,0:T(8,128)(2,1)S(1)} %get-tuple-element.26), channel_id=1, source_target_pairs={{0,1},{1,0},{2,3},{3,2},{4,5},{5,4},{6,7},{7,6},{8,9},{9,8},{10,11... | collective-permute-start | bytes 147464 | tf_op jit(solution)/shard_map/ppermute | solution.py:304
  3.8 8.6 %collective-permute-start.4 = (bf16[208,128]{1,0:T(8,128)(2,1)S(1)}, bf16[208,128]{1,0:T(8,128)(2,1)S(1)}, u32[]{:S(2)}, u32[]{:S(2)}) collective-permute-start(bf16[208,128]{1,0:T(8,128)(2,1)S(1)} %get-tuple-element.28.refs_1_), channel_id=1, source_target_pairs={{4,0},{13,1},{6,2},{15,3},{0,4},{9,5},{2,6},{11,7},{12,8},{5,9},{1... | collective-permute-start | bytes 159752 | tf_op jit(solution)/shard_map/ppermute | solution.py:242
  6.8 5.6 %collective-permute-start.3 = (bf16[208,128]{1,0:T(8,128)(2,1)S(1)}, bf16[208,128]{1,0:T(8,128)(2,1)S(1)}, u32[]{:S(2)}, u32[]{:S(2)}) collective-permute-start(bf16[208,128]{1,0:T(8,128)(2,1)S(1)} %get-tuple-element.28.refs_1_), channel_id=1, source_target_pairs={{6,0},{11,1},{4,2},{9,3},{2,4},{15,5},{0,6},{13,7},{14,8},{3,9},{1... | collective-permute-start | bytes 159752 | tf_op jit(solution)/shard_map/ppermute | solution.py:242
  8.2 4.3 %collective-permute-start.2 = (bf16[208,128]{1,0:T(8,128)(2,1)S(1)}, bf16[208,128]{1,0:T(8,128)(2,1)S(1)}, u32[]{:S(2)}, u32[]{:S(2)}) collective-permute-start(bf16[208,128]{1,0:T(8,128)(2,1)S(1)} %get-tuple-element.28.refs_1_), channel_id=1, source_target_pairs={{2,0},{15,1},{0,2},{13,3},{6,4},{11,5},{4,6},{9,7},{10,8},{7,9},{8... | collective-permute-start | bytes 159752 | tf_op jit(solution)/shard_map/ppermute | solution.py:242
  8.4 5.4 %collective-permute-start.1 = (bf16[208,128]{1,0:T(8,128)(2,1)S(1)}, bf16[208,128]{1,0:T(8,128)(2,1)S(1)}, u32[]{:S(2)}, u32[]{:S(2)}) collective-permute-start(bf16[208,128]{1,0:T(8,128)(2,1)S(1)} %get-tuple-element.28.refs_1_), channel_id=1, source_target_pairs={{8,0},{3,1},{10,2},{1,3},{12,4},{7,5},{14,6},{5,7},{0,8},{11,9},{2... | collective-permute-start | bytes 159752 | tf_op jit(solution)/shard_map/ppermute | solution.py:242
  13.9 1.9 %collective-permute-start.5 = (bf16[48,1024]{1,0:T(8,128)(2,1)S(1)}, bf16[48,1024]{1,0:T(8,128)(2,1)S(1)}, u32[]{:S(2)}, u32[]{:S(2)}) collective-permute-start(bf16[48,1024]{1,0:T(8,128)(2,1)S(1)} %get-tuple-element.35), channel_id=1, source_target_pairs={{0,1},{1,0},{2,3},{3,2},{4,5},{5,4},{6,7},{7,6},{8,9},{9,8},{10,11... | collective-permute-start | bytes 294920 | tf_op jit(solution)/shard_map/ppermute | solution.py:359

commit v9 on v8

--- a/solution.py
+++ b/solution.py
@@ -81,17 +81,6 @@
     for v in range(1, n_views):
         key = jnp.where(views == v, segments[v] + float(v * n_seg), key)
     key_ref[...] = key
-    copies[2].wait()
-    rows = jnp.dot(flat, vol_ref[...].astype(BF16), preferred_element_type=F32)
-    sums = jnp.zeros((n_seg * slot_rows, WINDOW), F32)
-    for v in range(n_views):
-        for a in range(n_seg):
-            spread_ref[v, a * slot_rows : (a + 1) * slot_rows, :] = jnp.where(key == v * n_seg + a, rows, 0.0).astype(BF16)
-        if v >= first_views:
-            window(v)
-        sums = sums + lax.dot_general(
-            spread_ref[v], win_ref[v], (((1,), (1,)), ((), ())), preferred_element_type=F32
-        )
     numbers = slot_lines(view_ref, block_ref, tile_rows, n_views, own_rows)
     across_ref[...] = slot_vector(numbers, 1, iota(across_ref.shape, 1) & (slot_rows - 1))
     down_ref[...] = slot_vector(numbers, 1, iota(down_ref.shape, 0))
@@ -106,6 +95,17 @@
     for a in range(n_seg):
         at = n_seg * slot_rows + a * lines
         own_ref[at : at + lines, :] = block[:, a * LANES : (a + 1) * LANES]
+    copies[2].wait()
+    rows = jnp.dot(flat, vol_ref[...].astype(BF16), preferred_element_type=F32)
+    sums = jnp.zeros((n_seg * slot_rows, WINDOW), F32)
+    for v in range(n_views):
+        for a in range(n_seg):
+            spread_ref[v, a * slot_rows : (a + 1) * slot_rows, :] = jnp.where(key == v * n_seg + a, rows, 0.0).astype(BF16)
+        if v >= first_views:
+            window(v)
+        sums = sums + lax.dot_general(
+            spread_ref[v], win_ref[v], (((1,), (1,)), ((), ())), preferred_element_type=F32
+        )
     edge = WINDOW - LANES
     own_ref[: n_seg * slot_rows, :] = sums[:, :LANES]
     own_ref[slot_rows : n_seg * slot_rows, :edge] += sums[: (n_seg - 1) * slot_rows, LANES:]

time: 17.5 us -> 17.5 us (level)
  transfers between devices with their start and end apart: 6 -> 6, of which waited for: 3 -> 4; matrix products, arithmetic and copies ran while one was open for 6% -> 6% of each run, Pallas kernels for 0% -> 0%
where the time goes in v9:
time: 17.5 us; the launch traced here: 17.2 us
  starting transfers between devices  9.01 us (51%)
  Pallas kernels  3.31 us (19%)
  waiting for transfers between devices  2.45 us (14%)
  between operations  1.33 us (8%)
  other arithmetic  1.09 us (6%)
    ppermute x4, starting transfers between devices, exchange(): return lax.ppermute(array, ('slab', 'trans'), pairs)  7.48 us
    pallas_call x1, Pallas kernels, body(): pl.pallas_call(project_kernel, out_shape=(jax.ShapeDtypeStruct((first_row...  1.78 us
    pallas_call x1, Pallas kernels, body(): pl.pallas_call(update_kernel, out_shape=(jax.ShapeDtypeStruct(volume.shap...  1.34 us
    ppermute x4, waiting for transfers between devices, exchange(): return lax.ppermute(array, ('slab', 'trans'), pairs)  1.28 us
    mul x1, other arithmetic, body(): scaled, send = lax.optimization_barrier((0.9 * col_weight, send))  1.09 us
    ppermute x1, starting transfers between devices, body(): other = lax.ppermute(send, 'trans', swap)  1 us
    ppermute x1, waiting for transfers between devices, body(): other = lax.ppermute(send, 'trans', swap)  0.94 us
    ppermute x1, starting transfers between devices, body(): got = lax.ppermute(send, 'trans', swap)  0.52 us
  transfers between devices with their start and end apart: 6, of which 4 were waited for; matrix products, arithmetic and copies ran while one was open for 6% of the time, Pallas kernels for 0%

profile of v9, /device:TPU:0, one launch (start us, length us, event | category | flops | bytes accessed | tf_op | source)
XLA Modules:
  0.0 17.2 jit_solution(9339543024988419170)
XLA Ops:
  0.6 1.8 %project.1 = (f32[192,128]{1,0:T(8,128)S(1)}, bf16[192,128]{1,0:T(8,128)(2,1)S(1)}, bf16[4,144,1024]{2,1,0:T(8,128)(2,1)S(1)}, f32[16,1024]{1,0:T(8,128)S(1)}, b...) custom-call(s32[8]{0:T(128)} %view_hbm.1, s32[8]{0:T(128)} %block_hbm.1, ...), custom_call_target="tpu_custom_call" | custom-call | tf_op jit(solution)/shard_map/project/pallas_call | solution.py:274
  2.4 0.5 %collective-permute-start = (bf16[192,128]{1,0:T(8,128)(2,1)S(1)}, bf16[192,128]{1,0:T(8,128)(2,1)S(1)}, u32[]{:S(2)}, u32[]{:S(2)}) collective-permute-start(bf16[192,128]{1,0:T(8,128)(2,1)S(1)} %get-tuple-element.26), channel_id=1, source_target_pairs={{0,1},{1,0},{2,3},{3,2},{4,5},{5,4},{6,7},{7,6},{8,9},{9,8},{10,11... | collective-permute-start | bytes 147464 | tf_op jit(solution)/shard_map/ppermute | solution.py:304
  3.6 0.2 %collective-permute-done.refs_4_ = bf16[192,128]{1,0:T(8,128)(2,1)S(1)} collective-permute-done((bf16[192,128]{1,0:T(8,128)(2,1)S(1)}, bf16[192,128]{1,0:T(8,128)(2,1)S(1)}, u32[]{:S(2)}, u32[]{:S(2)}) %collective-permute-start) | collective-permute-done | bytes 49184 | tf_op jit(solution)/shard_map/ppermute | solution.py:304
  3.8 3.0 %collective-permute-start.4 = (bf16[208,128]{1,0:T(8,128)(2,1)S(1)}, bf16[208,128]{1,0:T(8,128)(2,1)S(1)}, u32[]{:S(2)}, u32[]{:S(2)}) collective-permute-start(bf16[208,128]{1,0:T(8,128)(2,1)S(1)} %get-tuple-element.28.refs_1_), channel_id=1, source_target_pairs={{4,0},{13,1},{6,2},{15,3},{0,4},{9,5},{2,6},{11,7},{12,8},{5,9},{1... | collective-permute-start | bytes 159752 | tf_op jit(solution)/shard_map/ppermute | solution.py:242
  6.8 1.4 %collective-permute-start.3 = (bf16[208,128]{1,0:T(8,128)(2,1)S(1)}, bf16[208,128]{1,0:T(8,128)(2,1)S(1)}, u32[]{:S(2)}, u32[]{:S(2)}) collective-permute-start(bf16[208,128]{1,0:T(8,128)(2,1)S(1)} %get-tuple-element.28.refs_1_), channel_id=1, source_target_pairs={{6,0},{11,1},{4,2},{9,3},{2,4},{15,5},{0,6},{13,7},{14,8},{3,9},{1... | collective-permute-start | bytes 159752 | tf_op jit(solution)/shard_map/ppermute | solution.py:242
  8.2 0.2 collective-permute-start.2
  8.4 3.0 %collective-permute-start.1 = (bf16[208,128]{1,0:T(8,128)(2,1)S(1)}, bf16[208,128]{1,0:T(8,128)(2,1)S(1)}, u32[]{:S(2)}, u32[]{:S(2)}) collective-permute-start(bf16[208,128]{1,0:T(8,128)(2,1)S(1)} %get-tuple-element.28.refs_1_), channel_id=1, source_target_pairs={{8,0},{3,1},{10,2},{1,3},{12,4},{7,5},{14,6},{5,7},{0,8},{11,9},{2... | collective-permute-start | bytes 159752 | tf_op jit(solution)/shard_map/ppermute | solution.py:242
  11.3 1.1 %broadcast_multiply_fusion.cw_ref = f32[128,1024]{1,0:T(8,128)S(1)} fusion(f32[128,1024]{1,0:T(8,128)} %param.11), kind=kLoop, calls=%fused_computation | loop fusion | flops 131072 | bytes 1048576 | tf_op jit(solution)/shard_map/mul | solution.py:358
  12.4 0.0 collective-permute-done.4.refs_5_
  12.4 0.0 collective-permute-done.3.refs_4_
  12.5 0.1 collective-permute-done.2.refs_3_
  12.5 1.2 %collective-permute-done.1.refs_2_ = bf16[208,128]{1,0:T(8,128)(2,1)S(1)} collective-permute-done((bf16[208,128]{1,0:T(8,128)(2,1)S(1)}, bf16[208,128]{1,0:T(8,128)(2,1)S(1)}, u32[]{:S(2)}, u32[]{:S(2)}) %collective-permute-start.1) | collective-permute-done | bytes 53280 | tf_op jit(solution)/shard_map/ppermute | solution.py:242
  13.7 0.2 %gather.1 = (f32[48,1024]{1,0:T(8,128)S(1)}, bf16[48,1024]{1,0:T(8,128)(2,1)S(1)}) custom-call(s32[24,128]{1,0:T(8,128)S(1)} %get-tuple-element.27.refs_0_, bf16[208,128]{1,0:T(8,128)(2,1)S(1)} %get-tuple-element.28.refs_1_, bf16[208,128]{1,0:T(8,128)(2,1)S(1)} %collective-permute-done.1.refs_2_, bf16[208,128]{1,0:T(8,128)(2,1)S(1)} %collective-permute-done.2.refs_3_, ...), custom_call_target="tpu_custom_call" | custom-call | tf_op jit(solution)/shard_map/gather/pallas_call | solution.py:335
  13.9 1.0 %collective-permute-start.5 = (bf16[48,1024]{1,0:T(8,128)(2,1)S(1)}, bf16[48,1024]{1,0:T(8,128)(2,1)S(1)}, u32[]{:S(2)}, u32[]{:S(2)}) collective-permute-start(bf16[48,1024]{1,0:T(8,128)(2,1)S(1)} %get-tuple-element.35), channel_id=1, source_target_pairs={{0,1},{1,0},{2,3},{3,2},{4,5},{5,4},{6,7},{7,6},{8,9},{9,8},{10,11... | collective-permute-start | bytes 294920 | tf_op jit(solution)/shard_map/ppermute | solution.py:359
  14.9 0.9 %collective-permute-done.5.got_ref = bf16[48,1024]{1,0:T(8,128)(2,1)S(1)} collective-permute-done((bf16[48,1024]{1,0:T(8,128)(2,1)S(1)}, bf16[48,1024]{1,0:T(8,128)(2,1)S(1)}, u32[]{:S(2)}, u32[]{:S(2)}) %collective-permute-start.5) | collective-permute-done | bytes 98336 | tf_op jit(solution)/shard_map/ppermute | solution.py:359
  15.9 1.3 %update.1 = (f32[128,1024]{1,0:T(8,128)}, bf16[1,2,1024]{2,1,0:T(2,128)(2,1)}) custom-call(f32[128,1024]{1,0:T(8,128)S(1)} %get-tuple-element.20.vol_ref, f32[128,1024]{1,0:T(8,128)S(1)} %broadcast_multiply_fusion.cw_ref, bf16[16,128]{1,0:T(8,128)(2,1)S(1)} %get-tuple-element.31.flat_ref, bf16[4,144,1024]{2,1,0:T(8,128)(2,1)S(1)} %get-tuple-element.32.win_ref, ...), custom_call_target="tpu_custom_call" | custom-call | tf_op jit(solution)/shard_map/update/pallas_call | solution.py:362
  (1 shorter events, 0.0 us)
Async XLA Ops:
  2.4 1.4 %collective-permute-start = (bf16[192,128]{1,0:T(8,128)(2,1)S(1)}, bf16[192,128]{1,0:T(8,128)(2,1)S(1)}, u32[]{:S(2)}, u32[]{:S(2)}) collective-permute-start(bf16[192,128]{1,0:T(8,128)(2,1)S(1)} %get-tuple-element.26), channel_id=1, source_target_pairs={{0,1},{1,0},{2,3},{3,2},{4,5},{5,4},{6,7},{7,6},{8,9},{9,8},{10,11... | collective-permute-start | bytes 147464 | tf_op jit(solution)/shard_map/ppermute | solution.py:304
  3.8 8.6 %collective-permute-start.4 = (bf16[208,128]{1,0:T(8,128)(2,1)S(1)}, bf16[208,128]{1,0:T(8,128)(2,1)S(1)}, u32[]{:S(2)}, u32[]{:S(2)}) collective-permute-start(bf16[208,128]{1,0:T(8,128)(2,1)S(1)} %get-tuple-element.28.refs_1_), channel_id=1, source_target_pairs={{4,0},{13,1},{6,2},{15,3},{0,4},{9,5},{2,6},{11,7},{12,8},{5,9},{1... | collective-permute-start | bytes 159752 | tf_op jit(solution)/shard_map/ppermute | solution.py:242
  6.8 5.6 %collective-permute-start.3 = (bf16[208,128]{1,0:T(8,128)(2,1)S(1)}, bf16[208,128]{1,0:T(8,128)(2,1)S(1)}, u32[]{:S(2)}, u32[]{:S(2)}) collective-permute-start(bf16[208,128]{1,0:T(8,128)(2,1)S(1)} %get-tuple-element.28.refs_1_), channel_id=1, source_target_pairs={{6,0},{11,1},{4,2},{9,3},{2,4},{15,5},{0,6},{13,7},{14,8},{3,9},{1... | collective-permute-start | bytes 159752 | tf_op jit(solution)/shard_map/ppermute | solution.py:242
  8.2 4.3 %collective-permute-start.2 = (bf16[208,128]{1,0:T(8,128)(2,1)S(1)}, bf16[208,128]{1,0:T(8,128)(2,1)S(1)}, u32[]{:S(2)}, u32[]{:S(2)}) collective-permute-start(bf16[208,128]{1,0:T(8,128)(2,1)S(1)} %get-tuple-element.28.refs_1_), channel_id=1, source_target_pairs={{2,0},{15,1},{0,2},{13,3},{6,4},{11,5},{4,6},{9,7},{10,8},{7,9},{8... | collective-permute-start | bytes 159752 | tf_op jit(solution)/shard_map/ppermute | solution.py:242
  8.4 5.4 %collective-permute-start.1 = (bf16[208,128]{1,0:T(8,128)(2,1)S(1)}, bf16[208,128]{1,0:T(8,128)(2,1)S(1)}, u32[]{:S(2)}, u32[]{:S(2)}) collective-permute-start(bf16[208,128]{1,0:T(8,128)(2,1)S(1)} %get-tuple-element.28.refs_1_), channel_id=1, source_target_pairs={{8,0},{3,1},{10,2},{1,3},{12,4},{7,5},{14,6},{5,7},{0,8},{11,9},{2... | collective-permute-start | bytes 159752 | tf_op jit(solution)/shard_map/ppermute | solution.py:242
  13.9 1.9 %collective-permute-start.5 = (bf16[48,1024]{1,0:T(8,128)(2,1)S(1)}, bf16[48,1024]{1,0:T(8,128)(2,1)S(1)}, u32[]{:S(2)}, u32[]{:S(2)}) collective-permute-start(bf16[48,1024]{1,0:T(8,128)(2,1)S(1)} %get-tuple-element.35), channel_id=1, source_target_pairs={{0,1},{1,0},{2,3},{3,2},{4,5},{5,4},{6,7},{7,6},{8,9},{9,8},{10,11... | collective-permute-start | bytes 294920 | tf_op jit(solution)/shard_map/ppermute | solution.py:359
